TPU v7x, 32 devices: a whole 2x2x4 slice. The times are simulated.
32 devices in a mesh: branch: 2 (over core), tp: 4 (over y, x), seq: 4 (over z).
Axes of the slice: x: 2, y: 2, z: 4, core: 2. Of those that a mesh axis runs over, the one named last changes fastest.
Arguments:
- block_input: bfloat16 [8, 2048, 2048], P('seq', 'tp'), may hold values from -6 to 6
- first_norm_gain: bfloat16 [2048], replicated, may hold values from 0.25 to 1.75
- first_norm_bias: bfloat16 [2048], replicated, may hold values from -1.5 to 1.5
- second_norm_gain: bfloat16 [2048], replicated, may hold values from 0.25 to 1.75
- second_norm_bias: bfloat16 [2048], replicated, may hold values from -1.5 to 1.5
- query_key_value: bfloat16 [2048, 6144], P(('branch', 'seq'), 'tp'), may hold values from -0.125 to 0.125
- query_key_value_bias: bfloat16 [6144], P('tp'), may hold values from -1.5 to 1.5
- attention_dense: bfloat16 [2048, 2048], P('tp', ('branch', 'seq')), may hold values from -0.375 to 0.375
- attention_dense_bias: bfloat16 [2048], replicated, may hold values from -1.5 to 1.5
- expand_weight: bfloat16 [2048, 8192], P(('branch', 'seq'), 'tp'), may hold values from -0.125 to 0.125
- expand_bias: bfloat16 [8192], P('tp'), may hold values from -2.5 to 2.5
- contract_weight: bfloat16 [8192, 2048], P('tp', ('branch', 'seq')), may hold values from -0.09375 to 0.09375
- contract_bias: bfloat16 [2048], replicated, may hold values from -1.5 to 1.5
- document_starts: int32 [8, 8], P('seq'), may hold values from 0 to 2048, as said below
- output_grad: bfloat16 [8, 2048, 2048], P('seq', 'tp'), may hold values from -6 to 6
Outputs:
- block_output: bfloat16 [8, 2048, 2048], P('seq', 'tp')
- input_grad: bfloat16 [8, 2048, 2048], P('seq', 'tp')
- first_gain_grad: float32 [2048], replicated
- first_bias_grad: float32 [2048], replicated
- second_gain_grad: float32 [2048], replicated
- second_bias_grad: float32 [2048], replicated
- query_key_value_grad: float32 [2048, 6144], P(('branch', 'seq'), 'tp')
- query_key_value_bias_grad: float32 [6144], P('tp')
- dense_grad: float32 [2048, 2048], P('tp', ('branch', 'seq'))
- dense_bias_grad: float32 [2048], replicated
- expand_grad: float32 [2048, 8192], P(('branch', 'seq'), 'tp')
- expand_bias_grad: float32 [8192], P('tp')
- contract_grad: float32 [8192, 2048], P('tp', ('branch', 'seq'))
- contract_bias_grad: float32 [2048], replicated
Inputs may be any that keep to these rules, and one draw needn't show every extreme that they name: `document_starts`: each row lists where the documents of one packed sequence begin: it starts with 0, rises strictly, and the entries after its last document are 2048. Among the 2 rows of each index of seq, one (drawn) has a document that begins before position 512 and ends after position 1536; the others hold 2 to 8 documents.
All inputs are finite; a program needn't handle non-finite values.
Results may differ from a plain program's by a relative error of at most 0.01.
Values may be sent and summed in bfloat16 or wider, within the bound.
No kernel may reach another device: no remote copies, remote signals or barrier semaphores. Data moves between devices by JAX's collectives and lax.ppermute only.
A program may use at most 704 MiB of HBM per device.

v0:
```python
from functools import partial
import math

import jax
import jax.numpy as jnp
from jax import lax
from jax.sharding import PartitionSpec as P

HD = 128
ROT = 32


EPSILON = 1e-05
NEGATIVE = -1e30
ROPE_BASE = 10000.0
CONTRACT_LAST = (((1,), (1,)), ((), ()))
CONTRACT_FIRST = (((0,), (0,)), ((), ()))


def layer_norm(values, gain_row, shift_row):
    average = jnp.mean(values, axis=-1, keepdims=True)
    centred = values - average
    variance = jnp.mean(centred * centred, axis=-1, keepdims=True)
    return centred * lax.rsqrt(variance + EPSILON) * gain_row + shift_row


def doc_layout(starts, length):
    places = jnp.arange(length, dtype=jnp.int32)
    started = starts[..., None, :] <= places[:, None]
    doc_ids = jnp.sum(started.astype(jnp.int32), axis=-1) - 1
    begin_at = jnp.max(jnp.where(started, starts[..., None, :], 0), axis=-1)
    return (doc_ids, places - begin_at)


def rotary_tables(relative):
    half_rot = ROT // 2
    exponent = jnp.arange(half_rot, dtype=jnp.float32) * (2.0 / ROT)
    frequency = ROPE_BASE ** (-exponent)
    angles = relative.astype(jnp.float32)[..., None] * frequency
    return (jnp.cos(angles), jnp.sin(angles))


def rotate(vectors, cosine_table, sine_table):
    half_rot = cosine_table.shape[-1]
    leading = vectors[..., :half_rot]
    second = vectors[..., half_rot : 2 * half_rot]
    return jnp.concatenate(
        [
            leading * cosine_table - second * sine_table,
            second * cosine_table + leading * sine_table,
            vectors[..., 2 * half_rot :],
        ],
        axis=-1,
    )


def to_sequence(flat, tiles, seq_count):
    columns = flat.shape[-1]
    return (
        flat.reshape(tiles, seq_count, -1, columns)
        .transpose(1, 0, 2, 3)
        .reshape(seq_count, -1, columns)
    )


def to_tiles(ordered, tiles):
    seq_count, length, columns = ordered.shape
    return (
        ordered.reshape(seq_count, tiles, length // tiles, columns)
        .transpose(1, 0, 2, 3)
        .reshape(-1, columns)
    )


def masked_scores(query_block, key_block, query_places, key_places, query_docs, key_docs, scaling):
    products = (
        jnp.einsum("bhqd,bhkd->bhqk", query_block, key_block, preferred_element_type=jnp.float32)
        * scaling
    )
    allowed = (query_places[:, None] >= key_places[None, :])[None] & (
        query_docs[:, :, None] == key_docs[:, None, :]
    )
    return jnp.where(allowed[:, None], products, NEGATIVE)


def attention_forward(queries, keys, values, doc_ids):
    seq_count, head_count, length, head_width = queries.shape
    block_rows = min(512, length)
    scaling = 1.0 / math.sqrt(head_width)
    places = jnp.arange(length, dtype=jnp.int32)
    outputs = []
    log_sums = []
    for number in range(length // block_rows):
        row_begin = number * block_rows
        row_end = row_begin + block_rows
        scores = masked_scores(
            queries[:, :, row_begin:row_end],
            keys,
            places[row_begin:row_end],
            places,
            doc_ids[:, row_begin:row_end],
            doc_ids,
            scaling,
        )
        row_max = jnp.max(scores, axis=-1, keepdims=True)
        exponent = jnp.exp(scores - row_max)
        row_total = jnp.sum(exponent, axis=-1, keepdims=True)
        weights = (exponent / row_total).astype(jnp.bfloat16)
        outputs.append(
            jnp.einsum("bhqk,bhkd->bhqd", weights, values, preferred_element_type=jnp.float32)
        )
        log_sums.append((row_max + jnp.log(row_total))[..., 0])
    return (jnp.concatenate(outputs, axis=2), jnp.concatenate(log_sums, axis=2))


def attention_backward(queries, keys, values, log_sums, attended_grad, doc_ids):
    seq_count, head_count, length, head_width = queries.shape
    block_rows = min(512, length)
    scaling = 1.0 / math.sqrt(head_width)
    places = jnp.arange(length, dtype=jnp.int32)
    query_parts = []
    key_grad = jnp.zeros(queries.shape, jnp.float32)
    value_grad = jnp.zeros(queries.shape, jnp.float32)
    for number in range(length // block_rows):
        row_begin = number * block_rows
        row_end = row_begin + block_rows
        query_block = queries[:, :, row_begin:row_end]
        grad_block = attended_grad[:, :, row_begin:row_end]
        scores = masked_scores(
            query_block,
            keys,
            places[row_begin:row_end],
            places,
            doc_ids[:, row_begin:row_end],
            doc_ids,
            scaling,
        )
        weights = jnp.exp(scores - log_sums[:, :, row_begin:row_end, None])
        weight_grad = jnp.einsum(
            "bhqd,bhkd->bhqk", grad_block, values, preferred_element_type=jnp.float32
        )
        row_inner = jnp.sum(weights * weight_grad, axis=-1, keepdims=True)
        score_grad = (weights * (weight_grad - row_inner) * scaling).astype(jnp.bfloat16)
        query_parts.append(
            jnp.einsum("bhqk,bhkd->bhqd", score_grad, keys, preferred_element_type=jnp.float32)
        )
        key_grad = key_grad.at[:, :, :length].add(
            jnp.einsum(
                "bhqk,bhqd->bhkd", score_grad, query_block, preferred_element_type=jnp.float32
            )
        )
        value_grad = value_grad.at[:, :, :length].add(
            jnp.einsum(
                "bhqk,bhqd->bhkd",
                weights.astype(jnp.bfloat16),
                grad_block,
                preferred_element_type=jnp.float32,
            )
        )
    return (jnp.concatenate(query_parts, axis=2), key_grad, value_grad)


def per_device(
    block_input,
    first_norm_gain,
    first_norm_bias,
    second_norm_gain,
    second_norm_bias,
    query_key_value,
    query_key_value_bias,
    attention_dense,
    attention_dense_bias,
    expand_weight,
    expand_bias,
    contract_weight,
    contract_bias,
    document_starts,
    output_grad,
):
    seq_count, rows_own, model_width = block_input.shape
    tiles = lax.axis_size("tp")
    branches = lax.axis_size("branch")
    seq_groups = lax.axis_size("seq")
    length = rows_own * tiles
    joined_cols = query_key_value.shape[1]
    head_count = joined_cols // (3 * HD)
    attn_cols = head_count * HD
    hidden_here = expand_weight.shape[1]
    grad_share = model_width // (branches * seq_groups)
    first_half = lax.axis_index("branch") == 0
    gain_row = jnp.where(first_half, first_norm_gain, second_norm_gain).astype(jnp.float32)
    shift_row = jnp.where(first_half, first_norm_bias, second_norm_bias).astype(jnp.float32)
    input_own = block_input.astype(jnp.float32)
    normed_own = layer_norm(input_own, gain_row, shift_row).astype(jnp.bfloat16)
    normed = lax.all_gather(normed_own[None], "tp", axis=0, tiled=True)
    normed_flat = normed.reshape(-1, model_width)
    all_rows = normed_flat.shape[0]
    joined_full, expand_full = (
        lax.all_gather(query_key_value, ("branch", "seq"), axis=0, tiled=True),
        lax.all_gather(expand_weight, ("branch", "seq"), axis=0, tiled=True),
    )
    dense_full, contract_full = (
        lax.all_gather(attention_dense, ("branch", "seq"), axis=1, tiled=True),
        lax.all_gather(contract_weight, ("branch", "seq"), axis=1, tiled=True),
    )
    doc_ids, relative = doc_layout(document_starts, length)
    cosine_table, sine_table = rotary_tables(relative)
    cosine_table = cosine_table[:, None]
    sine_table = sine_table[:, None]
    head_shape = (seq_count, head_count, length, HD)

    def attention_side():
        joined = jnp.dot(
            normed_flat, joined_full, preferred_element_type=jnp.float32
        ) + query_key_value_bias.astype(jnp.float32)
        joined = (
            to_sequence(joined, tiles, seq_count)
            .reshape(seq_count, length, head_count, 3, HD)
            .transpose(3, 0, 2, 1, 4)
        )
        queries = rotate(joined[0], cosine_table, sine_table).astype(jnp.bfloat16)
        keys = rotate(joined[1], cosine_table, sine_table).astype(jnp.bfloat16)
        values = joined[2].astype(jnp.bfloat16)
        attended, log_sums = attention_forward(queries, keys, values, doc_ids)
        attended = to_tiles(
            attended.transpose(0, 2, 1, 3).reshape(seq_count, length, attn_cols), tiles
        ).astype(jnp.bfloat16)
        return (
            queries,
            keys,
            values,
            log_sums,
            attended,
            jnp.zeros((all_rows, hidden_here), jnp.float32),
            jnp.zeros((all_rows, hidden_here), jnp.bfloat16),
        )

    def mlp_side():
        pre_act = jnp.dot(
            normed_flat, expand_full, preferred_element_type=jnp.float32
        ) + expand_bias.astype(jnp.float32)
        activated = jax.nn.gelu(pre_act, approximate=False).astype(jnp.bfloat16)
        empty_heads = jnp.zeros(head_shape, jnp.bfloat16)
        return (
            empty_heads,
            empty_heads,
            empty_heads,
            jnp.zeros(head_shape[:3], jnp.float32),
            jnp.zeros((all_rows, attn_cols), jnp.bfloat16),
            pre_act,
            activated,
        )

    queries, keys, values, log_sums, attended, pre_act, activated = lax.cond(
        first_half, attention_side, mlp_side
    )

    def branch_attention_term():
        return jnp.dot(attended, dense_full, preferred_element_type=jnp.float32)

    def branch_mlp_term():
        return jnp.dot(activated, contract_full, preferred_element_type=jnp.float32)

    branch_rows = lax.psum_scatter(
        lax.cond(first_half, branch_attention_term, branch_mlp_term),
        "tp",
        scatter_dimension=0,
        tiled=True,
    )
    combined = lax.psum(branch_rows.reshape(seq_count, rows_own, model_width), "branch")
    block_output = (
        input_own
        + combined
        + attention_dense_bias.astype(jnp.float32)
        + contract_bias.astype(jnp.float32)
    ).astype(jnp.bfloat16)
    grad_gathered = lax.all_gather(output_grad[None], "tp", axis=0, tiled=True)
    grad_flat = grad_gathered.reshape(-1, model_width)
    joined_back, expand_back = (
        lax.all_gather(query_key_value, ("branch", "seq"), axis=0, tiled=True),
        lax.all_gather(expand_weight, ("branch", "seq"), axis=0, tiled=True),
    )
    dense_back, contract_back = (
        lax.all_gather(attention_dense, ("branch", "seq"), axis=1, tiled=True),
        lax.all_gather(contract_weight, ("branch", "seq"), axis=1, tiled=True),
    )

    def attention_back():
        attended_grad = lax.dot_general(
            grad_flat, dense_back, CONTRACT_LAST, preferred_element_type=jnp.float32
        ).astype(jnp.bfloat16)
        grad_heads = (
            to_sequence(attended_grad, tiles, seq_count)
            .reshape(seq_count, length, head_count, HD)
            .transpose(0, 2, 1, 3)
        )
        query_grad, key_grad, value_grad = attention_backward(
            queries, keys, values, log_sums, grad_heads, doc_ids
        )
        query_grad = rotate(query_grad, cosine_table, -sine_table)
        key_grad = rotate(key_grad, cosine_table, -sine_table)
        joined_grad = (
            jnp.stack([query_grad, key_grad, value_grad], axis=0)
            .transpose(1, 3, 2, 0, 4)
            .reshape(seq_count, length, joined_cols)
        )
        joined_grad = to_tiles(joined_grad, tiles).astype(jnp.bfloat16)
        return (
            joined_grad,
            jnp.zeros((all_rows, hidden_here), jnp.bfloat16),
            jnp.sum(joined_grad.astype(jnp.float32), axis=0),
            jnp.zeros((hidden_here,), jnp.float32),
        )

    def mlp_back():
        activated_grad = lax.dot_general(
            grad_flat, contract_back, CONTRACT_LAST, preferred_element_type=jnp.float32
        )
        unused, gelu_back = jax.vjp(partial(jax.nn.gelu, approximate=False), pre_act)
        pre_grad = gelu_back(activated_grad)[0].astype(jnp.bfloat16)
        return (
            jnp.zeros((all_rows, joined_cols), jnp.bfloat16),
            pre_grad,
            jnp.zeros((joined_cols,), jnp.float32),
            jnp.sum(pre_grad.astype(jnp.float32), axis=0),
        )

    joined_grad, pre_grad, joined_bias_part, expand_bias_part = lax.cond(
        first_half, attention_back, mlp_back
    )

    def normed_attention_term():
        return lax.dot_general(
            joined_grad, joined_back, CONTRACT_LAST, preferred_element_type=jnp.float32
        )

    def normed_mlp_term():
        return lax.dot_general(
            pre_grad, expand_back, CONTRACT_LAST, preferred_element_type=jnp.float32
        )

    normed_grad = lax.psum_scatter(
        lax.cond(first_half, normed_attention_term, normed_mlp_term),
        "tp",
        scatter_dimension=0,
        tiled=True,
    )
    normed_grad = normed_grad.reshape(seq_count, rows_own, model_width)
    unused_norm, norm_back = jax.vjp(layer_norm, input_own, gain_row, shift_row)
    input_part, gain_part, shift_part = norm_back(normed_grad)
    input_both = lax.psum(input_part, "branch")
    grad_own = output_grad.astype(jnp.float32)
    input_grad = (grad_own + input_both).astype(jnp.bfloat16)

    def weight_attention_term():
        joined_part = lax.dot_general(
            normed_flat, joined_grad, CONTRACT_FIRST, preferred_element_type=jnp.float32
        )
        dense_part = lax.dot_general(
            grad_flat, attended, CONTRACT_FIRST, preferred_element_type=jnp.float32
        )
        empty_hidden = jnp.zeros(
            (grad_share * lax.axis_size(("branch", "seq")), hidden_here), jnp.float32
        )
        return jnp.concatenate([joined_part, empty_hidden, dense_part, empty_hidden], axis=1)

    def weight_mlp_term():
        expand_part = lax.dot_general(
            normed_flat, pre_grad, CONTRACT_FIRST, preferred_element_type=jnp.float32
        )
        contract_part = lax.dot_general(
            grad_flat, activated, CONTRACT_FIRST, preferred_element_type=jnp.float32
        )
        return jnp.concatenate(
            [
                jnp.zeros(
                    (grad_share * lax.axis_size(("branch", "seq")), joined_cols), jnp.float32
                ),
                expand_part,
                jnp.zeros((grad_share * lax.axis_size(("branch", "seq")), attn_cols), jnp.float32),
                contract_part,
            ],
            axis=1,
        )

    weight_rows = lax.psum_scatter(
        lax.cond(first_half, weight_attention_term, weight_mlp_term).astype(jnp.bfloat16),
        ("branch", "seq"),
        scatter_dimension=0,
        tiled=True,
    ).astype(jnp.float32)
    query_key_value_grad = weight_rows[:, :joined_cols]
    expand_grad = weight_rows[:, joined_cols : joined_cols + hidden_here]
    dense_grad = weight_rows[:, joined_cols + hidden_here : joined_cols + hidden_here + attn_cols].T
    contract_grad = weight_rows[:, joined_cols + hidden_here + attn_cols :].T
    query_key_value_bias_grad, expand_bias_grad = lax.psum(
        (joined_bias_part, expand_bias_part), ("branch", "seq")
    )
    empty_row = jnp.zeros_like(gain_part)
    grad_columns = jnp.sum(grad_own, axis=(0, 1))
    norm_results = lax.psum(
        (
            jnp.where(first_half, gain_part, empty_row),
            jnp.where(first_half, shift_part, empty_row),
            jnp.where(first_half, empty_row, gain_part),
            jnp.where(first_half, empty_row, shift_part),
            jnp.where(first_half, grad_columns, empty_row),
            jnp.where(first_half, empty_row, grad_columns),
        ),
        ("branch", "tp", "seq"),
    )
    (
        first_gain_grad,
        first_bias_grad,
        second_gain_grad,
        second_bias_grad,
        dense_bias_grad,
        contract_bias_grad,
    ) = norm_results
    return (
        block_output,
        input_grad,
        first_gain_grad,
        first_bias_grad,
        second_gain_grad,
        second_bias_grad,
        query_key_value_grad,
        query_key_value_bias_grad,
        dense_grad,
        dense_bias_grad,
        expand_grad,
        expand_bias_grad,
        contract_grad,
        contract_bias_grad,
    )


def solution(mesh):
    in_specs = (
        P("seq", "tp", None),
        P(),
        P(),
        P(),
        P(),
        P(("branch", "seq"), "tp"),
        P("tp"),
        P("tp", ("branch", "seq")),
        P(),
        P(("branch", "seq"), "tp"),
        P("tp"),
        P("tp", ("branch", "seq")),
        P(),
        P("seq", None),
        P("seq", "tp", None),
    )
    out_specs = (
        P("seq", "tp", None),
        P("seq", "tp", None),
        P(),
        P(),
        P(),
        P(),
        P(("branch", "seq"), "tp"),
        P("tp"),
        P("tp", ("branch", "seq")),
        P(),
        P(("branch", "seq"), "tp"),
        P("tp"),
        P("tp", ("branch", "seq")),
        P(),
    )
    return jax.shard_map(
        per_device, mesh=mesh, in_specs=in_specs, out_specs=out_specs, check_vma=False
    )
```

profile of v0, /device:TPU:0, one launch (start us, length us, event | category | flops | bytes accessed | tf_op | source)
XLA Modules:
  0.0 2892.1 jit_solution(4238215076032738188)
XLA Ops:
  32.3 62.1 %all-gather.9.cloned.1.call-done = bf16[2048,2048]{1,0:T(8,128)(2,1)} async-done(((bf16[256,2048]{1,0:T(8,128)(2,1)}), bf16[2048,2048]{1,0:T(8,128)(2,1)}) %all-gather.9.cloned.1.call-update) | async-done | bytes 8388624 | tf_op jit(solution)/shard_map/all_gather | solution.py:200
  94.4 158.4 %all-gather.17.cloned.1.call-done = bf16[8,512,2048]{2,1,0:T(8,128)(2,1)} async-done(((bf16[2,512,2048]{2,1,0:T(8,128)(2,1)}), bf16[8,512,2048]{2,1,0:T(8,128)(2,1)}) %all-gather.17.cloned.1.call-update) | async-done | bytes 16777232 | tf_op jit(solution)/shard_map/all_gather | solution.py:195
  252.8 66.4 %all-gather.11.cloned.1.call-done = bf16[2048,1536]{1,0:T(8,128)(2,1)} async-done(((bf16[256,1536]{1,0:T(8,128)(2,1)}), bf16[2048,1536]{1,0:T(8,128)(2,1)}) %all-gather.11.cloned.1.call-update) | async-done | bytes 6291472 | tf_op jit(solution)/shard_map/all_gather | solution.py:199
  319.2 445.7 %conditional.5 = (bf16[2,4,2048,128]{3,2,1,0:T(8,128)(2,1)}, bf16[2,4,2048,128]{3,2,1,0:T(8,128)(2,1)}, bf16[2,4,2048,128]{3,2,1,0:T(8,128)(2,1)}, f32[2,4,2048]...) conditional(s32[]{:T(128)} %convert_element_type.149, ...), branch_computations={%region_4.5_spmd, %region_5.14_spmd} | conditional | flops 43427856384 | bytes 902135040 | solution.py:254
  328.2 34.2 %convolution_add_fusion.1 = f32[4096,1536]{1,0:T(8,128)} fusion(bf16[4096,2048]{1,0:T(8,128)(2,1)} %get-tuple-element.246, bf16[2048,1536]{1,0:T(8,128)(2,1)} %get-tuple-element.247, f32[1536]{0:T(1024)S(1)} %convert_element_type.107), kind=kOutput, calls=%fused_computation.40 | convolution fusion | flops 25776095232 | bytes 48240640 | tf_op jit(solution)/shard_map/cond/branch_1_fun/dot_general | solution.py:213
  362.4 30.0 %copy.110 = f32[4,2,512,1536]{2,0,3,1:T(4,128)} copy(f32[4,2,512,1536]{3,2,1,0:T(8,128)} %bitcast.124) | data formatting | bytes 50331648 | tf_op jit(solution)/shard_map/cond/branch_1_fun/reshape | solution.py:60
  392.4 31.0 %reshape.623 = f32[2,2048,4,3,128]{1,4,3,2,0:T(8,128)} reshape(f32[2,4,512,1536]{2,1,3,0:T(4,128)} %bitcast.112) | data formatting | bytes 50331648 | tf_op jit(solution)/shard_map/cond/branch_1_fun/reshape;cond/branch_1_fun/reshape | solution.py:218
  423.4 24.8 copy.111
  714.1 20.7 copy.112
  765.1 902.9 %conditional.7 = (bf16[4096,1536]{1,0:T(8,128)(2,1)}, bf16[4096,2048]{1,0:T(8,128)(2,1)}, f32[1536]{0:T(1024)}, f32[2048]{0:T(1024)}) conditional(s32[]{:T(128)} %convert_element_type.149, (f32[4096,2048]{1,0:T(8,128)}, bf16[4096,2048]{1,0:T(8,128)(2,1)}, bf16[2048,2048]{1,0:T(8,128)(2,1)}) %tuple.198, (s32[2,2048]{1,0:T(2,128)}, ...), branch_computations={%region_18.20_spmd, %region_20.26_spmd} | conditional | flops 52510720000 | bytes 1747966208 | solution.py:328
  813.8 19.6 fusion.193
  946.6 25.6 add_bitcast_fusion
  987.5 61.1 %fusion.97 = f32[2,4,512,128]{3,2,1,0:T(8,128)} fusion(bf16[2,4,2048,128]{3,2,1,0:T(8,128)(2,1)} %get-tuple-element.261, f32[2,4,512,2048]{3,2,1,0:T(8,128)} %fusion.181, f32[2,4,512,2048]{3,2,1,0:T(8,128)} %fusion.193, f32[2,4,512]{2,1,0:T(4,128)S(1)} %get-tuple-element.447, pred[2,512,2048]{2,1,0:T(8,128)(4,1)} %copy-done.20), kind=kOutput, calls=%fused_computation.150 | convolution fusion | flops 2239764480 | bytes 75513856 | tf_op jit(solution)/shard_map/cond/branch_1_fun/bhqk,bhkd->bhqd/dot_general | solution.py:145
  1066.7 61.2 %fusion.90 = f32[2,4,512,128]{3,2,1,0:T(8,128)} fusion(bf16[2,4,2048,128]{3,2,1,0:T(8,128)(2,1)} %get-tuple-element.261, f32[2,4,512,2048]{3,2,1,0:T(8,128)} %fusion.184, f32[2,4,512,2048]{3,2,1,0:T(8,128)} %fusion.196, f32[2,4,512]{2,1,0:T(4,128)S(1)} %copy-done.43, pred[2,512,2048]{2,1,0:T(8,128)(4,1)} %get-tuple-element.452), kind=kOutput, calls=%fused_computation.147 | convolution fusion | flops 2239764480 | bytes 75513856 | tf_op jit(solution)/shard_map/cond/branch_1_fun/bhqk,bhkd->bhqd/dot_general | solution.py:145
  1127.8 67.4 %fusion.87 = f32[2,4,2048,128]{3,2,1,0:T(8,128)} fusion(f32[2,4,512,2048]{3,2,1,0:T(8,128)} %fusion.184, f32[2,4,512,2048]{3,2,1,0:T(8,128)} %fusion.196, f32[2,4,512]{2,1,0:T(4,128)S(1)} %copy-done.43, pred[2,512,2048]{2,1,0:T(8,128)(4,1)} %get-tuple-element.452, bf16[2,4,2048,128]{3,2,1,0:T(8,128)(2,1)} %get-tuple-element.260), kind=kOutput, calls=%fused_computation.146 | convolution fusion | flops 2239764480 | bytes 147881984 | tf_op jit(solution)/shard_map/cond/branch_1_fun/bhqk,bhqd->bhkd/dot_general | solution.py:148
  1213.4 60.9 %fusion.83 = f32[2,4,512,128]{3,2,1,0:T(8,128)} fusion(bf16[2,4,2048,128]{3,2,1,0:T(8,128)(2,1)} %get-tuple-element.261, f32[2,4,512,2048]{3,2,1,0:T(8,128)} %fusion.187, f32[2,4,512,2048]{3,2,1,0:T(8,128)} %fusion.199, f32[2,4,512]{2,1,0:T(4,128)S(1)} %copy-done.41, pred[2,512,2048]{2,1,0:T(8,128)(4,1)} %get-tuple-element.451), kind=kOutput, calls=%fused_computation.144 | convolution fusion | flops 2239764480 | bytes 75513856 | tf_op jit(solution)/shard_map/cond/branch_1_fun/bhqk,bhkd->bhqd/dot_general | solution.py:145
  1274.2 67.6 %fusion.80 = f32[2,4,2048,128]{3,2,1,0:T(8,128)} fusion(f32[2,4,512,2048]{3,2,1,0:T(8,128)} %fusion.187, f32[2,4,512,2048]{3,2,1,0:T(8,128)} %fusion.199, f32[2,4,512]{2,1,0:T(4,128)S(1)} %copy-done.41, pred[2,512,2048]{2,1,0:T(8,128)(4,1)} %get-tuple-element.451, bf16[2,4,2048,128]{3,2,1,0:T(8,128)(2,1)} %get-tuple-element.260), kind=kOutput, calls=%fused_computation.143 | convolution fusion | flops 2239764480 | bytes 147881984 | tf_op jit(solution)/shard_map/cond/branch_1_fun/bhqk,bhqd->bhkd/dot_general | solution.py:148
  1360.0 61.4 %fusion.76 = f32[2,4,512,128]{3,2,1,0:T(8,128)} fusion(bf16[2,4,2048,128]{3,2,1,0:T(8,128)(2,1)} %get-tuple-element.261, f32[2,4,512,2048]{3,2,1,0:T(8,128)} %fusion.190, f32[2,4,512,2048]{3,2,1,0:T(8,128)} %fusion.202, f32[2,4,512]{2,1,0:T(4,128)S(1)} %copy-done.27, pred[2,512,2048]{2,1,0:T(8,128)(4,1)} %get-tuple-element.450), kind=kOutput, calls=%fused_computation.141 | convolution fusion | flops 2239764480 | bytes 75513856 | tf_op jit(solution)/shard_map/cond/branch_1_fun/bhqk,bhkd->bhqd/dot_general | solution.py:145
  1421.3 67.7 %fusion.73 = f32[2,4,2048,128]{3,2,1,0:T(8,128)} fusion(f32[2,4,512,2048]{3,2,1,0:T(8,128)} %fusion.190, f32[2,4,512,2048]{3,2,1,0:T(8,128)} %fusion.202, f32[2,4,512]{2,1,0:T(4,128)S(1)} %copy-done.27, pred[2,512,2048]{2,1,0:T(8,128)(4,1)} %get-tuple-element.450, bf16[2,4,2048,128]{3,2,1,0:T(8,128)(2,1)} %get-tuple-element.260), kind=kOutput, calls=%fused_computation.140 | convolution fusion | flops 2239764480 | bytes 147881984 | tf_op jit(solution)/shard_map/cond/branch_1_fun/bhqk,bhqd->bhkd/dot_general | solution.py:148
  1489.1 68.8 %add_add_fusion = f32[2,4,2048,128]{3,2,1,0:T(8,128)} fusion(f32[2,4,2048,128]{3,2,1,0:T(8,128)} %fusion.87, f32[2,4,2048,128]{3,2,1,0:T(8,128)} %fusion.73, f32[2,4,2048,128]{3,2,1,0:T(8,128)} %fusion.80, f32[2,4,512,2048]{3,2,1,0:T(8,128)} %fusion.181, f32[2,4,512,2048]{3,2,1,0:T(8,128)} %fusion.193, f32[2,4,512]{2,1,0:T(4,128)S(1)} %copy-done.39, ...), kind=kOutput, calls=%fused_computation.198 | convolution fusion | flops 2246055936 | bytes 173047808 | tf_op jit(solution)/shard_map/cond/branch_1_fun/bhqk,bhqd->bhkd/dot_general | solution.py:148
  1619.9 21.3 convert_element_type.130
  1641.2 19.9 copy.129
  1668.0 33.8 %conditional.8 = (f32[4096,2048]{1,0:T(8,128)}) conditional(s32[]{:T(128)} %convert_element_type.149, (bf16[4096,2048]{1,0:T(8,128)(2,1)}, bf16[2048,2048]{1,0:T(8,128)(2,1)}) %tuple.104, (bf16[4096,1536]{1,0:T(8,128)(2,1)}, bf16[2048,1536]{1,0:T(8,128)(2,1)}) %tuple.105), branch_computations={%region_26.27_spmd, %region_27.28_spmd} | conditional | flops 34359738368 | bytes 58720264 | solution.py:343
  1668.0 33.7 %fusion.277 = f32[4096,2048]{1,0:T(8,128)} fusion(bf16[4096,1536]{1,0:T(8,128)(2,1)} %get-tuple-element.270, bf16[2048,1536]{1,0:T(8,128)(2,1)} %get-tuple-element.271), kind=kOutput, calls=%fused_computation.327 | convolution fusion | flops 25769803776 | bytes 52428800 | tf_op jit(solution)/shard_map/cond/branch_1_fun/dot_general | solution.py:333
  1722.2 79.2 %conditional.9 = (bf16[2048,6144]{0,1:T(8,128)(2,1)}) conditional(s32[]{:T(128)} %convert_element_type.149, (bf16[4096,2048]{1,0:T(8,128)(2,1)}, bf16[4096,2048]{1,0:T(8,128)(2,1)}, bf16[4096,2048]{1,0:T(8,128)(2,1)}, bf16[4096,2048]{1,0:T(8,128)(2,1)}) %tuple.200, (bf16[4096,2048]{1,0:T(8,128)(2,1)}, bf16[4096,1536]{1,0:T(8,128)(2,1)}, ...), branch_computations={%region_38.39_spmd, %region_39.40_spmd} | conditional | flops 68820140032 | bytes 125886472 | solution.py:387
  1730.6 34.5 %fusion.280 = bf16[2048,1536]{0,1:T(8,128)(2,1)} fusion(bf16[4096,2048]{1,0:T(8,128)(2,1)} %get-tuple-element.276, bf16[4096,1536]{1,0:T(8,128)(2,1)} %get-tuple-element.277), kind=kOutput, calls=%fused_computation.330 | convolution fusion | flops 25769803776 | bytes 35651584 | tf_op jit(solution)/shard_map/cond/branch_1_fun/dot_general | solution.py:356
  1801.8 186.8 %reduce-scatter.6.cloned.1.call-done = f32[1024,2048]{1,0:T(8,128)} async-done(((f32[4096,2048]{1,0:T(8,128)}), f32[1024,2048]{1,0:T(8,128)}) %reduce-scatter.6.cloned.1.call-update) | async-done | bytes 8388624 | tf_op jit(solution)/shard_map/reduce_scatter | solution.py:342
  2006.5 274.2 %reduce-scatter.4.cloned.1.call-done = f32[1024,2048]{1,0:T(8,128)} async-done(((f32[4096,2048]{1,0:T(8,128)}), f32[1024,2048]{1,0:T(8,128)}) %reduce-scatter.4.cloned.1.call-update) | async-done | bytes 8388624 | tf_op jit(solution)/shard_map/reduce_scatter | solution.py:264
  2280.7 34.6 %all-reduce.1 = (f32[1536]{0:T(1024)}, f32[2048]{0:T(1024)}) all-reduce(f32[1536]{0:T(1024)} %get-tuple-element.314, f32[2048]{0:T(1024)} %get-tuple-element.315), channel_id=1, replica_groups=mesh['branch'=2,'tp'=4,'seq'=4] {'branch','seq'}, use_global_device_ids=true, to_apply=%region_41.42 | all-reduce | flops 3584 | bytes 28672 | tf_op jit(solution)/shard_map/psum | solution.py:396
  2315.4 450.3 %reduce-scatter.8.cloned.1.call-done = bf16[256,6144]{0,1:T(8,128)(2,1)} async-done(((bf16[2048,6144]{0,1:T(8,128)(2,1)}), bf16[256,6144]{0,1:T(8,128)(2,1)}) %reduce-scatter.8.cloned.1.call-update) | async-done | bytes 3145744 | tf_op jit(solution)/shard_map/reduce_scatter | solution.py:386
  2785.6 44.7 %all-reduce.5.cloned.1.call-done = (f32[2,512,2048]{2,1,0:T(8,128)}, f32[2,512,2048]{2,1,0:T(8,128)}) async-done(((f32[2,512,2048]{2,1,0:T(8,128)}, f32[2,512,2048]{2,1,0:T(8,128)}), (f32[2,512,2048]{2,1,0:T(8,128)}, f32[2,512,2048]{2,1,0:T(8,128)})) %all-reduce.5.cloned.1.call-update) | async-done | bytes 16777232 | tf_op jit(solution)/shard_map/psum | solution.py:270
  2843.0 41.8 %all-reduce = (f32[2048]{0:T(1024)}, f32[2048]{0:T(1024)}, f32[2048]{0:T(1024)}, f32[2048]{0:T(1024)}, f32[2048]{0:T(1024)}, /*index=5*/f32[2048]{0:T(1024)}) all-reduce(f32[2048]{0:T(1024)S(1)} %get-tuple-element.472, f32[2048]{0:T(1024)S(1)} %get-tuple-element.469, ...), channel_id=1, replica_groups=mesh['branch'=2,'tp'=4,'seq'=4] {'branch','tp','seq'}, use_global_device_ids=true, to_apply=%region_33.34 | all-reduce | flops 12288 | bytes 98304 | tf_op jit(solution)/shard_map/psum | solution.py:401
  (234 shorter events, 740.4 us)
Async XLA Ops:
  7.2 312.0 %copy-start.44 = (bf16[2048]{0:T(1024)(128)(2,1)S(1)}, bf16[2048]{0:T(1024)(128)(2,1)}, u32[]{:S(2)}) copy-start(bf16[2048]{0:T(1024)(128)(2,1)} %param.67) | copy-start | bytes 12292
  7.2 312.0 %copy-start.45 = (bf16[1536]{0:T(1024)(128)(2,1)S(1)}, bf16[1536]{0:T(1024)(128)(2,1)}, u32[]{:S(2)}) copy-start(bf16[1536]{0:T(1024)(128)(2,1)} %param.63) | copy-start | bytes 9220
  7.2 87.2 %all-gather.9.cloned.1.call-start = ((), (), s32[]{:S(2)}) async-start(), calls=%async_computation.3 | async-start | bytes 9437184 | tf_op jit(solution)/shard_map/all_gather | solution.py:200
  7.9 244.9 %all-gather.17.cloned.1.call-start = ((), (), s32[]{:S(2)}) async-start(), calls=%async_computation.10 | async-start | bytes 20971520 | tf_op jit(solution)/shard_map/all_gather | solution.py:195
  20.9 298.3 %all-gather.11.cloned.1.call-start = ((), (), s32[]{:S(2)}) async-start(), calls=%async_computation.4 | async-start | bytes 7077888 | tf_op jit(solution)/shard_map/all_gather | solution.py:199
  21.7 743.3 %all-gather.13.cloned.1.call-start = ((), (), s32[]{:S(2)}) async-start(), calls=%async_computation.5 | async-start | bytes 9437184 | tf_op jit(solution)/shard_map/all_gather | solution.py:204
  22.2 742.8 %all-gather.19.cloned.1.call-start = ((), (), s32[]{:S(2)}) async-start(), calls=%async_computation.11 | async-start | bytes 20971520 | tf_op jit(solution)/shard_map/all_gather | solution.py:277
  22.8 742.2 %all-gather.15.cloned.1.call-start = ((), (), s32[]{:S(2)}) async-start(), calls=%async_computation.6 | async-start | bytes 2359296 | tf_op jit(solution)/shard_map/all_gather | solution.py:203
  23.4 1965.2 %reduce-scatter.6.cloned.1.call-start = ((), (), s32[]{:S(2)}) async-start(), calls=%async_computation.8 | async-start | bytes 41943040 | tf_op jit(solution)/shard_map/reduce_scatter | solution.py:342
  23.7 295.6 %copy-start.25 = (s32[2,2048]{1,0:T(2,128)}, s32[2,2048]{1,0:T(2,128)S(1)}, u32[]{:S(2)}) copy-start(s32[2,2048]{1,0:T(2,128)S(1)} %broadcast_add_fusion.1) | copy-start | bytes 49156
  32.3 286.9 %copy-start.9 = (f32[2,1,2048,16]{3,2,0,1:T(8,128)}, f32[2,1,2048,16]{3,2,0,1:T(8,128)S(1)}, u32[]{:S(2)}) copy-start(f32[2,1,2048,16]{3,2,0,1:T(8,128)S(1)} %get-tuple-element.464) | copy-start | bytes 786436
  328.1 34.3 %copy-start.10 = (f32[2,1,2048,16]{3,2,0,1:T(8,128)}, f32[2,1,2048,16]{3,2,0,1:T(8,128)S(1)}, u32[]{:S(2)}) copy-start(f32[2,1,2048,16]{3,2,0,1:T(8,128)S(1)} %get-tuple-element.250) | copy-start | bytes 786436 | tf_op jit(solution)/shard_map/cond
  459.2 125.6 %copy-start.7 = (pred[2,512,2048]{2,1,0:T(8,128)(4,1)}, pred[2,512,2048]{2,1,0:T(8,128)(4,1)S(1)}, u32[]{:S(2)}) copy-start(pred[2,512,2048]{2,1,0:T(8,128)(4,1)S(1)} %get-tuple-element.420) | copy-start | bytes 6291460 | tf_op jit(solution)/shard_map/cond
  600.0 19.1 copy-start.5
  713.8 32.9 %copy-start.32 = (f32[1,8,512]{2,1,0:T(8,128)S(1)}, f32[1,8,512]{2,1,0:T(8,128)}, u32[]{:S(2)}) copy-start(f32[1,8,512]{2,1,0:T(8,128)} %log_add_fusion) | copy-start | bytes 49156 | tf_op jit(solution)/shard_map/cond
  713.8 32.8 %copy-start.33 = (f32[1,8,512]{2,1,0:T(8,128)S(1)}, f32[1,8,512]{2,1,0:T(8,128)}, u32[]{:S(2)}) copy-start(f32[1,8,512]{2,1,0:T(8,128)} %log_add_fusion.1) | copy-start | bytes 49156 | tf_op jit(solution)/shard_map/cond
  772.8 98.4 %copy-start.42 = (f32[2,4,512]{2,1,0:T(4,128)}, f32[2,4,512]{2,1,0:T(4,128)S(1)}, u32[]{:S(2)}) copy-start(f32[2,4,512]{2,1,0:T(4,128)S(1)} %get-tuple-element.448) | copy-start | bytes 49156 | tf_op jit(solution)/shard_map/cond
  772.8 136.2 %copy-start.40 = (f32[2,4,512]{2,1,0:T(4,128)}, f32[2,4,512]{2,1,0:T(4,128)S(1)}, u32[]{:S(2)}) copy-start(f32[2,4,512]{2,1,0:T(4,128)S(1)} %get-tuple-element.449) | copy-start | bytes 49156 | tf_op jit(solution)/shard_map/cond
  772.8 214.7 %copy-start.38 = (f32[2,4,512]{2,1,0:T(4,128)}, f32[2,4,512]{2,1,0:T(4,128)S(1)}, u32[]{:S(2)}) copy-start(f32[2,4,512]{2,1,0:T(4,128)S(1)} %get-tuple-element.447) | copy-start | bytes 49156 | tf_op jit(solution)/shard_map/cond
  788.2 45.2 %copy-start.20 = (pred[2,512,2048]{2,1,0:T(8,128)(4,1)}, pred[2,512,2048]{2,1,0:T(8,128)(4,1)S(1)}, u32[]{:S(2)}) copy-start(pred[2,512,2048]{2,1,0:T(8,128)(4,1)S(1)} %get-tuple-element.453) | copy-start | bytes 6291460 | tf_op jit(solution)/shard_map/cond
  813.8 158.4 %copy-start.3 = (bf16[2,2048,4,128]{3,1,2,0:T(8,128)(2,1)}, bf16[2,2048,4,128]{3,1,2,0:T(8,128)(2,1)S(1)}, u32[]{:S(2)}) copy-start(bf16[2,2048,4,128]{3,1,2,0:T(8,128)(2,1)S(1)} %copy.147) | copy-start | bytes 12582916 | tf_op jit(solution)/shard_map/cond
  928.3 18.3 copy-start.14
  1421.3 67.7 %copy-start.39 = (f32[2,4,512]{2,1,0:T(4,128)S(1)}, f32[2,4,512]{2,1,0:T(4,128)}, u32[]{:S(2)}) copy-start(f32[2,4,512]{2,1,0:T(4,128)} %copy-done.38) | copy-start | bytes 49156 | tf_op jit(solution)/shard_map/cond
  1701.8 578.9 %reduce-scatter.4.cloned.1.call-start = ((), (), s32[]{:S(2)}) async-start(), calls=%async_computation.7 | async-start | bytes 41943040 | tf_op jit(solution)/shard_map/reduce_scatter | solution.py:264
  1722.2 1043.5 %reduce-scatter.8.cloned.1.call-start = ((), (), s32[]{:S(2)}) async-start(), calls=%async_computation.9 | async-start | bytes 28311552 | tf_op jit(solution)/shard_map/reduce_scatter | solution.py:386
  1801.5 187.2 %copy-start.29 = (f32[2048]{0:T(1024)S(1)}, f32[2048]{0:T(1024)}, u32[]{:S(2)}) copy-start(f32[2048]{0:T(1024)} %copy-done.28) | copy-start | bytes 24580
  1801.5 187.2 %copy-start.31 = (f32[2,512]{1,0:T(2,128)S(1)}, f32[2,512]{1,0:T(2,128)}, u32[]{:S(2)}) copy-start(f32[2,512]{1,0:T(2,128)} %copy-done.30) | copy-start | bytes 12292
  1801.5 192.8 %copy-start.37 = (f32[2,512]{1,0:T(2,128)S(1)}, f32[2,512]{1,0:T(2,128)}, u32[]{:S(2)}) copy-start(f32[2,512]{1,0:T(2,128)} %copy-done.36) | copy-start | bytes 12292
  1801.5 192.8 %copy-start.35 = (f32[2,512]{1,0:T(2,128)S(1)}, f32[2,512]{1,0:T(2,128)}, u32[]{:S(2)}) copy-start(f32[2,512]{1,0:T(2,128)} %copy-done.34) | copy-start | bytes 12292
  1801.5 1028.8 %all-reduce.5.cloned.1.call-start = ((), (), s32[]{:S(2)}) async-start(), calls=%async_computation.12 | async-start | bytes 33554432 | tf_op jit(solution)/shard_map/psum | solution.py:270
  2001.3 279.4 %copy-start.46 = (bf16[2048]{0:T(1024)(128)(2,1)S(1)}, bf16[2048]{0:T(1024)(128)(2,1)}, u32[]{:S(2)}) copy-start(bf16[2048]{0:T(1024)(128)(2,1)} %param.65) | copy-start | bytes 12292
  2001.3 279.4 %copy-start.47 = (bf16[2048]{0:T(1024)(128)(2,1)S(1)}, bf16[2048]{0:T(1024)(128)(2,1)}, u32[]{:S(2)}) copy-start(bf16[2048]{0:T(1024)(128)(2,1)} %param.69) | copy-start | bytes 12292
  (29 other events, 337.0 us)
Sparse Core Ops, SparseCore 0:
  9.6 84.7 all-gather.8
  96.8 155.9 all-gather.16
  254.4 64.7 all-gather.10
  320.7 81.1 all-gather.12
  403.5 155.5 all-gather.18
  560.6 30.8 all-gather.14
  1701.9 286.7 reduce-scatter.5
  1992.0 288.6 reduce-scatter.3
  2283.0 482.5 reduce-scatter.7
  2768.1 62.1 all-reduce.4
where the time goes:
time: 2900 us; the launch traced here: 2890 us
  waiting for transfers between devices  1250 us (43%)
  matrix products  1030 us (36%)
  local copies, waits for them, and re-layouts  274 us (9%)
  other arithmetic  230 us (8%)
  blocking collectives  76.4 us (3%)
    reduce_scatter x1, waiting for transfers between devices, per_device(): lax.psum_scatter(lax.cond(first_half, weight_attention_term, weight_mlp_t...  450 us
    reduce_scatter x1, waiting for transfers between devices, per_device(): lax.psum_scatter(lax.cond(first_half, branch_attention_term, branch_mlp_t...  274 us
    dot_general x4, matrix products, attention_backward(): jnp.einsum('bhqk,bhqd->bhkd', score_grad, query_block, preferred_element_...  272 us
    dot_general x4, matrix products, attention_backward(): jnp.einsum('bhqk,bhkd->bhqd', score_grad, keys, preferred_element_type=jn...  244 us
    reduce_scatter x1, waiting for transfers between devices, per_device(): lax.psum_scatter(lax.cond(first_half, normed_attention_term, normed_mlp_t...  187 us
    all_gather x1, waiting for transfers between devices, per_device(): normed = lax.all_gather(normed_own[None], 'tp', axis=0, tiled=True)  158 us
    dot_general x8, matrix products, masked_scores(): jnp.einsum('bhqd,bhkd->bhqk', query_block, key_block, preferred_element_t...  139 us
    dot_general x4, matrix products, attention_backward(): jnp.einsum('bhqk,bhqd->bhkd', weights.astype(jnp.bfloat16), grad_block, p...  83.9 us
  transfers between devices with their start and end apart: 10, of which 7 were waited for; matrix products, arithmetic and copies ran while one was open for 20% of the time, Pallas kernels for 0%

commit v1 on v0

v1 whole, which is shorter than its diff:
```python
from functools import partial
import math

import jax
import jax.numpy as jnp
from jax import lax
from jax.experimental import pallas as pl
from jax.experimental.pallas import tpu as pltpu
from jax.sharding import PartitionSpec as P

HD = 128
ROT = 32


EPSILON = 1e-05
NEGATIVE = -1e30
ROPE_BASE = 10000.0
LOG2E = math.log2(math.e)
F32 = jnp.float32
BF16 = jnp.bfloat16
CONTRACT_LAST = (((1,), (1,)), ((), ()))
CONTRACT_FIRST = (((0,), (0,)), ((), ()))
VMEM_BYTES = 56 * 1024 * 1024
ANY = pl.BlockSpec(memory_space=pl.ANY)


def params(steps):
    return pltpu.CompilerParams(
        dimension_semantics=("arbitrary",) * steps, vmem_limit_bytes=VMEM_BYTES
    )


def cost(flops, moved, transcendentals=0):
    return pl.CostEstimate(
        flops=int(flops), bytes_accessed=int(moved), transcendentals=int(transcendentals)
    )


def swap(value, axis, bit):
    size = lax.axis_size(axis)
    return lax.ppermute(value, axis, [(i, i ^ bit) for i in range(size)])


def onward(value, axis):
    size = lax.axis_size(axis)
    return lax.ppermute(value, axis, [(i, (i + 1) % size) for i in range(size)])


def after(value, other):
    return lax.optimization_barrier((value, other))[0]


def bit_orders(size):
    bits = [1 << k for k in range(size.bit_length() - 1)]
    return (bits, bits[::-1])


def last_bit(number, order):
    return [bit for bit in order if number & bit][-1]


def gather_tiles(own):
    size = lax.axis_size("tp")
    half = own.shape[0] // 2
    orders = bit_orders(size)
    whole = {0: own}
    halves = {}

    def part(j, q):
        return whole[j][q * half : (q + 1) * half] if j in whole else halves[j][q]

    for j in sorted(range(1, size), key=lambda j: bin(j).count("1")):
        steps = [(bit, j ^ bit) for bit in (last_bit(j, order) for order in orders)]
        if steps[0] == steps[1] and steps[0][1] in whole:
            whole[j] = swap(whole[steps[0][1]], "tp", steps[0][0])
        else:
            halves[j] = [swap(part(source, q), "tp", bit) for q, (bit, source) in enumerate(steps)]
    return whole, halves


def both_cores(whole, halves):
    entries = {}
    for j in list(whole) + list(halves):
        if j in whole:
            other = swap(whole[j], "branch", 1) if j else None
            entries[j] = [(whole[j], 0), (whole[j], 1), (other, 0), (other, 1)]
        else:
            others = [swap(item, "branch", 1) for item in halves[j]]
            entries[j] = [(item, 0) for item in halves[j]] + [(item, 0) for item in others]
    return entries


def reduce_tiles(pieces):
    size = lax.axis_size("tp")
    half = pieces[0].shape[0] // 2
    results = []
    for q, order in enumerate(bit_orders(size)):
        arrived = {j: [] for j in range(size)}
        for j in sorted(range(size), key=lambda j: -bin(j).count("1")):
            total = pieces[j][q * half : (q + 1) * half]
            if arrived[j] or j == 0:
                total = total.astype(F32)
                for item in arrived[j]:
                    total = total + item.astype(F32)
            if j == 0:
                results.append(total)
            else:
                bit = last_bit(j, order)
                arrived[j ^ bit].append(swap(total.astype(BF16), "tp", bit))
    return results


def ring_gather(piece, place, buffer):
    size = lax.axis_size("seq")
    me = lax.axis_index("seq")
    current = piece
    buffer = place(buffer, current, me)
    for step in range(1, size):
        current = onward(current, "seq")
        buffer = place(buffer, current, (me - step) % size)
    return buffer, current


def ring_scatter(block):
    size = lax.axis_size("seq")
    me = lax.axis_index("seq")
    total = block((me - 1) % size)
    for step in range(1, size):
        arrived = onward(total.astype(BF16), "seq")
        total = arrived.astype(F32) + block((me - 1 - step) % size).astype(F32)
    return total


def all_sum(value, axis):
    size = lax.axis_size(axis)
    bit = 1
    while bit < size:
        value = value + swap(value, axis, bit)
        bit *= 2
    return value


def rope(vectors, cosine, sine_up, sine_down):
    return (
        vectors * cosine
        + pltpu.roll(vectors, ROT // 2, 1) * sine_up
        + pltpu.roll(vectors, HD - ROT // 2, 1) * sine_down
    )


def norm_project_kernel(
    x0, x1, x2, x3, gain1, shift1, gain2, shift2, weight, bias, cosine, sine_up, sine_down, *rest
):
    normal, first, second, queries, keys, values, scratch = rest[-7:]
    step = pl.program_id(0)
    for number, x_ref in enumerate((x0, x1, x2, x3)):

        @pl.when(step == number)
        def _(x_ref=x_ref):
            scratch[...] = x_ref[...].astype(F32)

    x = scratch[...]
    centred = x - jnp.mean(x, axis=-1, keepdims=True)
    variance = jnp.mean(centred * centred, axis=-1, keepdims=True)
    n = centred * lax.rsqrt(variance + EPSILON)
    normal[...] = n.astype(BF16)
    second[...] = (n * gain2[...] + shift2[...]).astype(BF16)
    one = (n * gain1[...] + shift1[...]).astype(BF16)
    first[...] = one
    joined = jnp.dot(one, weight[...], preferred_element_type=F32) + bias[...]
    tables = (cosine[...], sine_up[...], sine_down[...])
    for head in range(queries.shape[0]):
        at = head * 3 * HD
        queries[head, 0, 0] = rope(joined[:, at : at + HD], *tables).astype(BF16)
        keys[head, 0, 0] = rope(joined[:, at + HD : at + 2 * HD], *tables).astype(BF16)
        values[head, 0, 0] = joined[:, at + 2 * HD : at + 3 * HD].astype(BF16)


def norm_project(j, entries, rows_in_all, gains, weight, bias, tables, held):
    rows = entries[1][0].shape[0] * (1 if entries[1][1] == 0 else 1)
    model_width, joined_cols = weight.shape
    heads = joined_cols // (3 * HD)
    size = lax.axis_size("tp")
    tile = rows_in_all // (2 * size)
    half = tile // 2
    steps = 4

    def fixed(block, *at):
        return pl.BlockSpec(block, lambda i: at)

    x_specs = [fixed((half, model_width), part, 0) for _, part in entries]
    row = fixed((1, model_width), 0, 0)
    table = pl.BlockSpec((half, HD), lambda i: (j * 4 + i, 0))
    wide = pl.BlockSpec((half, model_width), lambda i: (j * 4 + i, 0))
    narrow = pl.BlockSpec((heads, 1, 1, half, HD), lambda i: (0, j, i // 2, i % 2, 0))
    operands = [item for item, _ in entries] + list(gains) + [weight, bias] + list(tables)
    in_specs = (
        x_specs
        + [row] * 4
        + [fixed((model_width, joined_cols), 0, 0), fixed((1, joined_cols), 0, 0)]
        + [table] * 3
    )
    aliases = {}
    if held is not None:
        aliases = {len(operands) + k: k for k in range(6)}
        operands += list(held)
        in_specs += [ANY] * 6
    wide_shape = jax.ShapeDtypeStruct((rows_in_all, model_width), BF16)
    narrow_shape = jax.ShapeDtypeStruct((heads, size, 2, tile, HD), BF16)
    return pl.pallas_call(
        norm_project_kernel,
        grid=(steps,),
        in_specs=in_specs,
        out_specs=[wide] * 3 + [narrow] * 3,
        out_shape=[wide_shape] * 3 + [narrow_shape] * 3,
        scratch_shapes=[pltpu.VMEM((half, model_width), F32)],
        input_output_aliases=aliases,
        compiler_params=params(1),
        cost_estimate=cost(
            2 * 2 * tile * model_width * joined_cols, 2 * tile * model_width * 8 + weight.size * 2
        ),
        name="norm_project",
    )(*operands)


def attend_kernel(meta, q_ref, k_ref, v_ref, begin_ref, out_ref, lse_ref):
    seq_at, block = pl.program_id(1), pl.program_id(2)
    rows, blocks = q_ref.shape[-2], k_ref.shape[1]
    here = meta[0]
    low = meta[1 + seq_at * blocks + block]
    query = q_ref[0, 0, 0]
    begin = begin_ref[...]
    query_places = block * rows + lax.broadcasted_iota(jnp.int32, (rows, 1), 0)
    factor = LOG2E / math.sqrt(HD)

    def step(number, carry):
        top, total, mixed = carry
        key = k_ref[0, number ^ here, 0]
        value = v_ref[0, number ^ here, 0]
        scores = (
            lax.dot_general(query, key, CONTRACT_LAST, preferred_element_type=F32) * factor
        )
        key_places = number * rows + lax.broadcasted_iota(jnp.int32, (1, rows), 1)
        allowed = (key_places >= begin) & (key_places <= query_places)
        scores = jnp.where(allowed, scores, NEGATIVE)
        new_top = jnp.maximum(top, jnp.max(scores, axis=-1, keepdims=True))
        weights = jnp.exp2(scores - new_top)
        shrink = jnp.exp2(top - new_top)
        total = total * shrink + jnp.sum(weights, axis=-1, keepdims=True)
        mixed = mixed * shrink + jnp.dot(
            weights.astype(BF16), value, preferred_element_type=F32
        )
        return new_top, total, mixed

    top, total, mixed = lax.fori_loop(
        low,
        block + 1,
        step,
        (
            jnp.full((rows, 1), NEGATIVE, F32),
            jnp.zeros((rows, 1), F32),
            jnp.zeros((rows, HD), F32),
        ),
    )
    out_ref[...] = (mixed / total).astype(BF16)[None, None]
    log_sum = top + jnp.log(total) * LOG2E
    lse_ref[...] = jnp.broadcast_to(log_sum, (rows, HD)).T[:1][None, None, None]


def attend(meta, queries, keys, values, begin_column):
    heads, blocks, seqs, rows, _ = queries.shape

    def here(meta, i):
        return i ^ meta[0]

    one = pl.BlockSpec((1, 1, 1, rows, HD), lambda h, s, i, meta: (h, here(meta, i), s, 0, 0))
    full = pl.BlockSpec((1, blocks, 1, rows, HD), lambda h, s, i, meta: (h, 0, s, 0, 0))
    pairs = heads * seqs * blocks * (blocks + 1) // 2
    return pl.pallas_call(
        attend_kernel,
        grid_spec=pltpu.PrefetchScalarGridSpec(
            num_scalar_prefetch=1,
            grid=(heads, seqs, blocks),
            in_specs=[
                one,
                full,
                full,
                pl.BlockSpec((rows, 1), lambda h, s, i, meta: (here(meta, i) * seqs + s, 0)),
            ],
            out_specs=[
                pl.BlockSpec((1, 1, rows, HD), lambda h, s, i, meta: (here(meta, i), s, 0, h)),
                pl.BlockSpec(
                    (1, 1, 1, 1, rows), lambda h, s, i, meta: (h, here(meta, i), s, 0, 0)
                ),
            ],
        ),
        out_shape=[
            jax.ShapeDtypeStruct((blocks, seqs, rows, heads * HD), BF16),
            jax.ShapeDtypeStruct((heads, blocks, seqs, 1, rows), F32),
        ],
        compiler_params=params(3),
        cost_estimate=cost(
            pairs * 8 * rows * rows * HD, 4 * queries.size * 2, 4 * pairs * rows * rows
        ),
        name="attend",
    )(meta, queries, keys, values, begin_column)


def attend_back_kernel(
    meta,
    q_ref,
    k_ref,
    v_ref,
    grad_ref,
    out_ref,
    lse_ref,
    begin_ref,
    cosine,
    sine_up,
    sine_down,
    joined_ref,
    sum_ref,
    query_grad,
    delta,
):
    seq_at, block = pl.program_id(1), pl.program_id(2)
    blocks, rows = q_ref.shape[1], q_ref.shape[-2]
    here = meta[0]
    high = meta[1 + (2 + seq_at) * blocks + block]
    scaling = 1.0 / math.sqrt(HD)

    @pl.when(block == 0)
    def _():
        query_grad[...] = jnp.zeros_like(query_grad)

        def inner(j, carry):
            product = grad_ref[j, 0].astype(F32) * out_ref[j, 0].astype(F32)
            delta[j] = jnp.sum(product.T, axis=0, keepdims=True)
            return carry

        lax.fori_loop(0, blocks, inner, 0)

    own = block ^ here
    key = k_ref[0, own, 0]
    value = v_ref[0, own, 0]
    key_places = block * rows + lax.broadcasted_iota(jnp.int32, (rows, 1), 0)

    def step(number, carry):
        key_grad, value_grad = carry
        at = number ^ here
        query = q_ref[0, at, 0]
        grad = grad_ref[at, 0]
        scores = lax.dot_general(key, query, CONTRACT_LAST, preferred_element_type=F32)
        scores = scores * (scaling * LOG2E) - lse_ref[0, at, 0]
        query_places = number * rows + lax.broadcasted_iota(jnp.int32, (1, rows), 1)
        allowed = (key_places >= begin_ref[at, 0]) & (key_places <= query_places)
        weights = jnp.where(allowed, jnp.exp2(scores), 0.0)
        weight_grad = lax.dot_general(value, grad, CONTRACT_LAST, preferred_element_type=F32)
        score_grad = (weights * (weight_grad - delta[at]) * scaling).astype(BF16)
        value_grad = value_grad + jnp.dot(
            weights.astype(BF16), grad, preferred_element_type=F32
        )
        key_grad = key_grad + jnp.dot(score_grad, query, preferred_element_type=F32)
        query_grad[at] = query_grad[at] + lax.dot_general(
            score_grad, key, CONTRACT_FIRST, preferred_element_type=F32
        )
        return key_grad, value_grad

    empty = jnp.zeros((rows, HD), F32)
    key_grad, value_grad = lax.fori_loop(block, high + 1, step, (empty, empty))
    tables = (cosine[own, 0], -sine_up[own, 0], -sine_down[own, 0])
    joined_ref[own, 0, :, HD : 2 * HD] = rope(key_grad, *tables).astype(BF16)
    joined_ref[own, 0, :, 2 * HD :] = value_grad.astype(BF16)

    @pl.when(block == blocks - 1)
    def _():
        def inner(j, carry):
            tables = (cosine[j, 0], -sine_up[j, 0], -sine_down[j, 0])
            joined_ref[j, 0, :, :HD] = rope(query_grad[j], *tables).astype(BF16)
            return carry + jnp.sum(joined_ref[j, 0].astype(F32), axis=0, keepdims=True)

        sum_ref[0, 0] = lax.fori_loop(0, blocks, inner, jnp.zeros((1, 3 * HD), F32))


def attend_back(meta, queries, keys, values, grad, out, log_sums, begin_row, tables):
    heads, blocks, seqs, rows, _ = queries.shape
    head_spec = pl.BlockSpec((1, blocks, 1, rows, HD), lambda h, s, i, meta: (h, 0, s, 0, 0))
    side = pl.BlockSpec((blocks, 1, rows, HD), lambda h, s, i, meta: (0, s, 0, h))
    table = pl.BlockSpec((blocks, 1, rows, HD), lambda h, s, i, meta: (0, s, 0, 0))
    tables = [item.reshape(blocks, seqs, rows, HD) for item in tables]
    pairs = heads * seqs * blocks * (blocks + 1) // 2
    return pl.pallas_call(
        attend_back_kernel,
        grid_spec=pltpu.PrefetchScalarGridSpec(
            num_scalar_prefetch=1,
            grid=(heads, seqs, blocks),
            in_specs=[
                head_spec,
                head_spec,
                head_spec,
                side,
                side,
                pl.BlockSpec((1, blocks, 1, 1, rows), lambda h, s, i, meta: (h, 0, s, 0, 0)),
                pl.BlockSpec((blocks, 1, 1, rows), lambda h, s, i, meta: (0, s, 0, 0)),
                table,
                table,
                table,
            ],
            out_specs=[
                pl.BlockSpec((blocks, 1, rows, 3 * HD), lambda h, s, i, meta: (0, s, 0, h)),
                pl.BlockSpec((1, 1, 1, 3 * HD), lambda h, s, i, meta: (h, s, 0, 0)),
            ],
            scratch_shapes=[
                pltpu.VMEM((blocks, rows, HD), F32),
                pltpu.VMEM((blocks, 1, rows), F32),
            ],
        ),
        out_shape=[
            jax.ShapeDtypeStruct((blocks, seqs, rows, heads * 3 * HD), BF16),
            jax.ShapeDtypeStruct((heads, seqs, 1, 3 * HD), F32),
        ],
        compiler_params=params(3),
        cost_estimate=cost(
            pairs * 20 * rows * rows * HD, 12 * queries.size * 2, 4 * pairs * rows * rows
        ),
        name="attend_back",
    )(meta, queries, keys, values, grad, out, log_sums, begin_row, *tables)


def expand_kernel(rows_ref, weight, bias, activated, slope):
    cols = weight.shape[1]
    chunk = min(256, cols)
    left = rows_ref[...]
    for at in range(0, cols, chunk):
        pre = (
            jnp.dot(left, weight[:, at : at + chunk], preferred_element_type=F32)
            + bias[:, at : at + chunk]
        )
        share = 0.5 + 0.5 * lax.erf(pre * math.sqrt(0.5))
        density = jnp.exp2(pre * pre * (-0.5 * LOG2E)) * (1.0 / math.sqrt(2.0 * math.pi))
        activated[:, at : at + chunk] = (pre * share).astype(BF16)
        slope[:, at : at + chunk] = (share + pre * density).astype(BF16)


def expand(normed, weight, bias):
    rows, model_width = normed.shape
    cols = weight.shape[1]
    tile = 256
    out = pl.BlockSpec((tile, cols), lambda i: (i, 0))
    return pl.pallas_call(
        expand_kernel,
        grid=(rows // tile,),
        in_specs=[
            pl.BlockSpec((tile, model_width), lambda i: (i, 0)),
            pl.BlockSpec((model_width, cols), lambda i: (0, 0)),
            pl.BlockSpec((1, cols), lambda i: (0, 0)),
        ],
        out_specs=[out, out],
        out_shape=[jax.ShapeDtypeStruct((rows, cols), BF16)] * 2,
        compiler_params=params(1),
        cost_estimate=cost(
            2 * rows * model_width * cols,
            2 * (rows * model_width + weight.size + 2 * rows * cols),
            2 * rows * cols,
        ),
        name="expand",
    )(normed, weight, bias)


def output_kernel(att_ref, act_ref, dense, contract, keep, send):
    step = pl.program_id(0)
    total = jnp.dot(att_ref[...], dense[...], preferred_element_type=F32) + jnp.dot(
        act_ref[...], contract[...], preferred_element_type=F32
    )
    total = total.astype(BF16)
    half = pl.num_programs(0) // 2

    @pl.when(step < half)
    def _():
        keep[...] = total

    @pl.when(step >= half)
    def _():
        send[...] = total


def kept_and_sent(tile, steps, width):
    half = steps // 2
    return [
        pl.BlockSpec((tile, width), lambda i: (jnp.minimum(i, half - 1), 0)),
        pl.BlockSpec((tile, width), lambda i: (jnp.maximum(i - half, 0), 0)),
    ]


def output_piece(j, attended, activated, dense, contract):
    rows = attended.shape[0] // lax.axis_size("tp")
    width = dense.shape[1]
    tile = rows // 4
    shape = jax.ShapeDtypeStruct((rows // 2, width), BF16)
    return pl.pallas_call(
        output_kernel,
        grid=(4,),
        in_specs=[
            pl.BlockSpec((tile, attended.shape[1]), lambda i: (j * 4 + i, 0)),
            pl.BlockSpec((tile, activated.shape[1]), lambda i: (j * 4 + i, 0)),
            pl.BlockSpec(dense.shape, lambda i: (0, 0)),
            pl.BlockSpec(contract.shape, lambda i: (0, 0)),
        ],
        out_specs=kept_and_sent(tile, 4, width),
        out_shape=[shape, shape],
        compiler_params=params(1),
        cost_estimate=cost(
            2 * rows * width * (dense.shape[0] + contract.shape[0]),
            2 * (dense.size + contract.size + rows * (width + attended.shape[1] + activated.shape[1])),
        ),
        name="output_piece",
    )(attended, activated, dense, contract)


def pre_grad_kernel(grad_ref, slope, contract, out, sums):
    @pl.when(pl.program_id(0) == 0)
    def _():
        sums[...] = jnp.zeros_like(sums)

    left = grad_ref[...]
    cols = contract.shape[0]
    chunk = min(256, cols)
    for at in range(0, cols, chunk):
        part = lax.dot_general(
            left, contract[at : at + chunk, :], CONTRACT_LAST, preferred_element_type=F32
        )
        part = (part * slope[:, at : at + chunk].astype(F32)).astype(BF16)
        out[:, at : at + chunk] = part
        sums[:, at : at + chunk] += jnp.sum(part.astype(F32), axis=0, keepdims=True)


def pre_grad_of(grad, slope, contract):
    rows, width = grad.shape
    cols = contract.shape[0]
    tile = 256
    return pl.pallas_call(
        pre_grad_kernel,
        grid=(rows // tile,),
        in_specs=[
            pl.BlockSpec((tile, width), lambda i: (i, 0)),
            pl.BlockSpec((tile, cols), lambda i: (i, 0)),
            pl.BlockSpec((cols, width), lambda i: (0, 0)),
        ],
        out_specs=[
            pl.BlockSpec((tile, cols), lambda i: (i, 0)),
            pl.BlockSpec((1, cols), lambda i: (0, 0)),
        ],
        out_shape=[
            jax.ShapeDtypeStruct((rows, cols), BF16),
            jax.ShapeDtypeStruct((1, cols), F32),
        ],
        compiler_params=params(1),
        cost_estimate=cost(
            2 * rows * width * cols, 2 * (rows * width + contract.size + 2 * rows * cols)
        ),
        name="pre_grad",
    )(grad, slope, contract)


def normed_grad_kernel(joined, pre, normal, joined_weight, expand_weight, gain1, gain2, keep, send, sums):
    step = pl.program_id(0)
    half = pl.num_programs(0) // 2

    @pl.when(step == 0)
    def _():
        sums[...] = jnp.zeros_like(sums)

    width = joined_weight.shape[0]
    chunk = min(512, width)
    for at in range(0, width, chunk):
        cols = slice(at, at + chunk)
        first = lax.dot_general(
            joined[...], joined_weight[cols, :], CONTRACT_LAST, preferred_element_type=F32
        )
        second = lax.dot_general(
            pre[...], expand_weight[cols, :], CONTRACT_LAST, preferred_element_type=F32
        )
        n = normal[:, cols].astype(F32)
        sums[0:1, cols] += jnp.sum(first * n, axis=0, keepdims=True)
        sums[1:2, cols] += jnp.sum(first, axis=0, keepdims=True)
        sums[2:3, cols] += jnp.sum(second * n, axis=0, keepdims=True)
        sums[3:4, cols] += jnp.sum(second, axis=0, keepdims=True)
        total = (first * gain1[:, cols] + second * gain2[:, cols]).astype(BF16)

        @pl.when(step < half)
        def _(total=total, cols=cols):
            keep[:, cols] = total

        @pl.when(step >= half)
        def _(total=total, cols=cols):
            send[:, cols] = total


def normed_grad_piece(j, joined, pre, normal, joined_weight, expand_weight, gain1, gain2):
    rows = joined.shape[0] // lax.axis_size("tp")
    width = joined_weight.shape[0]
    tile = rows // 4
    shape = jax.ShapeDtypeStruct((rows // 2, width), BF16)
    return pl.pallas_call(
        normed_grad_kernel,
        grid=(4,),
        in_specs=[
            pl.BlockSpec((tile, joined.shape[1]), lambda i: (j * 4 + i, 0)),
            pl.BlockSpec((tile, pre.shape[1]), lambda i: (j * 4 + i, 0)),
            pl.BlockSpec((tile, width), lambda i: (j * 4 + i, 0)),
            pl.BlockSpec(joined_weight.shape, lambda i: (0, 0)),
            pl.BlockSpec(expand_weight.shape, lambda i: (0, 0)),
            pl.BlockSpec((1, width), lambda i: (0, 0)),
            pl.BlockSpec((1, width), lambda i: (0, 0)),
        ],
        out_specs=kept_and_sent(tile, 4, width) + [pl.BlockSpec((8, width), lambda i: (0, 0))],
        out_shape=[shape, shape, jax.ShapeDtypeStruct((8, width), F32)],
        compiler_params=params(1),
        cost_estimate=cost(
            2 * rows * width * (joined.shape[1] + pre.shape[1]),
            2 * (joined_weight.size + expand_weight.size)
            + 2 * rows * (2 * width + joined.shape[1] + pre.shape[1]),
        ),
        name="normed_grad_piece",
    )(joined, pre, normal, joined_weight, expand_weight, gain1, gain2)


def per_device(
    block_input,
    first_norm_gain,
    first_norm_bias,
    second_norm_gain,
    second_norm_bias,
    query_key_value,
    query_key_value_bias,
    attention_dense,
    attention_dense_bias,
    expand_weight,
    expand_bias,
    contract_weight,
    contract_bias,
    document_starts,
    output_grad,
):
    seqs, tile, model_width = block_input.shape
    tiles = lax.axis_size("tp")
    groups = lax.axis_size("seq")
    core = lax.axis_index("branch")
    here = lax.axis_index("tp")
    first_core = core == 0
    length = tile * tiles
    rows_in_all = length * seqs
    share = query_key_value.shape[0]

    def by_core(mine, others):
        return jnp.where(first_core, mine, others), jnp.where(first_core, others, mine)

    def halves_of(value, axis):
        size = value.shape[axis] // 2
        return (
            lax.dynamic_slice_in_dim(value, core * size, size, axis),
            lax.dynamic_slice_in_dim(value, (1 - core) * size, size, axis),
        )

    starts = jnp.stack(
        [
            lax.dynamic_index_in_dim(document_starts, core, 0, False),
            lax.dynamic_index_in_dim(document_starts, 1 - core, 0, False),
        ]
    )
    places = (
        (jnp.arange(tiles, dtype=jnp.int32) ^ here)[:, None] * tile
        + jnp.arange(tile, dtype=jnp.int32)[None, :]
    )[:, None, :]
    started = starts[None, :, None, :] <= places[..., None]
    begin_at = jnp.max(jnp.where(started, starts[None, :, None, :], 0), axis=-1)
    relative = (places - begin_at).astype(F32).reshape(rows_in_all, 1)
    exponent = jnp.arange(ROT // 2, dtype=F32) * (2.0 / ROT)
    angles = relative * (ROPE_BASE ** (-exponent))
    cosines, sines = jnp.cos(angles), jnp.sin(angles)
    rest = jnp.zeros((rows_in_all, HD - ROT), F32)
    nothing = jnp.zeros_like(sines)
    tables = (
        jnp.concatenate([cosines, cosines, rest + 1.0], axis=1),
        jnp.concatenate([nothing, sines, rest], axis=1),
        jnp.concatenate([-sines, nothing, rest], axis=1),
    )
    numbers = jnp.arange(tiles, dtype=jnp.int32)
    edges = numbers[None, :] * tile
    edge_begin = jnp.max(
        jnp.where(starts[:, None, :] <= edges[..., None], starts[:, None, :], 0), axis=-1
    )
    lows = edge_begin // tile
    highs = jnp.sum((lows[:, None, :] <= numbers[None, :, None]).astype(jnp.int32), axis=-1) - 1
    meta = jnp.concatenate(
        [here[None].astype(jnp.int32), lows.reshape(-1), highs.reshape(-1)]
    ).astype(jnp.int32)

    def row_piece(weight):
        mine, others = halves_of(weight, 1)
        return jnp.stack(by_core(mine, swap(others, "branch", 1)))

    def gather_rows(piece):
        buffer = jnp.zeros((2, groups) + piece.shape[1:], BF16)

        def place(buffer, item, at):
            return lax.dynamic_update_slice_in_dim(buffer, item[:, None], at, 1)

        buffer, last = ring_gather(piece, place, buffer)
        return buffer.reshape(-1, piece.shape[-1]), last

    def column_piece(weight):
        mine, others = halves_of(weight, 0)
        return jnp.stack(by_core(mine, swap(others, "branch", 1)))

    def gather_columns(piece):
        buffer = jnp.zeros((piece.shape[1], model_width), BF16)

        def place(buffer, item, at):
            for c in range(2):
                buffer = lax.dynamic_update_slice_in_dim(
                    buffer, item[c], (c * groups + at) * share, 1
                )
            return buffer

        return ring_gather(piece, place, buffer)

    joined_weight, last = gather_rows(row_piece(query_key_value))
    dense_full, last = gather_columns(after(column_piece(attention_dense), last))
    expand_full, last = gather_rows(after(row_piece(expand_weight), last))
    contract_full, last = gather_columns(after(column_piece(contract_weight), last))
    joined_bias = halves_of(query_key_value_bias, 0)[0].astype(F32)[None]
    hidden_bias = halves_of(expand_bias, 0)[0].astype(F32)[None]

    def own_and_other(value):
        return (
            lax.dynamic_index_in_dim(value, core, 0, False),
            lax.dynamic_index_in_dim(value, 1 - core, 0, False),
        )

    input_own, input_other = own_and_other(block_input)
    grad_own, grad_other = own_and_other(output_grad)
    whole, halves = gather_tiles(input_own)
    entries = both_cores(whole, halves)
    entries[0][2:] = [(input_other, 0), (input_other, 1)]
    last_input = [item for j in sorted(halves) for item in halves[j]] or [whole[tiles - 1]]
    whole, halves = gather_tiles(after(grad_own, tuple(last_input)))
    grad_entries = both_cores(whole, halves)
    grad_entries[0] = [(grad_own, 0), (grad_own, 1), (grad_other, 0), (grad_other, 1)]
    half = tile // 2
    grad_rows = jnp.concatenate(
        [
            item[part * half : (part + 1) * half]
            for j in range(tiles)
            for item, part in grad_entries[j]
        ]
    )

    gain1 = first_norm_gain.astype(F32)[None]
    gain2 = second_norm_gain.astype(F32)[None]
    gains = (
        gain1,
        first_norm_bias.astype(F32)[None],
        gain2,
        second_norm_bias.astype(F32)[None],
    )
    held = None
    for j in range(tiles):
        held = norm_project(
            j, entries[j], rows_in_all, gains, joined_weight, joined_bias, tables, held
        )
    normal, first_normed, second_normed, queries, keys, values = held
    attended, log_sums = attend(
        meta, queries, keys, values, begin_at.reshape(rows_in_all, 1)
    )
    attended_flat = attended.reshape(rows_in_all, -1)
    activated, slope = expand(second_normed, expand_full, hidden_bias)

    def reduced(pieces):
        summed = {}
        for j in sorted(pieces, key=lambda j: -bin(j).count("1")):
            keep, send = pieces[j]
            summed[j] = (keep.astype(F32) + swap(send, "branch", 1).astype(F32)).astype(BF16)
        return jnp.concatenate(reduce_tiles(summed))

    order = sorted(range(tiles), key=lambda j: -bin(j).count("1"))
    branch_sum = reduced(
        {j: output_piece(j, attended_flat, activated, dense_full, contract_full) for j in order}
    )
    output_own = (
        input_own.astype(F32)
        + branch_sum
        + attention_dense_bias.astype(F32)
        + contract_bias.astype(F32)
    ).astype(BF16)
    block_output = jnp.stack(by_core(output_own, swap(output_own, "branch", 1)))

    def weight_grad(left, right):
        return lax.dot_general(left, right, CONTRACT_FIRST, preferred_element_type=F32).astype(BF16)

    def scatter_rows(part):
        blocks = part.reshape(2, groups, share, part.shape[1])

        def block(at):
            return lax.dynamic_index_in_dim(blocks, at, 1, False)

        total = ring_scatter(block)
        mine, others = halves_of(total, 0)
        return jnp.concatenate(by_core(mine[0], swap(others[0], "branch", 1)), axis=1)

    def scatter_columns(part):
        def block(at):
            return jnp.stack(
                [
                    lax.dynamic_slice_in_dim(part, (c * groups + at) * share, share, 1)
                    for c in range(2)
                ]
            )

        total = ring_scatter(block)
        mine, others = halves_of(total, 0)
        return jnp.concatenate(by_core(mine[0], swap(others[0], "branch", 1)), axis=0)

    contract_grad = scatter_columns(weight_grad(activated, grad_rows))
    dense_grad = scatter_columns(weight_grad(attended_flat, grad_rows))
    attended_grad = lax.dot_general(
        grad_rows, dense_full, CONTRACT_LAST, preferred_element_type=F32
    ).astype(BF16)
    joined_grad, joined_sums = attend_back(
        meta,
        queries,
        keys,
        values,
        attended_grad.reshape(attended.shape),
        attended,
        log_sums,
        begin_at[:, :, None, :],
        tables,
    )
    joined_grad = joined_grad.reshape(rows_in_all, -1)
    pre_grad, pre_sums = pre_grad_of(grad_rows, slope, contract_full)
    expand_grad = scatter_rows(weight_grad(second_normed, pre_grad))
    query_key_value_grad = scatter_rows(weight_grad(first_normed, joined_grad))
    normed_pieces = {}
    sums = jnp.zeros((8, model_width), F32)
    for j in order:
        keep, send, part = normed_grad_piece(
            j, joined_grad, pre_grad, normal, joined_weight, expand_full, gain1, gain2
        )
        normed_pieces[j] = (keep, send)
        sums = sums + part
    term_sum = reduced(normed_pieces)
    x = input_own.astype(F32)
    centred = x - jnp.mean(x, axis=-1, keepdims=True)
    rate = lax.rsqrt(jnp.mean(centred * centred, axis=-1, keepdims=True) + EPSILON)
    n = centred * rate
    terms = rate * (
        term_sum
        - jnp.mean(term_sum, axis=-1, keepdims=True)
        - n * jnp.mean(term_sum * n, axis=-1, keepdims=True)
    )
    grad_own_wide = grad_own.astype(F32)
    input_grad_own = (grad_own_wide + terms).astype(BF16)
    input_grad = jnp.stack(by_core(input_grad_own, swap(input_grad_own, "branch", 1)))

    joined_part = jnp.sum(joined_sums, axis=1).reshape(-1)
    hidden_part = pre_sums[0]
    small = jnp.concatenate(
        [
            sums[:4].reshape(-1),
            jnp.sum(grad_own_wide, axis=0),
            joined_part,
            hidden_part,
        ]
    )
    small = all_sum(small, "seq")
    everywhere = 5 * model_width
    per_core = small[everywhere:]
    both = jnp.stack(by_core(per_core, swap(per_core, "branch", 1)))
    query_key_value_bias_grad = both[:, : joined_part.shape[0]].reshape(-1)
    expand_bias_grad = both[:, joined_part.shape[0] :].reshape(-1)
    shared = all_sum(all_sum(small[:everywhere], "tp"), "branch").reshape(5, model_width)
    return (
        block_output,
        input_grad,
        shared[0],
        shared[1],
        shared[2],
        shared[3],
        query_key_value_grad,
        query_key_value_bias_grad,
        dense_grad,
        shared[4],
        expand_grad,
        expand_bias_grad,
        contract_grad,
        shared[4],
    )


def solution(mesh):
    in_specs = (
        P("seq", "tp", None),
        P(),
        P(),
        P(),
        P(),
        P(("branch", "seq"), "tp"),
        P("tp"),
        P("tp", ("branch", "seq")),
        P(),
        P(("branch", "seq"), "tp"),
        P("tp"),
        P("tp", ("branch", "seq")),
        P(),
        P("seq", None),
        P("seq", "tp", None),
    )
    out_specs = (
        P("seq", "tp", None),
        P("seq", "tp", None),
        P(),
        P(),
        P(),
        P(),
        P(("branch", "seq"), "tp"),
        P("tp"),
        P("tp", ("branch", "seq")),
        P(),
        P(("branch", "seq"), "tp"),
        P("tp"),
        P("tp", ("branch", "seq")),
        P(),
    )
    return jax.shard_map(
        per_device, mesh=mesh, in_specs=in_specs, out_specs=out_specs, check_vma=False
    )
```

time: 2900 us -> 996 us (0.34)
  matrix products: 1030 us -> 77.6 us
  waiting for transfers between devices: 1250 us -> 334 us
  Pallas kernels: 0 us -> 318 us
  local copies, waits for them, and re-layouts: 274 us -> 92.4 us
  other arithmetic: 230 us -> 92.8 us
  blocking collectives: 76.4 us -> 0 us
  starting transfers between devices: 0.65 us -> 69.1 us
    dot_general x34 -> x5, matrix products: 1030 us -> 77.6 us  [the longest x4 70.6 us: weight_grad(): lax.dot_general(left, right, CONTRACT_FIRST, preferred_element_type=F32)]
    reduce_scatter x3 -> x0, waiting for transfers between devices: 911 us -> none  [the longest x1 450 us: per_device(): lax.psum_scatter(lax.cond(first_half, weight_attention_term, weight_mlp_t...]
    ppermute x0 -> x76, waiting for transfers between devices: none -> 334 us  [the longest x24 199 us: onward(): return lax.ppermute(value, axis, [(i, (i + 1) % size) for i in range(size)])]
    pallas_call x0 -> x16, Pallas kernels: none -> 318 us  [the longest x4 71.9 us: normed_grad_piece(): pl.pallas_call(normed_grad_kernel, grid=(4,), in_specs=[pl.BlockSpec((til...]
    all_gather x6 -> x0, waiting for transfers between devices: 287 us -> none  [the longest x1 158 us: per_device(): normed = lax.all_gather(normed_own[None], 'tp', axis=0, tiled=True)]
    reshape x6 -> x2, local copies, waits for them, and re-layouts: 98 us -> 0.62 us  [the longest x1 0.61 us: per_device(): query_key_value_bias_grad = both[:, :joined_part.shape[0]].reshape(-1)]
    convert_element_type x7 -> x0, local copies, waits for them, and re-layouts: 97.3 us -> none  [the longest x3 58 us: attention_back(): joined_grad = to_tiles(joined_grad, tiles).astype(jnp.bfloat16)]
    reduce_sum x12 -> x6, other arithmetic: 100 us -> 6.29 us  [the longest x1 2.36 us: per_device(): jnp.sum(grad_own_wide, axis=0)]
  transfers between devices with their start and end apart: 10 -> 76, of which waited for: 7 -> 26; matrix products, arithmetic and copies ran while one was open for 20% -> 25% of each run, Pallas kernels for 0% -> 32%
where the time goes in v1:
time: 996 us; the launch traced here: 985 us
  waiting for transfers between devices  334 us (34%)
  Pallas kernels  318 us (32%)
  other arithmetic  92.8 us (9%)
  local copies, waits for them, and re-layouts  92.4 us (9%)
  matrix products  77.6 us (8%)
  starting transfers between devices  69.1 us (7%)
    ppermute x24, waiting for transfers between devices, onward(): return lax.ppermute(value, axis, [(i, (i + 1) % size) for i in range(size)])  199 us
    ppermute x52, waiting for transfers between devices, swap(): return lax.ppermute(value, axis, [(i, i ^ bit) for i in range(size)])  135 us
    pallas_call x4, Pallas kernels, normed_grad_piece(): pl.pallas_call(normed_grad_kernel, grid=(4,), in_specs=[pl.BlockSpec((til...  71.9 us
    dot_general x4, matrix products, weight_grad(): lax.dot_general(left, right, CONTRACT_FIRST, preferred_element_type=F32)  70.6 us
    pallas_call x1, Pallas kernels, attend_back(): pl.pallas_call(attend_back_kernel, grid_spec=pltpu.PrefetchScalarGridSpec...  54.6 us
    pallas_call x4, Pallas kernels, norm_project(): pl.pallas_call(norm_project_kernel, grid=(steps,), in_specs=in_specs, out...  53.2 us
    pallas_call x4, Pallas kernels, output_piece(): pl.pallas_call(output_kernel, grid=(4,), in_specs=[pl.BlockSpec((tile, at...  44.4 us
    pallas_call x1, Pallas kernels, attend(): pl.pallas_call(attend_kernel, grid_spec=pltpu.PrefetchScalarGridSpec(num_...  37 us
  transfers between devices with their start and end apart: 76, of which 26 were waited for; matrix products, arithmetic and copies ran while one was open for 25% of the time, Pallas kernels for 32%

profile of v1, /device:TPU:0, one launch (start us, length us, event | category | flops | bytes accessed | tf_op | source)
XLA Modules:
  0.0 985.5 jit_solution(1674499432775073036)
XLA Ops:
  87.0 17.5 %collective-permute-done.8 = bf16[2,256,768]{2,1,0:T(8,128)(2,1)S(1)} collective-permute-done((bf16[2,256,768]{2,1,0:T(8,128)(2,1)}, bf16[2,256,768]{2,1,0:T(8,128)(2,1)S(1)}, u32[]{:S(2)}, u32[]{:S(2)}) %collective-permute-start.8) | collective-permute-done | bytes 786464 | tf_op jit(solution)/shard_map/ppermute | solution.py:46
  112.5 12.3 %collective-permute-done.9 = bf16[2,256,768]{2,1,0:T(8,128)(2,1)S(1)} collective-permute-done((bf16[2,256,768]{2,1,0:T(8,128)(2,1)S(1)}, bf16[2,256,768]{2,1,0:T(8,128)(2,1)S(1)}, u32[]{:S(2)}, u32[]{:S(2)}) %collective-permute-start.9) | collective-permute-done | bytes 786464 | tf_op jit(solution)/shard_map/ppermute | solution.py:46
  133.0 13.1 %norm_project.4 = (bf16[4096,2048]{1,0:T(8,128)(2,1)}, bf16[4096,2048]{1,0:T(8,128)(2,1)}, bf16[4096,2048]{1,0:T(8,128)(2,1)}, bf16[2,4,2,512,128]{4,3,2,1,0:T(8...) custom-call(bf16[512,2048]{1,0:T(8,128)(2,1)} %copy-done.2, ...), custom_call_target="tpu_custom_call" | custom-call | flops 3221225472 | bytes 19922944 | tf_op jit(solution)/shard_map/norm_project/pallas_call | solution.py:210
  162.4 16.9 %collective-permute-done.17 = bf16[2,256,1024]{2,1,0:T(8,128)(2,1)} collective-permute-done((bf16[2,256,1024]{2,1,0:T(8,128)(2,1)S(1)}, bf16[2,256,1024]{2,1,0:T(8,128)(2,1)}, u32[]{:S(2)}, u32[]{:S(2)}) %collective-permute-start.17) | collective-permute-done | bytes 1048608 | tf_op jit(solution)/shard_map/ppermute | solution.py:46
  180.0 13.4 %norm_project.5 = (bf16[4096,2048]{1,0:T(8,128)(2,1)}, bf16[4096,2048]{1,0:T(8,128)(2,1)}, bf16[4096,2048]{1,0:T(8,128)(2,1)}, bf16[2,4,2,512,128]{4,3,2,1,0:T(8...) custom-call(bf16[512,2048]{1,0:T(8,128)(2,1)} %collective-permute-do, ...), custom_call_target="tpu_custom_call", output_to_operand_aliasing={{0}: (13, {}), {1}: (14, {}), {2}: (15, {}), {3}: (16, {}),... | custom-call | flops 3221225472 | bytes 19922944 | tf_op jit(solution)/shard_map/norm_project/pallas_call | solution.py:210
  193.4 13.4 %norm_project.6 = (bf16[4096,2048]{1,0:T(8,128)(2,1)}, bf16[4096,2048]{1,0:T(8,128)(2,1)}, bf16[4096,2048]{1,0:T(8,128)(2,1)}, bf16[2,4,2,512,128]{4,3,2,1,0:T(8...) custom-call(bf16[512,2048]{1,0:T(8,128)(2,1)} %collective-permute-do, ...), custom_call_target="tpu_custom_call", output_to_operand_aliasing={{0}: (13, {}), {1}: (14, {}), {2}: (15, {}), {3}: (16, {}),... | custom-call | flops 3221225472 | bytes 19922944 | tf_op jit(solution)/shard_map/norm_project/pallas_call | solution.py:210
  206.8 13.4 %norm_project.7 = (bf16[4096,2048]{1,0:T(8,128)(2,1)}, bf16[4096,2048]{1,0:T(8,128)(2,1)}, bf16[4096,2048]{1,0:T(8,128)(2,1)}, bf16[2,4,2,512,128]{4,3,2,1,0:T(8...) custom-call(bf16[256,2048]{1,0:T(8,128)(2,1)} %collective-permute-do, ...), custom_call_target="tpu_custom_call", output_to_operand_aliasing={{0}: (13, {}), {1}: (14, {}), {2}: (15, {}), {3}: (16, {}),... | custom-call | flops 3221225472 | bytes 19922944 | tf_op jit(solution)/shard_map/norm_project/pallas_call | solution.py:210
  228.3 37.0 %attend.1 = (bf16[4,2,512,256]{3,2,1,0:T(8,128)(2,1)}, f32[2,4,2,1,512]{4,3,2,1,0:T(1,128)}) custom-call(s32[17]{0:T(128)} %pad_add_fusion.1.meta, bf16[2,4,2,512,128]{4,3,2,1,0:T(8,128)(2,1)} %get-tuple-element.88.q_ref, bf16[2,4,2,512,128]{4,3,2,1,0:T(8,128)(2,1)} %get-tuple-element.89.k_ref, bf16[2,4,2,512,128]{4,3,2,1,0:T(8,128)(2,1)} %get-tuple-element.90.v_ref, ...), custom_call_target="tpu_custom_call" | custom-call | flops 10737418240 | bytes 8388608 | tf_op jit(solution)/shard_map/attend/pallas_call | solution.py:279
  288.7 29.1 %expand.1 = (bf16[4096,1024]{1,0:T(8,128)(2,1)}, bf16[4096,1024]{1,0:T(8,128)(2,1)}) custom-call(bf16[4096,2048]{1,0:T(8,128)(2,1)} %get-tuple-element.92.rows_ref, bf16[2048,1024]{1,0:T(8,128)(2,1)} %bitcast.261, f32[1,1024]{1,0:T(1,128)} %bitcast.314), custom_call_target="tpu_custom_call" | custom-call | flops 17179869184 | bytes 37748736 | tf_op jit(solution)/shard_map/expand/pallas_call | solution.py:450
  335.0 23.0 %convolution_convert_fusion.1 = bf16[1024,2048]{1,0:T(8,128)(2,1)S(1)} fusion(bf16[4096,1024]{1,0:T(8,128)(2,1)} %get-tuple-element.95.act_ref, bf16[4096,2048]{1,0:T(8,128)(2,1)} %constant_dynamic-update-slice_fusion.grad_ref), kind=kOutput, calls=%fused_computation.29 | convolution fusion | flops 17181966336 | bytes 29360128 | tf_op jit(solution)/shard_map/dot_general | solution.py:799
  379.0 54.6 %attend_back.1 = (bf16[4,2,512,768]{3,2,1,0:T(8,128)(2,1)}, f32[2,2,1,384]{3,2,1,0:T(1,128)}) custom-call(s32[17]{0:T(128)} %pad_add_fusion.1.meta, bf16[2,4,2,512,128]{4,3,2,1,0:T(8,128)(2,1)} %get-tuple-element.88.q_ref, bf16[2,4,2,512,128]{4,3,2,1,0:T(8,128)(2,1)} %get-tuple-element.89.k_ref, bf16[2,4,2,512,128]{4,3,2,1,0:T(8,128)(2,1)} %get-tuple-element.90.v_ref, ...), custom_call_target="tpu_custom_call" | custom-call | flops 26843545600 | bytes 25165824 | tf_op jit(solution)/shard_map/attend_back/pallas_call | solution.py:392
  433.6 20.1 %convolution_convert_fusion.3 = bf16[2048,768]{1,0:T(8,128)(2,1)} fusion(bf16[4096,2048]{1,0:T(8,128)(2,1)} %get-tuple-element.125, bf16[4096,768]{1,0:T(8,128)(2,1)} %bitcast.266), kind=kOutput, calls=%fused_computation.31 | convolution fusion | flops 12886474752 | bytes 26214400 | tf_op jit(solution)/shard_map/dot_general | solution.py:799
  467.1 17.7 %collective-permute-done.65 = bf16[2,256,256]{2,1,0:T(8,128)(2,1)S(1)} collective-permute-done((bf16[2,256,256]{2,1,0:T(8,128)(2,1)S(1)}, bf16[2,256,256]{2,1,0:T(8,128)(2,1)S(1)}, u32[]{:S(2)}, u32[]{:S(2)}) %collective-permute-start.65) | collective-permute-done | bytes 262176 | tf_op jit(solution)/shard_map/ppermute | solution.py:46
  487.7 25.2 %collective-permute-done.66 = bf16[2,256,256]{2,1,0:T(8,128)(2,1)S(1)} collective-permute-done((bf16[2,256,256]{2,1,0:T(8,128)(2,1)S(1)}, bf16[2,256,256]{2,1,0:T(8,128)(2,1)S(1)}, u32[]{:S(2)}, u32[]{:S(2)}) %collective-permute-start.66) | collective-permute-done | bytes 262176 | tf_op jit(solution)/shard_map/ppermute | solution.py:46
  514.7 15.0 %collective-permute-done.60 = bf16[2,256,768]{2,1,0:T(8,128)(2,1)S(1)} collective-permute-done((bf16[2,256,768]{2,1,0:T(8,128)(2,1)S(1)}, bf16[2,256,768]{2,1,0:T(8,128)(2,1)S(1)}, u32[]{:S(2)}, u32[]{:S(2)}) %collective-permute-start.60) | collective-permute-done | bytes 786464 | tf_op jit(solution)/shard_map/ppermute | solution.py:46
  535.0 17.2 %collective-permute-done.73 = bf16[2,1024,256]{2,1,0:T(8,128)(2,1)S(1)} collective-permute-done((bf16[2,1024,256]{2,1,0:T(8,128)(2,1)S(1)}, bf16[2,1024,256]{2,1,0:T(8,128)(2,1)S(1)}, u32[]{:S(2)}, u32[]{:S(2)}) %collective-permute-start.73) | collective-permute-done | bytes 1048608 | tf_op jit(solution)/shard_map/ppermute | solution.py:46
  553.6 15.5 %collective-permute-done.61 = bf16[2,256,768]{2,1,0:T(8,128)(2,1)S(1)} collective-permute-done((bf16[2,256,768]{2,1,0:T(8,128)(2,1)S(1)}, bf16[2,256,768]{2,1,0:T(8,128)(2,1)S(1)}, u32[]{:S(2)}, u32[]{:S(2)}) %collective-permute-start.61) | collective-permute-done | bytes 786464 | tf_op jit(solution)/shard_map/ppermute | solution.py:46
  569.3 22.2 %collective-permute-done.23 = bf16[2,1024,256]{2,1,0:T(8,128)(2,1)S(1)} collective-permute-done((bf16[2,1024,256]{2,1,0:T(8,128)(2,1)S(1)}, bf16[2,1024,256]{2,1,0:T(8,128)(2,1)S(1)}, u32[]{:S(2)}, u32[]{:S(2)}) %collective-permute-start.23) | collective-permute-done | bytes 1048608 | tf_op jit(solution)/shard_map/ppermute | solution.py:46
  593.2 27.3 %pre_grad.1 = (bf16[4096,1024]{1,0:T(8,128)(2,1)}, f32[1,1024]{1,0:T(1,128)}) custom-call(bf16[4096,2048]{1,0:T(8,128)(2,1)} %constant_dynamic-update-slice_fusion.grad_ref, bf16[4096,1024]{1,0:T(8,128)(2,1)} %get-tuple-element.108.slope, bf16[1024,2048]{1,0:T(8,128)(2,1)} %fusion.23.contract), custom_call_target="tpu_custom_call" | custom-call | flops 17179869184 | bytes 37748736 | tf_op jit(solution)/shard_map/pre_grad/pallas_call | solution.py:541
  620.5 18.0 %normed_grad_piece.4 = (bf16[512,2048]{1,0:T(8,128)(2,1)}, bf16[512,2048]{1,0:T(8,128)(2,1)}, f32[8,2048]{1,0:T(8,128)}) custom-call(bf16[4096,768]{1,0:T(8,128)(2,1)} %bitcast.267, bf16[4096,1024]{1,0:T(8,128)(2,1)} %get-tuple-element.109.pre, bf16[4096,2048]{1,0:T(8,128)(2,1)} %get-tuple-element.110.normal, bf16[2048,768]{1,0:T(8,128)(2,1)} %bitcast.257, ...), custom_call_target="tpu_custom_call" | custom-call | flops 7516192768 | bytes 19398656 | tf_op jit(solution)/shard_map/normed_grad_piece/pallas_call | solution.py:604
  638.5 18.0 %normed_grad_piece.5 = (bf16[512,2048]{1,0:T(8,128)(2,1)}, bf16[512,2048]{1,0:T(8,128)(2,1)}, f32[8,2048]{1,0:T(8,128)}) custom-call(bf16[4096,768]{1,0:T(8,128)(2,1)} %bitcast.268, bf16[4096,1024]{1,0:T(8,128)(2,1)} %get-tuple-element.109.pre, bf16[4096,2048]{1,0:T(8,128)(2,1)} %get-tuple-element.110.normal, bf16[2048,768]{1,0:T(8,128)(2,1)} %bitcast.258, ...), custom_call_target="tpu_custom_call" | custom-call | flops 7516192768 | bytes 19398656 | tf_op jit(solution)/shard_map/normed_grad_piece/pallas_call | solution.py:604
  656.5 18.0 %normed_grad_piece.6 = (bf16[512,2048]{1,0:T(8,128)(2,1)}, bf16[512,2048]{1,0:T(8,128)(2,1)}, f32[8,2048]{1,0:T(8,128)}) custom-call(bf16[4096,768]{1,0:T(8,128)(2,1)} %bitcast.269, bf16[4096,1024]{1,0:T(8,128)(2,1)} %get-tuple-element.109.pre, bf16[4096,2048]{1,0:T(8,128)(2,1)} %get-tuple-element.110.normal, bf16[2048,768]{1,0:T(8,128)(2,1)} %bitcast.259, ...), custom_call_target="tpu_custom_call" | custom-call | flops 7516192768 | bytes 19398656 | tf_op jit(solution)/shard_map/normed_grad_piece/pallas_call | solution.py:604
  674.5 17.9 %normed_grad_piece.7 = (bf16[512,2048]{1,0:T(8,128)(2,1)}, bf16[512,2048]{1,0:T(8,128)(2,1)}, f32[8,2048]{1,0:T(8,128)}) custom-call(bf16[4096,768]{1,0:T(8,128)(2,1)} %bitcast.270, bf16[4096,1024]{1,0:T(8,128)(2,1)} %get-tuple-element.109.pre, bf16[4096,2048]{1,0:T(8,128)(2,1)} %get-tuple-element.110.normal, bf16[2048,768]{1,0:T(8,128)(2,1)} %bitcast.260, ...), custom_call_target="tpu_custom_call" | custom-call | flops 7516192768 | bytes 19398656 | tf_op jit(solution)/shard_map/normed_grad_piece/pallas_call | solution.py:604
  692.4 23.0 %convolution_convert_fusion.2 = bf16[2048,1024]{1,0:T(8,128)(2,1)S(1)} fusion(bf16[4096,2048]{1,0:T(8,128)(2,1)} %get-tuple-element.92.rows_ref, bf16[4096,1024]{1,0:T(8,128)(2,1)} %get-tuple-element.109.pre), kind=kOutput, calls=%fused_computation.30 | convolution fusion | flops 17181966336 | bytes 29360128 | tf_op jit(solution)/shard_map/dot_general | solution.py:799
  715.4 12.2 %output_piece.6 = (bf16[512,2048]{1,0:T(8,128)(2,1)}, bf16[512,2048]{1,0:T(8,128)(2,1)}) custom-call(bf16[4096,256]{1,0:T(8,128)(2,1)} %bitcast.275, bf16[4096,1024]{1,0:T(8,128)(2,1)} %get-tuple-element.95.act_ref, bf16[256,2048]{1,0:T(8,128)(2,1)} %fusion.29.dense, bf16[1024,2048]{1,0:T(8,128)(2,1)} %fusion.23.contract), custom_call_target="tpu_custom_call" | custom-call | flops 5368709120 | bytes 12058624 | tf_op jit(solution)/shard_map/output_piece/pallas_call | solution.py:500
  755.9 11.6 %collective-permute-done.55 = f32[12032]{0:T(1024)S(1)} collective-permute-done((f32[12032]{0:T(1024)S(1)}, f32[12032]{0:T(1024)S(1)}, u32[]{:S(2)}, u32[]{:S(2)}) %collective-permute-start.55) | collective-permute-done | bytes 48160 | tf_op jit(solution)/shard_map/ppermute | solution.py:41
  791.5 19.0 %collective-permute-done.69 = bf16[2,256,1024]{2,1,0:T(8,128)(2,1)} collective-permute-done((bf16[2,256,1024]{2,1,0:T(8,128)(2,1)}, bf16[2,256,1024]{2,1,0:T(8,128)(2,1)}, u32[]{:S(2)}, u32[]{:S(2)}) %collective-permute-start.69) | collective-permute-done | bytes 1048608 | tf_op jit(solution)/shard_map/ppermute | solution.py:46
  832.8 16.4 %collective-permute-done.32 = bf16[256,2048]{1,0:T(8,128)(2,1)S(1)} collective-permute-done((bf16[256,2048]{1,0:T(8,128)(2,1)}, bf16[256,2048]{1,0:T(8,128)(2,1)S(1)}, u32[]{:S(2)}, u32[]{:S(2)}) %collective-permute-start.32) | collective-permute-done | bytes 1048608 | tf_op jit(solution)/shard_map/ppermute | solution.py:41
  853.1 40.2 %collective-permute-done.51 = bf16[256,2048]{1,0:T(8,128)(2,1)S(1)} collective-permute-done((bf16[256,2048]{1,0:T(8,128)(2,1)S(1)}, bf16[256,2048]{1,0:T(8,128)(2,1)S(1)}, u32[]{:S(2)}, u32[]{:S(2)}) %collective-permute-start.51) | collective-permute-done | bytes 1048608 | tf_op jit(solution)/shard_map/ppermute | solution.py:41
  899.8 19.6 %collective-permute-done.33 = bf16[256,2048]{1,0:T(8,128)(2,1)S(1)} collective-permute-done((bf16[256,2048]{1,0:T(8,128)(2,1)S(1)}, bf16[256,2048]{1,0:T(8,128)(2,1)S(1)}, u32[]{:S(2)}, u32[]{:S(2)}) %collective-permute-start.33) | collective-permute-done | bytes 1048608 | tf_op jit(solution)/shard_map/ppermute | solution.py:41
  922.6 21.3 %collective-permute-done.50 = bf16[256,2048]{1,0:T(8,128)(2,1)S(1)} collective-permute-done((bf16[256,2048]{1,0:T(8,128)(2,1)S(1)}, bf16[256,2048]{1,0:T(8,128)(2,1)S(1)}, u32[]{:S(2)}, u32[]{:S(2)}) %collective-permute-start.50) | collective-permute-done | bytes 1048608 | tf_op jit(solution)/shard_map/ppermute | solution.py:41
  944.1 18.4 %collective-permute-done.52 = bf16[256,2048]{1,0:T(8,128)(2,1)S(1)} collective-permute-done((bf16[256,2048]{1,0:T(8,128)(2,1)S(1)}, bf16[256,2048]{1,0:T(8,128)(2,1)S(1)}, u32[]{:S(2)}, u32[]{:S(2)}) %collective-permute-start.52) | collective-permute-done | bytes 1048608 | tf_op jit(solution)/shard_map/ppermute | solution.py:41
  (442 shorter events, 325.6 us)
Async XLA Ops:
  2.7 104.4 %collective-permute-start = (bf16[512,2048]{1,0:T(8,128)(2,1)S(1)}, bf16[512,2048]{1,0:T(8,128)(2,1)}, u32[]{:S(2)}, u32[]{:S(2)}) collective-permute-start(bf16[512,2048]{1,0:T(8,128)(2,1)S(1)} %get-tuple-element.131.x0.x1), channel_id=1, source_target_pairs={{0,4},{4,0},{8,12},{12,8},{1,5},{5,1},{9,13},{13,9},{2,6},{6,2},{1... | collective-permute-start | bytes 6291464 | tf_op jit(solution)/shard_map/ppermute | solution.py:41
  5.7 103.3 %collective-permute-start.2 = (bf16[512,2048]{1,0:T(8,128)(2,1)S(1)}, bf16[512,2048]{1,0:T(8,128)(2,1)}, u32[]{:S(2)}, u32[]{:S(2)}) collective-permute-start(bf16[512,2048]{1,0:T(8,128)(2,1)S(1)} %get-tuple-element.131.x0.x1), channel_id=1, source_target_pairs={{0,8},{4,12},{8,0},{12,4},{1,9},{5,13},{9,1},{13,5},{2,10},{6,14},... | collective-permute-start | bytes 6291464 | tf_op jit(solution)/shard_map/ppermute | solution.py:41
  9.0 50.9 %collective-permute-start.6 = (bf16[256,768]{1,0:T(8,128)(2,1)}, bf16[256,768]{1,0:T(8,128)(2,1)S(1)}, u32[]{:S(2)}, u32[]{:S(2)}) collective-permute-start(bf16[256,768]{1,0:T(8,128)(2,1)} %constant_dynamic-slice_fusion.3), channel_id=1, source_target_pairs={{0,16},{16,0},{1,17},{17,1},{2,18},{18,2},{3,19},{19,3},{4,20},{20... | collective-permute-start | bytes 1179656 | tf_op jit(solution)/shard_map/ppermute | solution.py:41
  10.6 65.8 %collective-permute-start.13 = (bf16[256,256]{1,0:T(8,128)(2,1)}, bf16[256,256]{1,0:T(8,128)(2,1)}, u32[]{:S(2)}, u32[]{:S(2)}) collective-permute-start(bf16[256,256]{1,0:T(8,128)(2,1)} %constant_dynamic-slice_fusion.1), channel_id=1, source_target_pairs={{0,16},{16,0},{1,17},{17,1},{2,18},{18,2},{3,19},{19,3},{4,20},{20... | collective-permute-start | bytes 393224 | tf_op jit(solution)/shard_map/ppermute | solution.py:41
  11.9 72.5 %collective-permute-start.12 = (bf16[256,1024]{1,0:T(8,128)(2,1)}, bf16[256,1024]{1,0:T(8,128)(2,1)}, u32[]{:S(2)}, u32[]{:S(2)}) collective-permute-start(bf16[256,1024]{1,0:T(8,128)(2,1)} %constant_dynamic-slice_fusion.2), channel_id=1, source_target_pairs={{0,16},{16,0},{1,17},{17,1},{2,18},{18,2},{3,19},{19,3},{4,20},{20... | collective-permute-start | bytes 1572872 | tf_op jit(solution)/shard_map/ppermute | solution.py:41
  108.5 49.1 %collective-permute-start.1 = (bf16[256,2048]{1,0:T(8,128)(2,1)S(1)}, bf16[256,2048]{1,0:T(8,128)(2,1)}, u32[]{:S(2)}, u32[]{:S(2)}) collective-permute-start(bf16[256,2048]{1,0:T(8,128)(2,1)S(1)} %slice.234), channel_id=1, source_target_pairs={{0,8},{4,12},{8,0},{12,4},{1,9},{5,13},{9,1},{13,5},{2,10},{6,14},... | collective-permute-start | bytes 3145736 | tf_op jit(solution)/shard_map/ppermute | solution.py:41
  111.3 46.2 %collective-permute-start.3 = (bf16[256,2048]{1,0:T(8,128)(2,1)}, bf16[256,2048]{1,0:T(8,128)(2,1)}, u32[]{:S(2)}, u32[]{:S(2)}) collective-permute-start(bf16[256,2048]{1,0:T(8,128)(2,1)} %slice.235), channel_id=1, source_target_pairs={{0,4},{4,0},{8,12},{12,8},{1,5},{5,1},{9,13},{13,9},{2,6},{6,2},{1... | collective-permute-start | bytes 3145736 | tf_op jit(solution)/shard_map/ppermute | solution.py:41
  112.0 48.9 %collective-permute-start.11 = (bf16[512,2048]{1,0:T(8,128)(2,1)}, bf16[512,2048]{1,0:T(8,128)(2,1)}, u32[]{:S(2)}, u32[]{:S(2)}) collective-permute-start(bf16[512,2048]{1,0:T(8,128)(2,1)} %collective-permute-done.x0.x1), channel_id=1, source_target_pairs={{0,16},{16,0},{1,17},{17,1},{2,18},{18,2},{3,19},{19,3},{4,20},{20... | collective-permute-start | bytes 6291464 | tf_op jit(solution)/shard_map/ppermute | solution.py:41
  112.0 49.0 %collective-permute-start.10 = (bf16[512,2048]{1,0:T(8,128)(2,1)}, bf16[512,2048]{1,0:T(8,128)(2,1)S(1)}, u32[]{:S(2)}, u32[]{:S(2)}) collective-permute-start(bf16[512,2048]{1,0:T(8,128)(2,1)} %collective-permute-done.2.x0.x1), channel_id=1, source_target_pairs={{0,16},{16,0},{1,17},{17,1},{2,18},{18,2},{3,19},{19,3},{4,20},{20... | collective-permute-start | bytes 6291464 | tf_op jit(solution)/shard_map/ppermute | solution.py:41
  157.6 62.5 %collective-permute-start.35 = (bf16[512,2048]{1,0:T(8,128)(2,1)}, bf16[512,2048]{1,0:T(8,128)(2,1)}, u32[]{:S(2)}, u32[]{:S(2)}) collective-permute-start(bf16[512,2048]{1,0:T(8,128)(2,1)} %get-tuple-element.105), channel_id=1, source_target_pairs={{0,4},{4,0},{8,12},{12,8},{1,5},{5,1},{9,13},{13,9},{2,6},{6,2},{1... | collective-permute-start | bytes 6291464 | tf_op jit(solution)/shard_map/ppermute | solution.py:41
  158.1 64.8 %collective-permute-start.37 = (bf16[512,2048]{1,0:T(8,128)(2,1)}, bf16[512,2048]{1,0:T(8,128)(2,1)}, u32[]{:S(2)}, u32[]{:S(2)}) collective-permute-start(bf16[512,2048]{1,0:T(8,128)(2,1)} %get-tuple-element.105), channel_id=1, source_target_pairs={{0,8},{4,12},{8,0},{12,4},{1,9},{5,13},{9,1},{13,5},{2,10},{6,14},... | collective-permute-start | bytes 6291464 | tf_op jit(solution)/shard_map/ppermute | solution.py:41
  179.3 46.7 %collective-permute-start.18 = (bf16[2,256,1024]{2,1,0:T(8,128)(2,1)}, bf16[2,256,1024]{2,1,0:T(8,128)(2,1)}, u32[]{:S(2)}, u32[]{:S(2)}) collective-permute-start(bf16[2,256,1024]{2,1,0:T(8,128)(2,1)} %collective-permute-done.17), channel_id=1, source_target_pairs={{0,1},{1,2},{2,3},{3,0},{4,5},{5,6},{6,7},{7,4},{8,9},{9,10},{10,1... | collective-permute-start | bytes 3145736 | tf_op jit(solution)/shard_map/ppermute | solution.py:46
  222.5 49.4 %collective-permute-start.39 = (bf16[256,2048]{1,0:T(8,128)(2,1)}, bf16[256,2048]{1,0:T(8,128)(2,1)}, u32[]{:S(2)}, u32[]{:S(2)}) collective-permute-start(bf16[256,2048]{1,0:T(8,128)(2,1)} %slice.256), channel_id=1, source_target_pairs={{0,8},{4,12},{8,0},{12,4},{1,9},{5,13},{9,1},{13,5},{2,10},{6,14},... | collective-permute-start | bytes 3145736 | tf_op jit(solution)/shard_map/ppermute | solution.py:41
  225.3 46.7 %collective-permute-start.40 = (bf16[256,2048]{1,0:T(8,128)(2,1)}, bf16[256,2048]{1,0:T(8,128)(2,1)}, u32[]{:S(2)}, u32[]{:S(2)}) collective-permute-start(bf16[256,2048]{1,0:T(8,128)(2,1)} %slice.257), channel_id=1, source_target_pairs={{0,4},{4,0},{8,12},{12,8},{1,5},{5,1},{9,13},{13,9},{2,6},{6,2},{1... | collective-permute-start | bytes 3145736 | tf_op jit(solution)/shard_map/ppermute | solution.py:41
  225.9 46.5 %collective-permute-start.19 = (bf16[2,256,1024]{2,1,0:T(8,128)(2,1)}, bf16[2,256,1024]{2,1,0:T(8,128)(2,1)}, u32[]{:S(2)}, u32[]{:S(2)}) collective-permute-start(bf16[2,256,1024]{2,1,0:T(8,128)(2,1)} %collective-permute-done.18), channel_id=1, source_target_pairs={{0,1},{1,2},{2,3},{3,0},{4,5},{5,6},{6,7},{7,4},{8,9},{9,10},{10,1... | collective-permute-start | bytes 3145736 | tf_op jit(solution)/shard_map/ppermute | solution.py:46
  266.6 51.2 %collective-permute-start.36 = (bf16[512,2048]{1,0:T(8,128)(2,1)}, bf16[512,2048]{1,0:T(8,128)(2,1)}, u32[]{:S(2)}, u32[]{:S(2)}) collective-permute-start(bf16[512,2048]{1,0:T(8,128)(2,1)} %collective-permute-done.35), channel_id=1, source_target_pairs={{0,16},{16,0},{1,17},{17,1},{2,18},{18,2},{3,19},{19,3},{4,20},{20... | collective-permute-start | bytes 6291464 | tf_op jit(solution)/shard_map/ppermute | solution.py:41
  266.7 57.5 %collective-permute-start.38 = (bf16[512,2048]{1,0:T(8,128)(2,1)}, bf16[512,2048]{1,0:T(8,128)(2,1)S(1)}, u32[]{:S(2)}, u32[]{:S(2)}) collective-permute-start(bf16[512,2048]{1,0:T(8,128)(2,1)} %collective-permute-done.37), channel_id=1, source_target_pairs={{0,16},{16,0},{1,17},{17,1},{2,18},{18,2},{3,19},{19,3},{4,20},{20... | collective-permute-start | bytes 6291464 | tf_op jit(solution)/shard_map/ppermute | solution.py:41
  271.8 58.5 %collective-permute-start.41 = (bf16[256,2048]{1,0:T(8,128)(2,1)}, bf16[256,2048]{1,0:T(8,128)(2,1)}, u32[]{:S(2)}, u32[]{:S(2)}) collective-permute-start(bf16[256,2048]{1,0:T(8,128)(2,1)} %collective-permute-done.39), channel_id=1, source_target_pairs={{0,16},{16,0},{1,17},{17,1},{2,18},{18,2},{3,19},{19,3},{4,20},{20... | collective-permute-start | bytes 3145736 | tf_op jit(solution)/shard_map/ppermute | solution.py:41
  272.0 60.6 %collective-permute-start.42 = (bf16[256,2048]{1,0:T(8,128)(2,1)}, bf16[256,2048]{1,0:T(8,128)(2,1)}, u32[]{:S(2)}, u32[]{:S(2)}) collective-permute-start(bf16[256,2048]{1,0:T(8,128)(2,1)} %collective-permute-done.40), channel_id=1, source_target_pairs={{0,16},{16,0},{1,17},{17,1},{2,18},{18,2},{3,19},{19,3},{4,20},{20... | collective-permute-start | bytes 3145736 | tf_op jit(solution)/shard_map/ppermute | solution.py:41
  272.4 190.1 %collective-permute-start.21 = (bf16[2,1024,256]{2,1,0:T(8,128)(2,1)S(1)}, bf16[2,1024,256]{2,1,0:T(8,128)(2,1)}, u32[]{:S(2)}, u32[]{:S(2)}) collective-permute-start(bf16[2,1024,256]{2,1,0:T(8,128)(2,1)S(1)} %copy-done.15), channel_id=1, source_target_pairs={{0,1},{1,2},{2,3},{3,0},{4,5},{5,6},{6,7},{7,4},{8,9},{9,10},{10,1... | collective-permute-start | bytes 3145736 | tf_op jit(solution)/shard_map/ppermute | solution.py:46
  360.6 152.5 %collective-permute-start.72 = (bf16[2,1024,256]{2,1,0:T(8,128)(2,1)}, bf16[2,1024,256]{2,1,0:T(8,128)(2,1)}, u32[]{:S(2)}, u32[]{:S(2)}) collective-permute-start(bf16[2,1024,256]{2,1,0:T(8,128)(2,1)} %pad_maximum_fusion.8), channel_id=1, source_target_pairs={{0,1},{1,2},{2,3},{3,0},{4,5},{5,6},{6,7},{7,4},{8,9},{9,10},{10,1... | collective-permute-start | bytes 3145736 | tf_op jit(solution)/shard_map/ppermute | solution.py:46
  378.6 76.4 %collective-permute-start.64 = (bf16[2,256,256]{2,1,0:T(8,128)(2,1)}, bf16[2,256,256]{2,1,0:T(8,128)(2,1)}, u32[]{:S(2)}, u32[]{:S(2)}) collective-permute-start(bf16[2,256,256]{2,1,0:T(8,128)(2,1)} %pad_maximum_fusion.12), channel_id=1, source_target_pairs={{0,1},{1,2},{2,3},{3,0},{4,5},{5,6},{6,7},{7,4},{8,9},{9,10},{10,1... | collective-permute-start | bytes 786440 | tf_op jit(solution)/shard_map/ppermute | solution.py:46
  462.5 68.4 %collective-permute-start.22 = (bf16[2,1024,256]{2,1,0:T(8,128)(2,1)}, bf16[2,1024,256]{2,1,0:T(8,128)(2,1)S(1)}, u32[]{:S(2)}, u32[]{:S(2)}) collective-permute-start(bf16[2,1024,256]{2,1,0:T(8,128)(2,1)} %collective-permute-done.21), channel_id=1, source_target_pairs={{0,1},{1,2},{2,3},{3,0},{4,5},{5,6},{6,7},{7,4},{8,9},{9,10},{10,1... | collective-permute-start | bytes 3145736 | tf_op jit(solution)/shard_map/ppermute | solution.py:46
  530.9 60.7 %collective-permute-start.23 = (bf16[2,1024,256]{2,1,0:T(8,128)(2,1)S(1)}, bf16[2,1024,256]{2,1,0:T(8,128)(2,1)S(1)}, u32[]{:S(2)}, u32[]{:S(2)}) collective-permute-start(bf16[2,1024,256]{2,1,0:T(8,128)(2,1)S(1)} %collective-permute-done.22), channel_id=1, source_target_pairs={{0,1},{1,2},{2,3},{3,0},{4,5},{5,6},{6,7},{7,4},{8,9},{9,10},{10,1... | collective-permute-start | bytes 3145736 | tf_op jit(solution)/shard_map/ppermute | solution.py:46
  553.5 236.2 %collective-permute-start.74 = (bf16[2,1024,256]{2,1,0:T(8,128)(2,1)}, bf16[2,1024,256]{2,1,0:T(8,128)(2,1)}, u32[]{:S(2)}, u32[]{:S(2)}) collective-permute-start(bf16[2,1024,256]{2,1,0:T(8,128)(2,1)} %add_convert_fusion.8), channel_id=1, source_target_pairs={{0,1},{1,2},{2,3},{3,0},{4,5},{5,6},{6,7},{7,4},{8,9},{9,10},{10,1... | collective-permute-start | bytes 3145736 | tf_op jit(solution)/shard_map/ppermute | solution.py:46
  819.3 77.3 %collective-permute-start.43 = (bf16[512,2048]{1,0:T(8,128)(2,1)}, bf16[512,2048]{1,0:T(8,128)(2,1)S(1)}, u32[]{:S(2)}, u32[]{:S(2)}) collective-permute-start(bf16[512,2048]{1,0:T(8,128)(2,1)} %get-tuple-element.112), channel_id=1, source_target_pairs={{0,16},{16,0},{1,17},{17,1},{2,18},{18,2},{3,19},{19,3},{4,20},{20... | collective-permute-start | bytes 6291464 | tf_op jit(solution)/shard_map/ppermute | solution.py:41
  828.4 69.5 %collective-permute-start.31 = (bf16[256,2048]{1,0:T(8,128)(2,1)S(1)}, bf16[256,2048]{1,0:T(8,128)(2,1)S(1)}, u32[]{:S(2)}, u32[]{:S(2)}) collective-permute-start(bf16[256,2048]{1,0:T(8,128)(2,1)S(1)} %slice.253), channel_id=1, source_target_pairs={{0,4},{4,0},{8,12},{12,8},{1,5},{5,1},{9,13},{13,9},{2,6},{6,2},{1... | collective-permute-start | bytes 3145736 | tf_op jit(solution)/shard_map/ppermute | solution.py:41
  830.3 68.9 %collective-permute-start.30 = (bf16[256,2048]{1,0:T(8,128)(2,1)S(1)}, bf16[256,2048]{1,0:T(8,128)(2,1)S(1)}, u32[]{:S(2)}, u32[]{:S(2)}) collective-permute-start(bf16[256,2048]{1,0:T(8,128)(2,1)S(1)} %slice.251), channel_id=1, source_target_pairs={{0,8},{4,12},{8,0},{12,4},{1,9},{5,13},{9,1},{13,5},{2,10},{6,14},... | collective-permute-start | bytes 3145736 | tf_op jit(solution)/shard_map/ppermute | solution.py:41
  896.6 47.2 %collective-permute-start.50 = (bf16[256,2048]{1,0:T(8,128)(2,1)S(1)}, bf16[256,2048]{1,0:T(8,128)(2,1)S(1)}, u32[]{:S(2)}, u32[]{:S(2)}) collective-permute-start(bf16[256,2048]{1,0:T(8,128)(2,1)S(1)} %slice.263), channel_id=1, source_target_pairs={{0,4},{4,0},{8,12},{12,8},{1,5},{5,1},{9,13},{13,9},{2,6},{6,2},{1... | collective-permute-start | bytes 3145736 | tf_op jit(solution)/shard_map/ppermute | solution.py:41
  897.8 46.1 %collective-permute-start.49 = (bf16[256,2048]{1,0:T(8,128)(2,1)}, bf16[256,2048]{1,0:T(8,128)(2,1)S(1)}, u32[]{:S(2)}, u32[]{:S(2)}) collective-permute-start(bf16[256,2048]{1,0:T(8,128)(2,1)} %slice.261), channel_id=1, source_target_pairs={{0,8},{4,12},{8,0},{12,4},{1,9},{5,13},{9,1},{13,5},{2,10},{6,14},... | collective-permute-start | bytes 3145736 | tf_op jit(solution)/shard_map/ppermute | solution.py:41
  899.2 63.4 %collective-permute-start.52 = (bf16[256,2048]{1,0:T(8,128)(2,1)S(1)}, bf16[256,2048]{1,0:T(8,128)(2,1)S(1)}, u32[]{:S(2)}, u32[]{:S(2)}) collective-permute-start(bf16[256,2048]{1,0:T(8,128)(2,1)S(1)} %add_convert_fusion.10), channel_id=1, source_target_pairs={{0,8},{4,12},{8,0},{12,4},{1,9},{5,13},{9,1},{13,5},{2,10},{6,14},... | collective-permute-start | bytes 3145736 | tf_op jit(solution)/shard_map/ppermute | solution.py:41
  921.4 51.1 %collective-permute-start.62 = (f32[256,768]{1,0:T(8,128)S(1)}, f32[256,768]{1,0:T(8,128)}, u32[]{:S(2)}, u32[]{:S(2)}) collective-permute-start(f32[256,768]{1,0:T(8,128)S(1)} %dynamic-slice_bitcast_fusion.10), channel_id=1, source_target_pairs={{0,16},{16,0},{1,17},{17,1},{2,18},{18,2},{3,19},{19,3},{4,20},{20... | collective-permute-start | bytes 2359304 | tf_op jit(solution)/shard_map/ppermute | solution.py:41
  (104 other events, 2007.8 us)

commit v2 on v0

v2 whole, which is shorter than its diff:
```python
from functools import partial
import math

import jax
import jax.numpy as jnp
from jax import lax
from jax.experimental import pallas as pl
from jax.experimental.pallas import tpu as pltpu
from jax.sharding import PartitionSpec as P

HD = 128
ROT = 32


EPSILON = 1e-05
NEGATIVE = -1e30
ROPE_BASE = 10000.0
LOG2E = math.log2(math.e)
F32 = jnp.float32
BF16 = jnp.bfloat16
CONTRACT_LAST = (((1,), (1,)), ((), ()))
CONTRACT_FIRST = (((0,), (0,)), ((), ()))
VMEM_BYTES = 56 * 1024 * 1024
ANY = pl.BlockSpec(memory_space=pl.ANY)
HINT = 0.02


def cost(flops, moved, transcendentals=0):
    return pl.CostEstimate(
        flops=1 + int(flops * HINT), bytes_accessed=1 + int(moved * HINT), transcendentals=0
    )


def launch(
    kernel,
    operands,
    in_specs,
    grid,
    out_specs,
    out_shape,
    name,
    cost_estimate,
    prefetch=(),
    held=(),
    tokens=(),
    scratch_shapes=(),
):
    lead = len(prefetch) + len(operands)
    extra = len(held) + len(tokens)

    def body(*refs):
        kernel(*refs[:lead], *refs[lead + extra :])

    return pl.pallas_call(
        body,
        grid_spec=pltpu.PrefetchScalarGridSpec(
            num_scalar_prefetch=len(prefetch),
            grid=grid,
            in_specs=list(in_specs) + [ANY] * extra,
            out_specs=out_specs,
            scratch_shapes=list(scratch_shapes),
        ),
        out_shape=out_shape,
        input_output_aliases={lead + k: k for k in range(len(held))},
        compiler_params=pltpu.CompilerParams(
            dimension_semantics=("arbitrary",) * len(grid), vmem_limit_bytes=VMEM_BYTES
        ),
        cost_estimate=cost_estimate,
        name=name,
    )(*prefetch, *operands, *held, *tokens)


def hold(value, *tokens):
    def nothing(out):
        pass

    return launch(
        nothing,
        [],
        [],
        (1,),
        ANY,
        jax.ShapeDtypeStruct(value.shape, value.dtype),
        "hold",
        cost(1, 1),
        held=[value],
        tokens=tokens,
    )


def swap(value, axis, bit):
    size = lax.axis_size(axis)
    return lax.ppermute(value, axis, [(i, i ^ bit) for i in range(size)])


def onward(value, axis):
    size = lax.axis_size(axis)
    return lax.ppermute(value, axis, [(i, (i + 1) % size) for i in range(size)])


def bit_orders(size):
    bits = [1 << k for k in range(size.bit_length() - 1)]
    return (bits, bits[::-1])


def last_bit(number, order):
    return [bit for bit in order if number & bit][-1]


def gather_near(own, number):
    size = lax.axis_size("tp")
    bits = [1 << k for k in range(size.bit_length() - 1)]
    return {
        (bit, (n + number) % 2): swap(own[(n + number) % 2], "tp", bit)
        for n, bit in enumerate(bits)
    }


def hold_all(items, *tokens):
    return {key: hold(item, *tokens) for key, item in items.items()}


def in_pieces(first, second):
    items = {**first, **second}
    return {j: [items[j, 0], items[j, 1]] for j in sorted({j for j, _ in items})}


def gather_far(near):
    size = lax.axis_size("tp")
    pieces = dict(near)
    far = {}
    for j in sorted(range(1, size), key=lambda j: bin(j).count("1")):
        if j not in near:
            bits = [last_bit(j, order) for order in bit_orders(size)]
            far[j] = [swap(pieces[j ^ bit][q], "tp", bit) for q, bit in enumerate(bits)]
            pieces[j] = far[j]
    return far


def with_other_core(items):
    return items + [swap(item, "branch", 1) for item in items]


def add_up(items):
    total = items[0].astype(F32)
    for item in items[1:]:
        total = total + item.astype(F32)
    return total


class TileSum:
    def __init__(self):
        self.orders = bit_orders(lax.axis_size("tp"))
        size = lax.axis_size("tp")
        self.waiting = [(q, j) for j in range(1, size) for q in range(2)]
        self.expected = {(q, j): 0 for j in range(size) for q in range(2)}
        for q, j in self.waiting:
            self.expected[q, j ^ last_bit(j, self.orders[q])] += 1
        self.waiting.sort(key=lambda at: (-bin(at[1]).count("1"), not self.expected[at]))
        self.pieces = {}
        self.arrived = {}
        self.moving = []

    def part(self, q, j):
        half = self.pieces[j].shape[0] // 2
        return self.pieces[j][q * half : (q + 1) * half]

    def send(self, most=None):
        ready = [
            (q, j)
            for q, j in self.waiting
            if j in self.pieces and len(self.arrived.get((q, j), [])) == self.expected[q, j]
        ][:most]
        operands = []
        for q, j in ready:
            if (q, j) not in self.waiting:
                continue
            bit = last_bit(j, self.orders[q])
            both = (1 - q, j) in ready and last_bit(j, self.orders[1 - q]) == bit
            if both:
                operand = self.pieces[j]
                half = operand.shape[0] // 2
                for side in range(2):
                    if self.arrived.get((side, j)):
                        total = add_up([self.part(side, j)] + self.taken(side, j)).astype(BF16)
                        operand = lax.dynamic_update_slice_in_dim(operand, total, side * half, 0)
            else:
                operand = add_up([self.part(q, j)] + self.taken(q, j)).astype(BF16)
            sides = [0, 1] if both else [q]
            for side in sides:
                self.waiting.remove((side, j))
            self.moving.append((sides, j ^ bit, swap(operand, "tp", bit)))
            operands.append(operand)
        return operands

    def taken(self, q, j):
        half = self.pieces[j].shape[0] // 2
        return [
            item[at * half : (at + 1) * half] for item, at in self.arrived.get((q, j), [])
        ]

    def land(self, *tokens):
        items = []
        for sides, j, item in self.moving:
            item = hold(item, *tokens) if tokens else item
            items.append(item)
            for at, side in enumerate(sides):
                self.arrived.setdefault((side, j), []).append((item, at))
        self.moving = []
        return items

    def terms(self):
        return [[(self.pieces[0], 0), (self.pieces[0], 1)]] + [
            list(pair) for pair in zip(self.arrived[0, 0], self.arrived[1, 0])
        ]


def all_sum(value, axis):
    size = lax.axis_size(axis)
    bit = 1
    while bit < size:
        value = value + swap(value, axis, bit)
        bit *= 2
    return value


def rope(vectors, cosine, sine_up, sine_down):
    return (
        vectors * cosine
        + pltpu.roll(vectors, ROT // 2, 1) * sine_up
        + pltpu.roll(vectors, HD - ROT // 2, 1) * sine_down
    )


class Documents:
    def __init__(self, place, starts, seq_at, rows):
        self.row = place[1] ^ seq_at
        self.starts = starts
        self.rows = rows

    def begin(self, places):
        begin = jnp.zeros_like(places)
        for number in range(self.starts.shape[1]):
            start = self.starts[self.row, number]
            begin = jnp.where(places >= start, start, begin)
        return begin

    def first_key_block(self, block):
        return lax.div(self.begin(block * self.rows), jnp.int32(self.rows))

    def last_query_block(self, block, blocks):
        last = block
        for number in range(1, blocks):
            after = jnp.minimum(block + number, blocks - 1)
            last = jnp.where(self.first_key_block(after) <= block, jnp.maximum(last, after), last)
        return last


def table_kernel(place, starts, cosine, sine_up, sine_down):
    rows = cosine.shape[0]
    blocks = lax.axis_size("tp")
    step = pl.program_id(0)
    block, seq_at = lax.rem(step, blocks) ^ place[0], lax.div(step, blocks)
    places = block * rows + lax.broadcasted_iota(jnp.int32, (rows, 1), 0)
    begin = Documents(place, starts, seq_at, rows).begin(places)
    lane = lax.broadcasted_iota(jnp.int32, (1, HD), 1)
    half = ROT // 2
    number = jnp.where(lane < half, lane, lane - half).astype(F32)
    frequency = jnp.exp2(number * (-2.0 / ROT * math.log2(ROPE_BASE)))
    angles = (places - begin).astype(F32) * jnp.where(lane < ROT, frequency, 0.0)
    cosine[...] = jnp.cos(angles)
    sines = jnp.sin(angles)
    sine_up[...] = jnp.where((lane >= half) & (lane < ROT), sines, 0.0)
    sine_down[...] = jnp.where(lane < half, -sines, 0.0)


def rotary_tables(place, starts, rows, tokens):
    steps = 2 * lax.axis_size("tp")
    tile = rows // steps
    out = pl.BlockSpec((tile, HD), lambda i, *_: (i, 0))
    return launch(
        table_kernel,
        [],
        [],
        (steps,),
        [out] * 3,
        [jax.ShapeDtypeStruct((rows, HD), F32)] * 3,
        "rotary_tables",
        cost(rows * HD * 100, rows * HD * 48),
        prefetch=[place, starts],
        tokens=tokens,
    )


def place_kernel(x0, x1, x2, x3, out):
    step = pl.program_id(0)
    for number, x_ref in enumerate((x0, x1, x2, x3)):

        @pl.when(step == number)
        def _(x_ref=x_ref):
            out[...] = x_ref[...]


def half_of_piece(j):
    size = lax.axis_size("tp")
    return lambda i: ((lax.div(i, 2) * size + j) * 2 + lax.rem(i, 2), 0)


def place_piece(j, halves, rows_in_all, held, tokens=()):
    half, model_width = halves[0].shape
    return launch(
        place_kernel,
        halves,
        [whole_spec(halves[0])] * 4,
        (4,),
        pl.BlockSpec((half, model_width), half_of_piece(j)),
        jax.ShapeDtypeStruct((rows_in_all, model_width), BF16),
        "place_piece",
        cost(1, 4 * half * model_width * 4),
        held=held,
        tokens=tokens,
    )


def norm_kernel(x0, x1, x2, x3, gain1, shift1, gain2, shift2, *rest):
    normal, first, second, mark, scratch = rest[-5:]
    step = pl.program_id(0)
    mark[...] = jnp.zeros_like(mark)
    for number, x_ref in enumerate((x0, x1, x2, x3)):

        @pl.when(step == number)
        def _(x_ref=x_ref):
            scratch[...] = x_ref[...].astype(F32)

    x = scratch[...]
    centred = x - jnp.mean(x, axis=-1, keepdims=True)
    variance = jnp.mean(centred * centred, axis=-1, keepdims=True)
    n = centred * lax.rsqrt(variance + EPSILON)
    normal[...] = n.astype(BF16)
    first[...] = (n * gain1[...] + shift1[...]).astype(BF16)
    second[...] = (n * gain2[...] + shift2[...]).astype(BF16)


def norm_piece(j, halves, rows_in_all, gains, held, tokens):
    half, model_width = halves[0].shape
    wide = pl.BlockSpec((half, model_width), half_of_piece(j))
    return launch(
        norm_kernel,
        halves + list(gains),
        [whole_spec(item) for item in halves + list(gains)],
        (4,),
        [wide] * 3 + [pl.BlockSpec((8, HD), lambda i: (0, 0))],
        [jax.ShapeDtypeStruct((rows_in_all, model_width), BF16)] * 3
        + [jax.ShapeDtypeStruct((8, HD), F32)],
        "norm_piece",
        cost(4 * half * model_width * 16, 4 * half * model_width * 16),
        held=held,
        tokens=tokens,
        scratch_shapes=[pltpu.VMEM((half, model_width), F32)],
    )


def chunks_of(weight):
    groups, cores = weight.shape[:2]
    return [(z, c, c * groups + z) for c in range(cores) for z in range(groups)]


def row_product(left, weight, share):
    total = None
    for z, c, at in chunks_of(weight):
        part = jnp.dot(
            left[:, at * share : (at + 1) * share], weight[z, c], preferred_element_type=F32
        )
        total = part if total is None else total + part
    return total


def column_back(left, weight, share):
    total = None
    for z, c, at in chunks_of(weight):
        part = lax.dot_general(
            left[:, at * share : (at + 1) * share],
            weight[z, c],
            CONTRACT_LAST,
            preferred_element_type=F32,
        )
        total = part if total is None else total + part
    return total


def whole_spec(array, prefetched=0):
    rank = array.ndim
    return pl.BlockSpec(array.shape, lambda *at: (0,) * rank)


def project_kernel(normed, weight, bias, cosine, sine_up, sine_down, queries, keys, values):
    joined = row_product(normed, weight, weight.shape[2]) + bias[...]
    tables = (cosine[...], sine_up[...], sine_down[...])
    for head in range(queries.shape[0]):
        at = head * 3 * HD
        queries[head, 0, 0] = rope(joined[:, at : at + HD], *tables).astype(BF16)
        keys[head, 0, 0] = rope(joined[:, at + HD : at + 2 * HD], *tables).astype(BF16)
        values[head, 0, 0] = joined[:, at + 2 * HD : at + 3 * HD].astype(BF16)


def project(first, last, normed, weight, bias, tables, held):
    rows, model_width = normed.shape
    joined_cols = weight.shape[3]
    heads = joined_cols // (3 * HD)
    size = lax.axis_size("tp")
    tile = rows // (2 * size)
    table = pl.BlockSpec((tile, HD), lambda s, i: (s * size + first + i, 0))
    share = (last - first) / size
    return launch(
        project_kernel,
        [normed, weight, bias] + list(tables),
        [
            pl.BlockSpec((tile, model_width), lambda s, i: (s * size + first + i, 0)),
            whole_spec(weight),
            whole_spec(bias),
            table,
            table,
            table,
        ],
        (2, last - first),
        [pl.BlockSpec((heads, 1, 1, tile, HD), lambda s, i: (0, s, first + i, 0, 0))] * 3,
        [jax.ShapeDtypeStruct((heads, 2, size, tile, HD), BF16)] * 3,
        "project",
        cost(
            2 * rows * share * model_width * joined_cols,
            2 * (rows * share * (model_width + joined_cols) + weight.size),
        ),
        held=held,
    )


def attend_kernel(place, starts, q_ref, k_ref, v_ref, out_ref, send_ref, lse_ref):
    block = pl.program_id(1)
    heads, rows = q_ref.shape[0], q_ref.shape[-2]
    here = place[0]
    documents = Documents(place, starts, pl.program_id(0), rows)
    low = documents.first_key_block(block)
    query_places = block * rows + lax.broadcasted_iota(jnp.int32, (rows, 1), 0)
    begin = documents.begin(query_places)
    factor = LOG2E / math.sqrt(HD)

    def step(number, carry):
        key_places = number * rows + lax.broadcasted_iota(jnp.int32, (1, rows), 1)
        allowed = (key_places >= begin) & (key_places <= query_places)
        results = []
        for head in range(heads):
            top, total, mixed = carry[head]
            key = k_ref[head, 0, number ^ here]
            value = v_ref[head, 0, number ^ here]
            scores = lax.dot_general(
                q_ref[head, 0, 0], key, CONTRACT_LAST, preferred_element_type=F32
            )
            scores = jnp.where(allowed, scores * factor, NEGATIVE)
            new_top = jnp.maximum(top, jnp.max(scores, axis=-1, keepdims=True))
            weights = jnp.exp2(scores - new_top)
            shrink = jnp.exp2(top - new_top)
            total = total * shrink + jnp.sum(weights, axis=-1, keepdims=True)
            mixed = mixed * shrink + jnp.dot(
                weights.astype(BF16), value, preferred_element_type=F32
            )
            results.append((new_top, total, mixed))
        return tuple(results)

    empty = (
        jnp.full((rows, 1), NEGATIVE, F32),
        jnp.zeros((rows, 1), F32),
        jnp.zeros((rows, HD), F32),
    )
    results = lax.fori_loop(low, block + 1, step, (empty,) * heads)
    for head, (top, total, mixed) in enumerate(results):
        result = (mixed / total).astype(BF16)
        out_ref[0, 0, :, head * HD : (head + 1) * HD] = result
        send_ref[0, :, head * HD : (head + 1) * HD] = result
        log_sum = top + jnp.log(total) * LOG2E
        lse_ref[head, 0, 0] = jnp.broadcast_to(log_sum, (rows, HD)).T[:1]


def attend(place, starts, queries, keys, values, tokens):
    heads, seqs, blocks, rows, _ = queries.shape
    one = pl.BlockSpec(
        (heads, 1, 1, rows, HD), lambda s, i, place, starts: (0, s, i ^ place[0], 0, 0)
    )
    full = pl.BlockSpec((heads, 1, blocks, rows, HD), lambda s, i, *_: (0, s, 0, 0, 0))
    pairs = heads * seqs * blocks * (blocks + 1) // 2
    return launch(
        attend_kernel,
        [queries, keys, values],
        [one, full, full],
        (seqs, blocks),
        [
            pl.BlockSpec(
                (1, 1, rows, heads * HD), lambda s, i, place, starts: (s, i ^ place[0], 0, 0)
            ),
            pl.BlockSpec(
                (1, rows, heads * HD), lambda s, i, place, starts: ((s * i) ^ place[0], 0, 0)
            ),
            pl.BlockSpec(
                (heads, 1, 1, 1, rows), lambda s, i, place, starts: (0, s, i ^ place[0], 0, 0)
            ),
        ],
        [
            jax.ShapeDtypeStruct((seqs, blocks, rows, heads * HD), BF16),
            jax.ShapeDtypeStruct((blocks, rows, heads * HD), BF16),
            jax.ShapeDtypeStruct((heads, seqs, blocks, 1, rows), F32),
        ],
        "attend",
        cost(pairs * 30 * rows * rows * HD, 4 * queries.size * 2),
        prefetch=[place, starts],
        tokens=tokens,
    )


def attend_back_kernel(
    place,
    starts,
    q_ref,
    k_ref,
    v_ref,
    grad_ref,
    out_ref,
    lse_ref,
    cosine,
    sine_up,
    sine_down,
    joined_ref,
    send_ref,
    sum_ref,
    query_grad,
    delta,
):
    block = pl.program_id(1)
    heads, blocks, rows = q_ref.shape[0], q_ref.shape[2], q_ref.shape[-2]
    here = place[0]
    documents = Documents(place, starts, pl.program_id(0), rows)
    high = documents.last_query_block(block, blocks)
    scaling = 1.0 / math.sqrt(HD)

    @pl.when(block == 0)
    def _():
        query_grad[...] = jnp.zeros_like(query_grad)

        def inner(j, carry):
            for head in range(heads):
                cols = slice(head * HD, (head + 1) * HD)
                product = grad_ref[0, j, :, cols].astype(F32) * out_ref[0, j, :, cols].astype(F32)
                delta[head, j] = jnp.sum(product.T, axis=0, keepdims=True)
            return carry

        lax.fori_loop(0, blocks, inner, 0)

    own = block ^ here
    key_places = block * rows + lax.broadcasted_iota(jnp.int32, (rows, 1), 0)

    def step(number, carry):
        at = number ^ here
        query_places = number * rows + lax.broadcasted_iota(jnp.int32, (1, rows), 1)
        allowed = (key_places >= documents.begin(query_places)) & (key_places <= query_places)
        results = []
        for head in range(heads):
            key_grad, value_grad = carry[head]
            key = k_ref[head, 0, own]
            value = v_ref[head, 0, own]
            query = q_ref[head, 0, at]
            grad = grad_ref[0, at, :, head * HD : (head + 1) * HD]
            scores = lax.dot_general(key, query, CONTRACT_LAST, preferred_element_type=F32)
            scores = scores * (scaling * LOG2E) - lse_ref[head, 0, at]
            weights = jnp.where(allowed, jnp.exp2(scores), 0.0)
            weight_grad = lax.dot_general(value, grad, CONTRACT_LAST, preferred_element_type=F32)
            score_grad = (weights * (weight_grad - delta[head, at]) * scaling).astype(BF16)
            value_grad = value_grad + jnp.dot(
                weights.astype(BF16), grad, preferred_element_type=F32
            )
            key_grad = key_grad + jnp.dot(score_grad, query, preferred_element_type=F32)
            query_grad[head, at] = query_grad[head, at] + lax.dot_general(
                score_grad, key, CONTRACT_FIRST, preferred_element_type=F32
            )
            results.append((key_grad, value_grad))
        return tuple(results)

    empty = jnp.zeros((rows, HD), F32)
    results = lax.fori_loop(block, high + 1, step, ((empty, empty),) * heads)
    tables = (cosine[0, own], -sine_up[0, own], -sine_down[0, own])
    for head, (key_grad, value_grad) in enumerate(results):
        at = head * 3 * HD
        joined_ref[0, own, :, at + HD : at + 2 * HD] = rope(key_grad, *tables).astype(BF16)
        joined_ref[0, own, :, at + 2 * HD : at + 3 * HD] = value_grad.astype(BF16)

    @pl.when(block == blocks - 1)
    def _():
        def inner(j, carry):
            tables = (cosine[0, j], -sine_up[0, j], -sine_down[0, j])
            for head in range(heads):
                at = head * 3 * HD
                joined_ref[0, j, :, at : at + HD] = rope(query_grad[head, j], *tables).astype(BF16)
            send_ref[j] = joined_ref[0, j]
            return carry + jnp.sum(joined_ref[0, j].astype(F32), axis=0, keepdims=True)

        sum_ref[0] = lax.fori_loop(0, blocks, inner, jnp.zeros((1, heads * 3 * HD), F32))


def attend_back(place, starts, queries, keys, values, grad, out, log_sums, tables, tokens):
    heads, seqs, blocks, rows, _ = queries.shape
    joined_cols = heads * 3 * HD
    head_spec = pl.BlockSpec((heads, 1, blocks, rows, HD), lambda s, i, *_: (0, s, 0, 0, 0))
    side = pl.BlockSpec((1, blocks, rows, heads * HD), lambda s, i, *_: (s, 0, 0, 0))
    table = pl.BlockSpec((1, blocks, rows, HD), lambda s, i, *_: (s, 0, 0, 0))
    pairs = heads * seqs * blocks * (blocks + 1) // 2
    return launch(
        attend_back_kernel,
        [queries, keys, values, grad, out, log_sums]
        + [item.reshape(seqs, blocks, rows, HD) for item in tables],
        [
            head_spec,
            head_spec,
            head_spec,
            side,
            side,
            pl.BlockSpec((heads, 1, blocks, 1, rows), lambda s, i, *_: (0, s, 0, 0, 0)),
            table,
            table,
            table,
        ],
        (seqs, blocks),
        [
            pl.BlockSpec((1, blocks, rows, joined_cols), lambda s, i, *_: (s, 0, 0, 0)),
            pl.BlockSpec((blocks, rows, joined_cols), lambda s, i, *_: (0, 0, 0)),
            pl.BlockSpec((1, 1, joined_cols), lambda s, i, *_: (s, 0, 0)),
        ],
        [
            jax.ShapeDtypeStruct((seqs, blocks, rows, joined_cols), BF16),
            jax.ShapeDtypeStruct((blocks, rows, joined_cols), BF16),
            jax.ShapeDtypeStruct((seqs, 1, joined_cols), F32),
        ],
        "attend_back",
        cost(pairs * 50 * rows * rows * HD, 12 * queries.size * 2),
        prefetch=[place, starts],
        tokens=tokens,
        scratch_shapes=[
            pltpu.VMEM((heads, blocks, rows, HD), F32),
            pltpu.VMEM((heads, blocks, 1, rows), F32),
        ],
    )


def expand_kernel(normed, weight, bias, activated, send, slope):
    pre = row_product(normed, weight, weight.shape[2]) + bias[...]
    share = 0.5 + 0.5 * lax.erf(pre * math.sqrt(0.5))
    density = jnp.exp2(pre * pre * (-0.5 * LOG2E)) * (1.0 / math.sqrt(2.0 * math.pi))
    result = (pre * share).astype(BF16)
    activated[...] = result
    send[...] = result
    slope[...] = (share + pre * density).astype(BF16)


def later_half(tile, width, steps):
    half = steps // 2
    return pl.BlockSpec((tile, width), lambda i: (jnp.maximum(i - half, 0), 0))


def expand(normed, weight, bias, tokens):
    rows, model_width = normed.shape
    cols = weight.shape[3]
    tile = 512
    steps = rows // tile
    out = pl.BlockSpec((tile, cols), lambda i: (i, 0))
    shape = jax.ShapeDtypeStruct((rows, cols), BF16)
    return launch(
        expand_kernel,
        [normed, weight, bias],
        [pl.BlockSpec((tile, model_width), lambda i: (i, 0)), whole_spec(weight), whole_spec(bias)],
        (steps,),
        [out, later_half(tile, cols, steps), out],
        [shape, jax.ShapeDtypeStruct((rows // 2, cols), BF16), shape],
        "expand",
        cost(
            2 * rows * model_width * cols,
            2 * (rows * model_width + weight.size + 2 * rows * cols),
        ),
        tokens=tokens,
    )


def output_kernel(att, att_other, act, act_other, dense, dense_other, contract, contract_other, out):
    share = dense.shape[3]
    for n in range(dense.shape[0]):
        total = jnp.dot(att[...], dense[n, 0], preferred_element_type=F32)
        for left, right in (
            (att_other, dense_other),
            (act, contract),
            (act_other, contract_other),
        ):
            total = total + jnp.dot(left[...], right[n, 0], preferred_element_type=F32)
        out[:, n * share : (n + 1) * share] = total.astype(BF16)


def by_columns(weight):
    groups = weight.shape[0] // 2
    return pl.BlockSpec(
        (2, 1) + weight.shape[2:], lambda i: (lax.rem(i, groups), lax.div(i, groups), 0, 0)
    )


def output_piece(j, pieces, attended, activated, dense, contract, tokens):
    tile = attended[1].shape[0] // pieces
    groups, cores, _, share = dense[0].shape
    steps, share = groups * cores // 2, 2 * share
    lefts = [*attended, *activated]
    rights = [*dense, *contract]
    return launch(
        output_kernel,
        lefts + rights,
        [pl.BlockSpec((tile, item.shape[1]), lambda i: (j, 0)) for item in lefts]
        + [by_columns(item) for item in rights],
        (steps,),
        pl.BlockSpec((tile, share), lambda i: (0, i)),
        jax.ShapeDtypeStruct((tile, steps * share), BF16),
        "output_piece",
        cost(4 * tile * sum(item.size for item in rights), 4 * sum(item.size for item in rights)),
        tokens=tokens,
    )


def dense_back_kernel(grad_ref, att_ref, dense, out, blocks, total):
    step = pl.program_id(0)
    share = dense.shape[3]

    @pl.when(step == 0)
    def _():
        total[...] = jnp.zeros_like(total)

    out[...] = column_back(grad_ref, dense, share).astype(BF16)
    total[...] += lax.dot_general(
        att_ref[...], grad_ref[...], CONTRACT_FIRST, preferred_element_type=F32
    )

    @pl.when(step == pl.num_programs(0) - 1)
    def _():
        for z, c, at in chunks_of(dense):
            blocks[z, c] = total[:, at * share : (at + 1) * share].T.astype(BF16)


def dense_back(grad, attended, dense, tokens):
    rows, width = grad.shape
    groups, cores, cols, share = dense.shape
    turned = jax.ShapeDtypeStruct((groups, cores, share, cols), BF16)
    tile = 512
    return launch(
        dense_back_kernel,
        [grad, attended, dense],
        [
            pl.BlockSpec((tile, width), lambda i: (i, 0)),
            pl.BlockSpec((tile, cols), lambda i: (i, 0)),
            whole_spec(dense),
        ],
        (rows // tile,),
        [pl.BlockSpec((tile, cols), lambda i: (i, 0)), whole_spec(turned)],
        [jax.ShapeDtypeStruct((rows, cols), BF16), turned],
        "dense_back",
        cost(4 * rows * dense.size, 2 * (rows * (width + cols) + dense.size)),
        tokens=tokens,
        scratch_shapes=[pltpu.VMEM((cols, width), F32)],
    )


def pre_grad_kernel(grad_ref, slope, contract, out, send, sums):
    @pl.when(pl.program_id(0) == 0)
    def _():
        sums[...] = jnp.zeros_like(sums)

    part = column_back(grad_ref, contract, contract.shape[3]) * slope[...].astype(F32)
    part = part.astype(BF16)
    out[...] = part
    send[...] = part
    sums[...] += jnp.sum(part.astype(F32), axis=0, keepdims=True)


def pre_grad_of(grad, slope, contract, tokens):
    rows, width = grad.shape
    cols = contract.shape[2]
    tile = 512
    steps = rows // tile
    return launch(
        pre_grad_kernel,
        [grad, slope, contract],
        [
            pl.BlockSpec((tile, width), lambda i: (i, 0)),
            pl.BlockSpec((tile, cols), lambda i: (i, 0)),
            whole_spec(contract),
        ],
        (steps,),
        [
            pl.BlockSpec((tile, cols), lambda i: (i, 0)),
            later_half(tile, cols, steps),
            pl.BlockSpec((1, cols), lambda i: (0, 0)),
        ],
        [
            jax.ShapeDtypeStruct((rows, cols), BF16),
            jax.ShapeDtypeStruct((rows // 2, cols), BF16),
            jax.ShapeDtypeStruct((1, cols), F32),
        ],
        "pre_grad",
        cost(2 * rows * contract.size, 2 * (rows * width + contract.size + 2 * rows * cols)),
        tokens=tokens,
    )


def normed_grad_kernel(
    joined,
    joined_other,
    pre,
    pre_other,
    joined_weight,
    joined_weight_other,
    expand_weight,
    expand_weight_other,
    normal,
    gain1,
    gain2,
    out,
    sums,
):
    share = joined_weight.shape[2]
    for number in range(joined_weight.shape[0]):

        def back(left, weight):
            return lax.dot_general(
                left[...], weight[number, 0], CONTRACT_LAST, preferred_element_type=F32
            )

        cols = slice(number * share, (number + 1) * share)
        first = back(joined, joined_weight) + back(joined_other, joined_weight_other)
        second = back(pre, expand_weight) + back(pre_other, expand_weight_other)
        n = normal[:, cols].astype(F32)
        sums[0:1, cols] = jnp.sum(first * n, axis=0, keepdims=True)
        sums[1:2, cols] = jnp.sum(first, axis=0, keepdims=True)
        sums[2:3, cols] = jnp.sum(second * n, axis=0, keepdims=True)
        sums[3:4, cols] = jnp.sum(second, axis=0, keepdims=True)
        out[:, cols] = (first * gain1[:, cols] + second * gain2[:, cols]).astype(BF16)


def normed_grad_piece(
    j, pieces, joined, pre, joined_weight, expand_weight, normal, gain1, gain2, tokens
):
    tile = joined[1].shape[0] // pieces
    groups, cores, share, _ = joined_weight[0].shape
    steps, share = groups * cores // 2, 2 * share
    lefts = [*joined, *pre]
    rights = [*joined_weight, *expand_weight]
    row = pl.BlockSpec((1, share), lambda i: (0, i))
    return launch(
        normed_grad_kernel,
        lefts + rights + [normal, gain1, gain2],
        [pl.BlockSpec((tile, item.shape[1]), lambda i: (j, 0)) for item in lefts]
        + [by_columns(item) for item in rights]
        + [pl.BlockSpec((tile, share), lambda i: (j, i)), row, row],
        (steps,),
        [
            pl.BlockSpec((tile, share), lambda i: (0, i)),
            pl.BlockSpec((8, share), lambda i: (0, i)),
        ],
        [
            jax.ShapeDtypeStruct((tile, steps * share), BF16),
            jax.ShapeDtypeStruct((8, steps * share), F32),
        ],
        "normed_grad_piece",
        cost(4 * tile * sum(item.size for item in rights), 4 * sum(item.size for item in rights)),
        tokens=tokens,
    )


def rows_at(half, width, here):
    if here:
        return pl.BlockSpec((1, half, width), lambda i, place: (place[1], i, 0))
    return pl.BlockSpec((1, half, width), lambda i, place: (1 - place[1], i, 0))


def finish_tile(body, name, place, operands, whole, tile, width, tokens=()):
    half = tile // 2
    listed, specs, picks = [], [], []
    for pair in operands:
        if pair[0][0] is pair[1][0] and (pair[0][1], pair[1][1]) == (0, 1):
            picks.append((len(listed), False))
            listed.append(pair[0][0])
            specs.append(pl.BlockSpec((half, width), lambda i, place: (i, 0)))
        else:
            picks.append((len(listed), True))
            for item, at in pair:
                listed.append(item)
                specs.append(pl.BlockSpec((half, width), lambda i, place, at=at: (at, 0)))
    count = len(listed)

    def kernel(place, *refs):
        both, own = refs[count + len(whole) :]
        first = pl.program_id(0) == 0
        values = [
            jnp.where(first, refs[at][...], refs[at + 1][...]) if pair else refs[at][...]
            for at, pair in picks
        ]
        result = body(values, refs[count : count + len(whole)]).astype(BF16)
        both[0] = result
        own[...] = result

    return launch(
        kernel,
        listed + list(whole),
        specs + [pl.BlockSpec(item.shape, lambda i, place: (0, 0)) for item in whole],
        (2,),
        [rows_at(half, width, True), pl.BlockSpec((half, width), lambda i, place: (i, 0))],
        [
            jax.ShapeDtypeStruct((2, tile, width), BF16),
            jax.ShapeDtypeStruct((tile, width), BF16),
        ],
        name,
        cost(20 * tile * width, 20 * tile * width),
        prefetch=[place],
        tokens=tokens,
    )


def both_halves(item):
    return [(item, 0), (item, 1)]


def fill_other(place, both, other):
    tile, width = other.shape

    def kernel(place, value, out):
        out[0] = value[...]

    return launch(
        kernel,
        [other],
        [pl.BlockSpec((tile // 2, width), lambda i, place: (i, 0))],
        (2,),
        rows_at(tile // 2, width, False),
        jax.ShapeDtypeStruct(both.shape, BF16),
        "fill_other",
        cost(1, 4 * tile * width),
        prefetch=[place],
        held=[both],
    )


def per_device(
    block_input,
    first_norm_gain,
    first_norm_bias,
    second_norm_gain,
    second_norm_bias,
    query_key_value,
    query_key_value_bias,
    attention_dense,
    attention_dense_bias,
    expand_weight,
    expand_bias,
    contract_weight,
    contract_bias,
    document_starts,
    output_grad,
):
    seqs, tile, model_width = block_input.shape
    tiles = lax.axis_size("tp")
    groups = lax.axis_size("seq")
    core = lax.axis_index("branch")
    here = lax.axis_index("tp")
    first_core = core == 0
    length = tile * tiles
    rows_in_all = length * seqs
    share = query_key_value.shape[0]

    def by_core(mine, others):
        return jnp.where(first_core, mine, others), jnp.where(first_core, others, mine)

    def halves_of(value, axis):
        size = value.shape[axis] // 2
        return (
            lax.dynamic_slice_in_dim(value, core * size, size, axis),
            lax.dynamic_slice_in_dim(value, (1 - core) * size, size, axis),
        )

    place = jnp.stack([here, core]).astype(jnp.int32)

    def core_halves(weight, axis):
        mine, others = halves_of(weight, axis)
        return jnp.stack(by_core(mine, swap(others, "branch", 1)))

    def gather_seq(piece):
        return lax.all_gather(piece, "seq", axis=0)

    weight_pieces = [
        core_halves(query_key_value, 1),
        core_halves(expand_weight, 1),
        core_halves(attention_dense, 0),
        core_halves(contract_weight, 0),
    ]
    joined_weight, expand_full, dense_full, contract_full = map(gather_seq, weight_pieces)
    joined_bias = halves_of(query_key_value_bias, 0)[0].astype(F32)[None]
    hidden_bias = halves_of(expand_bias, 0)[0].astype(F32)[None]

    def own_and_other(value):
        return (
            lax.dynamic_index_in_dim(value, core, 0, False),
            lax.dynamic_index_in_dim(value, 1 - core, 0, False),
        )

    def in_halves(value):
        return [value[: tile // 2], value[tile // 2 :]]

    input_own, input_other = own_and_other(block_input)
    grad_own, grad_other = own_and_other(output_grad)
    gain1 = first_norm_gain.astype(F32)[None]
    gain2 = second_norm_gain.astype(F32)[None]
    gains = (
        gain1,
        first_norm_bias.astype(F32)[None],
        gain2,
        second_norm_bias.astype(F32)[None],
    )
    input_halves = in_halves(input_own)
    near = {**gather_near(input_halves, 0), **gather_near(input_halves, 1)}
    grad_halves = in_halves(grad_own)
    grad_rows = place_piece(
        0, grad_halves + in_halves(grad_other), rows_in_all, (), weight_pieces
    )
    tables = rotary_tables(place, document_starts, rows_in_all, [*weight_pieces, grad_rows])
    *normed, mark = norm_piece(
        0, input_halves + in_halves(input_other), rows_in_all, gains, (), [tables[0]]
    )
    near = in_pieces(hold_all(near, mark), {})
    far = gather_far(near)
    for j in sorted(near):
        *normed, mark = norm_piece(j, with_other_core(near[j]), rows_in_all, gains, normed, [])
    heads_held = ()
    far_from = tiles
    if tiles == 4:
        heads_held = project(0, 3, normed[1], joined_weight, joined_bias, tables, ())
        far_from = 3
    for j in sorted(far):
        last_items = [hold(item, mark) for item in far[j]]
        *normed, mark = norm_piece(
            j, with_other_core(last_items), rows_in_all, gains, normed, heads_held[:1]
        )
    heads_held = project(
        far_from % tiles, tiles, normed[1], joined_weight, joined_bias, tables, heads_held
    )
    normal, first_normed, second_normed = normed
    queries, keys, values = heads_held

    first = gather_near([hold(item, *last_items) for item in grad_halves], 0)
    first = hold_all(first, queries)
    second = gather_near([hold(item, *first.values()) for item in grad_halves], 1)
    attended, attended_send, log_sums = attend(
        place, document_starts, queries, keys, values, [*first.values()]
    )
    attended_flat = attended.reshape(rows_in_all, -1)
    near = in_pieces(first, hold_all(second, log_sums))
    far = gather_far(near)
    activated, activated_send, slope = expand(
        second_normed, expand_full, hidden_bias, [item for j in near for item in near[j]]
    )
    near = {
        j: items + [hold(swap(item, "branch", 1), slope) for item in items]
        for j, items in near.items()
    }
    far = {j: [hold(item, slope) for item in items] for j, items in far.items()}
    arrived = [item for items in [*near.values(), *far.values()] for item in items]
    for j in sorted(near):
        grad_rows = place_piece(j, near[j], rows_in_all, [grad_rows], [slope])
    for j in sorted(far):
        items = with_other_core(far[j])
        grad_rows = place_piece(j, items, rows_in_all, [grad_rows], [slope])

    def weight_grad(left, right):
        return lax.dot_general(left, right, CONTRACT_FIRST, preferred_element_type=F32).astype(BF16)

    def in_order(part):
        return part.reshape(2, groups, share, part.shape[1]).transpose(1, 0, 2, 3)

    def scatter(blocks):
        return lax.psum_scatter(blocks, "seq", scatter_dimension=0, tiled=False)

    def finish(total, axis, *tokens):
        total = hold(total, *tokens)
        mine = jnp.where(first_core, total[0], total[1])
        others = swap(jnp.where(first_core, total[1], total[0]), "branch", 1)
        return jnp.concatenate(by_core(mine.astype(F32), others.astype(F32)), axis=axis)

    def exchanged(own, send, *tokens):
        send = send.reshape(-1, send.shape[-1])
        return own.reshape(-1, own.shape[-1]), swap(hold(send, *tokens) if tokens else send, "branch", 1)

    def with_other_weight(weight):
        return weight, swap(weight, "branch", 1)

    attended_pair = exchanged(attended, attended_send, *arrived)
    activated_pair = exchanged(activated, activated_send, *arrived)
    contract_blocks = in_order(weight_grad(grad_rows, activated))
    contract_total = scatter(contract_blocks)
    pre_grad, pre_send, pre_sums = pre_grad_of(
        grad_rows, slope, contract_full, [contract_blocks, attended_pair[1], activated_pair[1]]
    )
    pre_pair = exchanged(pre_grad, pre_send)
    contract_pair = with_other_weight(contract_full)
    expand_blocks = in_order(weight_grad(second_normed, pre_grad))
    expand_total = scatter(expand_blocks)
    attended_grad, dense_blocks = dense_back(
        grad_rows, attended_flat, dense_full, [expand_blocks, pre_pair[1], contract_pair[1]]
    )
    dense_pair = with_other_weight(dense_full)
    order = [tiles - 1] + list(range(1, tiles - 1)) + [0]
    outputs = TileSum()
    mark = attended_grad
    operands = []
    for j in order:
        mark = outputs.pieces[j] = output_piece(
            j,
            tiles,
            attended_pair,
            activated_pair,
            dense_pair,
            contract_pair,
            [mark, *operands],
        )
        operands = outputs.send() if j == order[0] else []
    landed = outputs.land(mark)
    operands = outputs.send()
    joined_grad, joined_send, joined_sums = attend_back(
        place,
        document_starts,
        queries,
        keys,
        values,
        attended_grad.reshape(attended.shape),
        attended,
        log_sums,
        tables,
        [*landed, *operands],
    )
    landed = outputs.land(joined_sums)
    joined_pair = exchanged(joined_grad, joined_send, *landed)
    joined_weight_pair = with_other_weight(joined_weight)
    expand_weight_pair = with_other_weight(expand_full)
    joined_grad = joined_pair[0]
    joined_blocks = jnp.concatenate(
        [in_order(weight_grad(hold(first_normed, *landed), joined_grad)), dense_blocks], axis=3
    )
    joined_total = scatter(joined_blocks)
    while outputs.waiting:
        outputs.send()
        outputs.land()

    inputs = TileSum()
    sums = jnp.zeros((8, model_width), F32)
    mark = joined_blocks
    landed = []
    for j in order:
        inputs.pieces[j], part = normed_grad_piece(
            j,
            tiles,
            joined_pair,
            pre_pair,
            joined_weight_pair,
            expand_weight_pair,
            normal,
            gain1,
            gain2,
            [mark] + landed,
        )
        sums = sums + part
        mark = part
        landed = inputs.land(mark) + inputs.send()
    tail = [mark]

    biases = (
        attention_dense_bias.astype(F32)[None],
        contract_bias.astype(F32)[None],
    )

    def output_body(values, whole):
        return add_up(values) + whole[0][...] + whole[1][...]

    output_both, output_own = finish_tile(
        output_body,
        "finish_output",
        place,
        [both_halves(input_own)] + outputs.terms(),
        biases,
        tile,
        model_width,
        tail,
    )
    block_output = fill_other(place, output_both, swap(output_own, "branch", 1))

    joined_bias_part = jnp.sum(joined_sums, axis=0).reshape(-1)
    hidden_bias_part = pre_sums[0]
    small = jnp.concatenate(
        [
            sums[:4].reshape(-1),
            jnp.sum(grad_own.astype(F32), axis=0),
            joined_bias_part,
            hidden_bias_part,
        ]
    )
    everywhere = 5 * model_width
    small = all_sum(hold(small, output_own), "seq")
    per_core = small[everywhere:]
    both = jnp.stack(by_core(per_core, swap(per_core, "branch", 1)))
    query_key_value_bias_grad = both[:, : joined_bias_part.shape[0]].reshape(-1)
    expand_bias_grad = both[:, joined_bias_part.shape[0] :].reshape(-1)
    shared = all_sum(all_sum(small[:everywhere], "tp"), "branch").reshape(5, model_width)
    expand_grad = finish(expand_total, 1, output_own)
    contract_grad = finish(contract_total, 1, output_own).T
    while inputs.waiting:
        inputs.land()
        inputs.send()
    inputs.land(shared, block_output, expand_grad, contract_grad)

    def input_body(values, whole):
        x, grad = values[0].astype(F32), values[1].astype(F32)
        total = add_up(values[2:])
        centred = x - jnp.mean(x, axis=-1, keepdims=True)
        rate = lax.rsqrt(jnp.mean(centred * centred, axis=-1, keepdims=True) + EPSILON)
        n = centred * rate
        middle = jnp.mean(total, axis=-1, keepdims=True)
        along = jnp.mean(total * n, axis=-1, keepdims=True)
        return grad + rate * (total - middle - n * along)

    input_both, input_grad_own = finish_tile(
        input_body,
        "finish_input",
        place,
        [both_halves(input_own), both_halves(grad_own)] + inputs.terms(),
        (),
        tile,
        model_width,
    )
    input_grad = fill_other(place, input_both, swap(input_grad_own, "branch", 1))
    joined_grads = finish(joined_total, 1, input_grad_own)
    half_cols = joined_grads.shape[1] // 2
    cols = joined_weight.shape[3]
    query_key_value_grad = jnp.concatenate(
        [joined_grads[:, at : at + cols] for at in (0, half_cols)], axis=1
    )
    dense_grad = jnp.concatenate(
        [joined_grads[:, at + cols : at + half_cols].T for at in (0, half_cols)], axis=0
    )
    return (
        block_output,
        input_grad,
        shared[0],
        shared[1],
        shared[2],
        shared[3],
        query_key_value_grad,
        query_key_value_bias_grad,
        dense_grad,
        shared[4],
        expand_grad,
        expand_bias_grad,
        contract_grad,
        shared[4],
    )


def solution(mesh):
    in_specs = (
        P("seq", "tp", None),
        P(),
        P(),
        P(),
        P(),
        P(("branch", "seq"), "tp"),
        P("tp"),
        P("tp", ("branch", "seq")),
        P(),
        P(("branch", "seq"), "tp"),
        P("tp"),
        P("tp", ("branch", "seq")),
        P(),
        P("seq", None),
        P("seq", "tp", None),
    )
    out_specs = (
        P("seq", "tp", None),
        P("seq", "tp", None),
        P(),
        P(),
        P(),
        P(),
        P(("branch", "seq"), "tp"),
        P("tp"),
        P("tp", ("branch", "seq")),
        P(),
        P(("branch", "seq"), "tp"),
        P("tp"),
        P("tp", ("branch", "seq")),
        P(),
    )
    return jax.shard_map(
        per_device, mesh=mesh, in_specs=in_specs, out_specs=out_specs, check_vma=False
    )
```

time: 2900 us -> 655 us (0.23)
  waiting for transfers between devices: 1250 us -> 67.7 us
  matrix products: 1030 us -> 64.9 us
  Pallas kernels: 0 us -> 379 us
  local copies, waits for them, and re-layouts: 274 us -> 50.3 us
  other arithmetic: 230 us -> 37.5 us
  blocking collectives: 76.4 us -> 0 us
  starting transfers between devices: 0.65 us -> 34.3 us
    dot_general x34 -> x3, matrix products: 1030 us -> 64.9 us  [weight_grad(): lax.dot_general(left, right, CONTRACT_FIRST, preferred_element_type=F32)]
    reduce_scatter x3, waiting for transfers between devices: 911 us -> 0.04 us  [scatter(): return lax.psum_scatter(blocks, 'seq', scatter_dimension=0, tiled=False)]
    pallas_call x0 -> x64, Pallas kernels: none -> 379 us  [launch(): pl.pallas_call(body, grid_spec=pltpu.PrefetchScalarGridSpec(num_scalar_pr...]
    all_gather x6 -> x4, waiting for transfers between devices: 287 us -> 0.01 us  [gather_seq(): return lax.all_gather(piece, 'seq', axis=0)]
    convert_element_type x7 -> x0, local copies, waits for them, and re-layouts: 97.3 us -> none  [the longest x3 58 us: attention_back(): joined_grad = to_tiles(joined_grad, tiles).astype(jnp.bfloat16)]
    reduce_sum x12 -> x2, other arithmetic: 100 us -> 3.56 us  [the longest x1 3.54 us: per_device(): jnp.sum(grad_own.astype(F32), axis=0)]
    reshape x6 -> x4, local copies, waits for them, and re-layouts: 98 us -> 5.72 us  [the longest x3 5.11 us: in_order(): return part.reshape(2, groups, share, part.shape[1]).transpose(1, 0, 2, 3)]
    psum x2 -> x0, blocking collectives: 76.4 us -> none  [the longest x1 41.8 us: per_device(): lax.psum((jnp.where(first_half, gain_part, empty_row), jnp.where(first_ha...]
  transfers between devices with their start and end apart: 10 -> 62, of which waited for: 7 -> 13; matrix products, arithmetic and copies ran while one was open for 20% -> 19% of each run, Pallas kernels for 0% -> 58%
where the time goes in v2:
time: 655 us; the launch traced here: 649 us
  Pallas kernels  379 us (58%)
  waiting for transfers between devices  67.7 us (10%)
  matrix products  64.9 us (10%)
  local copies, waits for them, and re-layouts  50.3 us (8%)
  other arithmetic  37.5 us (6%)
  starting transfers between devices  34.3 us (5%)
  between operations  15.1 us (2%)
    pallas_call x64, Pallas kernels, launch(): pl.pallas_call(body, grid_spec=pltpu.PrefetchScalarGridSpec(num_scalar_pr...  379 us
    ppermute x55, waiting for transfers between devices, swap(): return lax.ppermute(value, axis, [(i, i ^ bit) for i in range(size)])  67.6 us
    dot_general x3, matrix products, weight_grad(): lax.dot_general(left, right, CONTRACT_FIRST, preferred_element_type=F32)  64.9 us
    ppermute x55, starting transfers between devices, swap(): return lax.ppermute(value, axis, [(i, i ^ bit) for i in range(size)])  34 us
    unnamed x123, local copies, waits for them, and re-layouts  28.3 us
  transfers between devices with their start and end apart: 62, of which 13 were waited for; matrix products, arithmetic and copies ran while one was open for 19% of the time, Pallas kernels for 58%

profile of v2, /device:TPU:0, one launch (start us, length us, event | category | flops | bytes accessed | tf_op | source)
XLA Modules:
  0.0 648.8 jit_solution(4332955401308894417)
XLA Ops:
  36.2 4.7 place_piece.4.refs_6_.refs_4_
  41.0 10.8 %rotary_tables.1 = (f32[4096,128]{1,0:T(8,128)}, f32[4096,128]{1,0:T(8,128)}, f32[4096,128]{1,0:T(8,128)}) custom-call(s32[2]{0:T(128)} %pad_add_fusion.refs_0_, s32[2,8]{1,0:T(2,128)} %refs_1_.5, bf16[2,256,768]{2,1,0:T(8,128)(2,1)} %pad_maximum_fusion.5.refs_4_.refs_2_, bf16[2,256,1024]{2,1,0:T(8,128)(2,1)} %pad_maximum_fusion.3.refs_5_.refs_3_, ...), custom_call_target="tpu_custom_call" | custom-call | flops 1048577 | bytes 503317 | tf_op jit(solution)/shard_map/rotary_tables/pallas_call | solution.py:54
  51.8 8.9 %norm_piece.4 = (bf16[4096,2048]{1,0:T(8,128)(2,1)}, bf16[4096,2048]{1,0:T(8,128)(2,1)}, bf16[4096,2048]{1,0:T(8,128)(2,1)}, f32[8,128]{1,0:T(8,128)}) custom-call(bf16[256,2048]{1,0:T(8,128)(2,1)} %get-tuple-element.163.refs_0_, bf16[256,2048]{1,0:T(8,128)(2,1)} %get-tuple-element.162.refs_1_, bf16[256,2048]{1,0:T(8,128)(2,1)} %get-tuple-element.161.refs_2_, ...), custom_call_target="tpu_custom_call" | custom-call | flops 671089 | bytes 671089 | tf_op jit(solution)/shard_map/norm_piece/pallas_call | solution.py:54
  62.2 7.7 %collective-permute-done.refs_0_ = bf16[256,2048]{1,0:T(8,128)(2,1)} collective-permute-done((bf16[256,2048]{1,0:T(8,128)(2,1)}, bf16[256,2048]{1,0:T(8,128)(2,1)}, u32[]{:S(2)}, u32[]{:S(2)}) %collective-permute-start) | collective-permute-done | bytes 1048608 | tf_op jit(solution)/shard_map/ppermute | solution.py:93
  76.7 8.8 %norm_piece.5 = (bf16[4096,2048]{1,0:T(8,128)(2,1)}, bf16[4096,2048]{1,0:T(8,128)(2,1)}, bf16[4096,2048]{1,0:T(8,128)(2,1)}, f32[8,128]{1,0:T(8,128)}) custom-call(bf16[256,2048]{1,0:T(8,128)(2,1)} %hold.36.refs_0_, bf16[256,2048]{1,0:T(8,128)(2,1)} %hold.39.refs_1_, ...), custom_call_target="tpu_custom_call", output_to_operand_aliasing={{0}: (8, {}), {1}: (9, {}), {2}: (10, {})} | custom-call | flops 671089 | bytes 671089 | tf_op jit(solution)/shard_map/norm_piece/pallas_call | solution.py:54
  86.8 9.3 %norm_piece.6 = (bf16[4096,2048]{1,0:T(8,128)(2,1)}, bf16[4096,2048]{1,0:T(8,128)(2,1)}, bf16[4096,2048]{1,0:T(8,128)(2,1)}, f32[8,128]{1,0:T(8,128)}) custom-call(bf16[256,2048]{1,0:T(8,128)(2,1)} %hold.37.refs_0_, bf16[256,2048]{1,0:T(8,128)(2,1)} %hold.38.refs_1_, ...), custom_call_target="tpu_custom_call", output_to_operand_aliasing={{0}: (8, {}), {1}: (9, {}), {2}: (10, {})} | custom-call | flops 671089 | bytes 671089 | tf_op jit(solution)/shard_map/norm_piece/pallas_call | solution.py:54
  106.6 16.9 %project.2 = (bf16[2,2,4,512,128]{4,3,2,1,0:T(8,128)(2,1)}, bf16[2,2,4,512,128]{4,3,2,1,0:T(8,128)(2,1)}, bf16[2,2,4,512,128]{4,3,2,1,0:T(8,128)(2,1)}) custom-call(bf16[4096,2048]{1,0:T(8,128)(2,1)} %get-tuple-element.73.refs_0_.refs_9_, bf16[4,2,256,768]{3,2,1,0:T(8,128)(2,1)} %bitcast.112, f32[1,768]{1,0:T(1,128)} %reshape.129.refs_2_, ...), custom_call_target="tpu_custom_call" | custom-call | flops 193273536 | bytes 408945 | tf_op jit(solution)/shard_map/project/pallas_call | solution.py:54
  123.5 9.0 %norm_piece.7 = (bf16[4096,2048]{1,0:T(8,128)(2,1)}, bf16[4096,2048]{1,0:T(8,128)(2,1)}, bf16[4096,2048]{1,0:T(8,128)(2,1)}, f32[8,128]{1,0:T(8,128)}) custom-call(bf16[256,2048]{1,0:T(8,128)(2,1)} %hold.40.refs_0_.refs_1_, bf16[256,2048]{1,0:T(8,128)(2,1)} %hold.41.refs_1_.refs_2_, ...), custom_call_target="tpu_custom_call", output_to_operand_aliasing={{0}: (8, {}), {1}: (9, {}), {2}: (10, {})} | custom-call | flops 671089 | bytes 671089 | tf_op jit(solution)/shard_map/norm_piece/pallas_call | solution.py:54
  132.5 8.5 %project.3 = (bf16[2,2,4,512,128]{4,3,2,1,0:T(8,128)(2,1)}, bf16[2,2,4,512,128]{4,3,2,1,0:T(8,128)(2,1)}, bf16[2,2,4,512,128]{4,3,2,1,0:T(8,128)(2,1)}) custom-call(bf16[4096,2048]{1,0:T(8,128)(2,1)} %get-tuple-element.78.refs_0_, bf16[4,2,256,768]{3,2,1,0:T(8,128)(2,1)} %bitcast.113, ...), custom_call_target="tpu_custom_call", output_to_operand_aliasing={{0}: (6, {}), {1}: (7, {}), {2}: (8, {})} | custom-call | flops 64424512 | bytes 178258 | tf_op jit(solution)/shard_map/project/pallas_call | solution.py:54
  146.6 35.8 %attend.1 = (bf16[2,4,512,256]{3,2,1,0:T(8,128)(2,1)}, bf16[4,512,256]{2,1,0:T(8,128)(2,1)}, f32[2,2,4,1,512]{4,3,2,1,0:T(1,128)}) custom-call(s32[2]{0:T(128)} %pad_add_fusion.refs_0_, s32[2,8]{1,0:T(2,128)} %refs_1_.5, bf16[2,2,4,512,128]{4,3,2,1,0:T(8,128)(2,1)} %get-tuple-element.81.refs_1_.refs_2_, ...), custom_call_target="tpu_custom_call" | custom-call | flops 805306368 | bytes 167773 | tf_op jit(solution)/shard_map/attend/pallas_call | solution.py:54
  184.5 28.5 %expand.1 = (bf16[4096,1024]{1,0:T(8,128)(2,1)}, bf16[2048,1024]{1,0:T(8,128)(2,1)}, bf16[4096,1024]{1,0:T(8,128)(2,1)}) custom-call(bf16[4096,2048]{1,0:T(8,128)(2,1)} %get-tuple-element.87.refs_0_, bf16[4,2,256,1024]{3,2,1,0:T(8,128)(2,1)} %bitcast.26.refs_1_.refs_6_, f32[1,1024]{1,0:T(1,128)} %bitcast.185, ...), custom_call_target="tpu_custom_call" | custom-call | flops 343597376 | bytes 754975 | tf_op jit(solution)/shard_map/expand/pallas_call | solution.py:54
  220.9 4.7 place_piece.6.refs_4_
  226.6 4.7 place_piece.7.refs_0_
  231.3 22.7 %convolution_convert_fusion.1 = bf16[2048,1024]{1,0:T(8,128)(2,1)S(1)} fusion(bf16[4096,2048]{1,0:T(8,128)(2,1)} %place_piece.7.refs_0_, bf16[4096,1024]{1,0:T(8,128)(2,1)} %get-tuple-element.89.refs_2_), kind=kOutput, calls=%fused_computation.5 | convolution fusion | flops 17181966336 | bytes 29360128 | tf_op jit(solution)/shard_map/dot_general | solution.py:1079
  257.2 7.7 %collective-permute-done.26.refs_4_.refs_1_ = bf16[2048,256]{1,0:T(8,128)(2,1)S(1)} collective-permute-done((bf16[2048,256]{1,0:T(8,128)(2,1)}, bf16[2048,256]{1,0:T(8,128)(2,1)S(1)}, u32[]{:S(2)}, u32[]{:S(2)}) %collective-permute-start.26) | collective-permute-done | bytes 1048608 | tf_op jit(solution)/shard_map/ppermute | solution.py:93
  265.9 35.6 %pre_grad.1 = (bf16[4096,1024]{1,0:T(8,128)(2,1)}, bf16[2048,1024]{1,0:T(8,128)(2,1)}, f32[1,1024]{1,0:T(1,128)}) custom-call(bf16[4096,2048]{1,0:T(8,128)(2,1)} %place_piece.7.refs_0_, bf16[4096,1024]{1,0:T(8,128)(2,1)} %get-tuple-element.88.refs_1_.refs_5_, bf16[4,2,1024,256]{3,2,1,0:T(8,128)(2,1)} %bitcast.120, bf16[4,2,256,1024]{3,2,1,0:T(8,128)(2,1)} %bitcast.136, ...), custom_call_target="tpu_custom_call" | custom-call | flops 343597376 | bytes 754975 | tf_op jit(solution)/shard_map/pre_grad/pallas_call | solution.py:54
  302.1 22.8 %convolution_convert_fusion = bf16[2048,1024]{1,0:T(8,128)(2,1)S(1)} fusion(bf16[4096,2048]{1,0:T(8,128)(2,1)} %get-tuple-element.87.refs_0_, bf16[4096,1024]{1,0:T(8,128)(2,1)} %get-tuple-element.91.refs_2_), kind=kOutput, calls=%fused_computation.4 | convolution fusion | flops 17181966336 | bytes 29360128 | tf_op jit(solution)/shard_map/dot_general | solution.py:1079
  327.5 15.4 %dense_back.1 = (bf16[4096,256]{1,0:T(8,128)(2,1)}, bf16[4,2,256,256]{3,2,1,0:T(8,128)(2,1)}) custom-call(bf16[4096,2048]{1,0:T(8,128)(2,1)} %place_piece.7.refs_0_, bf16[4096,256]{1,0:T(8,128)(2,1)} %bitcast.130, bf16[4,2,256,256]{3,2,1,0:T(8,128)(2,1)} %bitcast.141, bf16[4,2,256,1024]{3,2,1,0:T(8,128)(2,1)} %bitcast.138, ...), custom_call_target="tpu_custom_call" | custom-call | flops 171798688 | bytes 398459 | tf_op jit(solution)/shard_map/dense_back/pallas_call | solution.py:54
  343.9 9.9 %output_piece.4.refs_8_ = bf16[512,2048]{1,0:T(8,128)(2,1)} custom-call(bf16[4096,256]{1,0:T(8,128)(2,1)} %bitcast.131, bf16[2048,256]{1,0:T(8,128)(2,1)} %copy-done.8, bf16[4096,1024]{1,0:T(8,128)(2,1)} %get-tuple-element.89.refs_2_, bf16[2048,1024]{1,0:T(8,128)(2,1)} %collective-permute-done.27.refs_5_.refs_3_, bf16[4,2,256,256]{3,2,1,0:T(8,128)(2,1)} %bitcast.142, ...), custom_call_target="tpu_custom_call" | custom-call | flops 214748368 | bytes 419431 | tf_op jit(solution)/shard_map/output_piece/pallas_call | solution.py:54
  358.2 10.0 %output_piece.5.refs_8_ = bf16[512,2048]{1,0:T(8,128)(2,1)} custom-call(bf16[4096,256]{1,0:T(8,128)(2,1)} %bitcast.132, bf16[2048,256]{1,0:T(8,128)(2,1)} %copy-done.8, bf16[4096,1024]{1,0:T(8,128)(2,1)} %get-tuple-element.89.refs_2_, bf16[2048,1024]{1,0:T(8,128)(2,1)} %collective-permute-done.27.refs_5_.refs_3_, bf16[4,2,256,256]{3,2,1,0:T(8,128)(2,1)} %bitcast.143, ...), custom_call_target="tpu_custom_call" | custom-call | flops 214748368 | bytes 419431 | tf_op jit(solution)/shard_map/output_piece/pallas_call | solution.py:54
  368.2 10.0 %output_piece.6.refs_8_ = bf16[512,2048]{1,0:T(8,128)(2,1)} custom-call(bf16[4096,256]{1,0:T(8,128)(2,1)} %bitcast.133, bf16[2048,256]{1,0:T(8,128)(2,1)} %copy-done.8, bf16[4096,1024]{1,0:T(8,128)(2,1)} %get-tuple-element.89.refs_2_, bf16[2048,1024]{1,0:T(8,128)(2,1)} %collective-permute-done.27.refs_5_.refs_3_, bf16[4,2,256,256]{3,2,1,0:T(8,128)(2,1)} %bitcast.144, ...), custom_call_target="tpu_custom_call" | custom-call | flops 214748368 | bytes 419431 | tf_op jit(solution)/shard_map/output_piece/pallas_call | solution.py:54
  378.2 10.1 %output_piece.7.refs_1_.refs_2_ = bf16[512,2048]{1,0:T(8,128)(2,1)} custom-call(bf16[4096,256]{1,0:T(8,128)(2,1)} %bitcast.134, bf16[2048,256]{1,0:T(8,128)(2,1)} %copy-done.8, bf16[4096,1024]{1,0:T(8,128)(2,1)} %get-tuple-element.89.refs_2_, bf16[2048,1024]{1,0:T(8,128)(2,1)} %collective-permute-done.27.refs_5_.refs_3_, bf16[4,2,256,256]{3,2,1,0:T(8,128)(2,1)} %bitcast.145, ...), custom_call_target="tpu_custom_call" | custom-call | flops 214748368 | bytes 419431 | tf_op jit(solution)/shard_map/output_piece/pallas_call | solution.py:54
  397.7 57.7 %attend_back.1 = (bf16[2,4,512,768]{3,2,1,0:T(8,128)(2,1)}, bf16[4,512,768]{2,1,0:T(8,128)(2,1)}, f32[2,1,768]{2,1,0:T(1,128)}) custom-call(s32[2]{0:T(128)} %pad_add_fusion.refs_0_, s32[2,8]{1,0:T(2,128)} %refs_1_.5, bf16[2,2,4,512,128]{4,3,2,1,0:T(8,128)(2,1)} %get-tuple-element.81.refs_1_.refs_2_, bf16[2,2,4,512,128]{4,3,2,1,0:T(8,128)(2,1)} %get-tuple-element.82.refs_3_, ...), custom_call_target="tpu_custom_call" | custom-call | flops 1342177280 | bytes 503317 | tf_op jit(solution)/shard_map/attend_back/pallas_call | solution.py:54
  458.6 19.4 %convolution_convert_fusion.2 = bf16[2048,768]{1,0:T(8,128)(2,1)S(1)} fusion(bf16[4096,2048]{1,0:T(8,128)(2,1)} %hold.63, bf16[4096,768]{1,0:T(8,128)(2,1)} %bitcast.125), kind=kOutput, calls=%fused_computation.6 | convolution fusion | flops 12886474752 | bytes 26214400 | tf_op jit(solution)/shard_map/dot_general | solution.py:1079
  481.8 13.9 %normed_grad_piece.4 = (bf16[512,2048]{1,0:T(8,128)(2,1)}, f32[8,2048]{1,0:T(8,128)}) custom-call(bf16[4096,768]{1,0:T(8,128)(2,1)} %bitcast.126, bf16[2048,768]{1,0:T(8,128)(2,1)} %collective-permute-done.37.refs_1_, bf16[4096,1024]{1,0:T(8,128)(2,1)} %get-tuple-element.91.refs_2_, bf16[2048,1024]{1,0:T(8,128)(2,1)} %collective-permute-done.32.refs_4_.refs_3_, ...), custom_call_target="tpu_custom_call" | custom-call | flops 300647712 | bytes 587203 | tf_op jit(solution)/shard_map/normed_grad_piece/pallas_call | solution.py:54
  499.4 13.2 %normed_grad_piece.5 = (bf16[512,2048]{1,0:T(8,128)(2,1)}, f32[8,2048]{1,0:T(8,128)}) custom-call(bf16[4096,768]{1,0:T(8,128)(2,1)} %bitcast.127, bf16[2048,768]{1,0:T(8,128)(2,1)} %collective-permute-done.37.refs_1_, bf16[4096,1024]{1,0:T(8,128)(2,1)} %get-tuple-element.91.refs_2_, bf16[2048,1024]{1,0:T(8,128)(2,1)} %collective-permute-done.32.refs_4_.refs_3_, ...), custom_call_target="tpu_custom_call" | custom-call | flops 300647712 | bytes 587203 | tf_op jit(solution)/shard_map/normed_grad_piece/pallas_call | solution.py:54
  512.6 10.5 %collective-permute-done.40.refs_0_ = bf16[256,2048]{1,0:T(8,128)(2,1)S(1)} collective-permute-done((bf16[256,2048]{1,0:T(8,128)(2,1)S(1)}, bf16[256,2048]{1,0:T(8,128)(2,1)S(1)}, u32[]{:S(2)}, u32[]{:S(2)}) %collective-permute-start.40) | collective-permute-done | bytes 1048608 | tf_op jit(solution)/shard_map/ppermute | solution.py:93
  529.5 13.4 %normed_grad_piece.6 = (bf16[512,2048]{1,0:T(8,128)(2,1)}, f32[8,2048]{1,0:T(8,128)}) custom-call(bf16[4096,768]{1,0:T(8,128)(2,1)} %bitcast.128, bf16[2048,768]{1,0:T(8,128)(2,1)} %collective-permute-done.37.refs_1_, bf16[4096,1024]{1,0:T(8,128)(2,1)} %get-tuple-element.91.refs_2_, bf16[2048,1024]{1,0:T(8,128)(2,1)} %collective-permute-done.32.refs_4_.refs_3_, ...), custom_call_target="tpu_custom_call" | custom-call | flops 300647712 | bytes 587203 | tf_op jit(solution)/shard_map/normed_grad_piece/pallas_call | solution.py:54
  552.6 21.8 %collective-permute-done.42.refs_0_ = bf16[512,2048]{1,0:T(8,128)(2,1)S(1)} collective-permute-done((bf16[512,2048]{1,0:T(8,128)(2,1)}, bf16[512,2048]{1,0:T(8,128)(2,1)S(1)}, u32[]{:S(2)}, u32[]{:S(2)}) %collective-permute-start.42) | collective-permute-done | bytes 2097184 | tf_op jit(solution)/shard_map/ppermute | solution.py:93
  575.8 13.2 %normed_grad_piece.7 = (bf16[512,2048]{1,0:T(8,128)(2,1)}, f32[8,2048]{1,0:T(8,128)}) custom-call(bf16[4096,768]{1,0:T(8,128)(2,1)} %bitcast.129, bf16[2048,768]{1,0:T(8,128)(2,1)} %collective-permute-done.37.refs_1_, bf16[4096,1024]{1,0:T(8,128)(2,1)} %get-tuple-element.91.refs_2_, bf16[2048,1024]{1,0:T(8,128)(2,1)} %collective-permute-done.32.refs_4_.refs_3_, ...), custom_call_target="tpu_custom_call" | custom-call | flops 300647712 | bytes 587203 | tf_op jit(solution)/shard_map/normed_grad_piece/pallas_call | solution.py:54
  589.0 6.3 finish_output.1
  607.4 8.1 %finish_input.1 = (bf16[2,512,2048]{2,1,0:T(8,128)(2,1)}, bf16[512,2048]{1,0:T(8,128)(2,1)}) custom-call(s32[2]{0:T(128)} %pad_add_fusion.refs_0_, bf16[512,2048]{1,0:T(8,128)(2,1)} %dynamic-slice_bitcast_fusion.1.refs_1_, bf16[512,2048]{1,0:T(8,128)(2,1)} %get-tuple-element.155.refs_2_, bf16[512,2048]{1,0:T(8,128)(2,1)} %get-tuple-element.108.refs_3_, ...), custom_call_target="tpu_custom_call" | custom-call | flops 419431 | bytes 419431 | tf_op jit(solution)/shard_map/finish_input/pallas_call | solution.py:54
  (355 shorter events, 153.6 us)
Async XLA Ops:
  7.2 99.4 %all-gather.9.cloned.1.call-start = ((), (), s32[]{:S(2)}) async-start(), calls=%async_computation.6 | async-start | bytes 3932160 | tf_op jit(solution)/shard_map/all_gather | solution.py:993
  12.3 172.2 %all-gather.11.cloned.1.call-start = ((), (), s32[]{:S(2)}) async-start(), calls=%async_computation.7 | async-start | bytes 5242880 | tf_op jit(solution)/shard_map/all_gather | solution.py:993
  15.8 241.3 %all-gather.15.cloned.1.call-start = ((), (), s32[]{:S(2)}) async-start(), calls=%async_computation.9 | async-start | bytes 5242880 | tf_op jit(solution)/shard_map/all_gather | solution.py:993
  20.8 39.9 %collective-permute-start.10 = (bf16[256,2048]{1,0:T(8,128)(2,1)}, bf16[256,2048]{1,0:T(8,128)(2,1)S(1)}, u32[]{:S(2)}, u32[]{:S(2)}) collective-permute-start(bf16[256,2048]{1,0:T(8,128)(2,1)} %get-tuple-element.162.refs_1_), channel_id=1, source_target_pairs={{0,4},{4,0},{8,12},{12,8},{1,5},{5,1},{9,13},{13,9},{2,6},{6,2},{1... | collective-permute-start | bytes 3145736 | tf_op jit(solution)/shard_map/ppermute | solution.py:93
  24.7 277.2 %all-gather.13.cloned.1.call-start = ((), (), s32[]{:S(2)}) async-start(), calls=%async_computation.8 | async-start | bytes 1310720 | tf_op jit(solution)/shard_map/all_gather | solution.py:993
  24.8 45.1 %collective-permute-start.7 = (bf16[256,2048]{1,0:T(8,128)(2,1)}, bf16[256,2048]{1,0:T(8,128)(2,1)S(1)}, u32[]{:S(2)}, u32[]{:S(2)}) collective-permute-start(bf16[256,2048]{1,0:T(8,128)(2,1)} %get-tuple-element.162.refs_1_), channel_id=1, source_target_pairs={{0,8},{4,12},{8,0},{12,4},{1,9},{5,13},{9,1},{13,5},{2,10},{6,14},... | collective-permute-start | bytes 3145736 | tf_op jit(solution)/shard_map/ppermute | solution.py:93
  26.4 43.5 %collective-permute-start = (bf16[256,2048]{1,0:T(8,128)(2,1)}, bf16[256,2048]{1,0:T(8,128)(2,1)}, u32[]{:S(2)}, u32[]{:S(2)}) collective-permute-start(bf16[256,2048]{1,0:T(8,128)(2,1)} %get-tuple-element.163.refs_0_), channel_id=1, source_target_pairs={{0,4},{4,0},{8,12},{12,8},{1,5},{5,1},{9,13},{13,9},{2,6},{6,2},{1... | collective-permute-start | bytes 3145736 | tf_op jit(solution)/shard_map/ppermute | solution.py:93
  26.9 45.8 %collective-permute-start.6 = (bf16[256,2048]{1,0:T(8,128)(2,1)}, bf16[256,2048]{1,0:T(8,128)(2,1)S(1)}, u32[]{:S(2)}, u32[]{:S(2)}) collective-permute-start(bf16[256,2048]{1,0:T(8,128)(2,1)} %get-tuple-element.163.refs_0_), channel_id=1, source_target_pairs={{0,8},{4,12},{8,0},{12,4},{1,9},{5,13},{9,1},{13,5},{2,10},{6,14},... | collective-permute-start | bytes 3145736 | tf_op jit(solution)/shard_map/ppermute | solution.py:93
  74.1 26.3 %collective-permute-start.5 = (bf16[256,2048]{1,0:T(8,128)(2,1)}, bf16[256,2048]{1,0:T(8,128)(2,1)S(1)}, u32[]{:S(2)}, u32[]{:S(2)}) collective-permute-start(bf16[256,2048]{1,0:T(8,128)(2,1)} %hold.36.refs_0_), channel_id=1, source_target_pairs={{0,8},{4,12},{8,0},{12,4},{1,9},{5,13},{9,1},{13,5},{2,10},{6,14},... | collective-permute-start | bytes 3145736 | tf_op jit(solution)/shard_map/ppermute | solution.py:93
  102.9 38.1 %collective-permute-start.17 = (bf16[256,2048]{1,0:T(8,128)(2,1)}, bf16[256,2048]{1,0:T(8,128)(2,1)}, u32[]{:S(2)}, u32[]{:S(2)}) collective-permute-start(bf16[256,2048]{1,0:T(8,128)(2,1)} %hold.44), channel_id=1, source_target_pairs={{0,8},{4,12},{8,0},{12,4},{1,9},{5,13},{9,1},{13,5},{2,10},{6,14},... | collective-permute-start | bytes 3145736 | tf_op jit(solution)/shard_map/ppermute | solution.py:93
  105.4 35.6 %collective-permute-start.16 = (bf16[256,2048]{1,0:T(8,128)(2,1)}, bf16[256,2048]{1,0:T(8,128)(2,1)S(1)}, u32[]{:S(2)}, u32[]{:S(2)}) collective-permute-start(bf16[256,2048]{1,0:T(8,128)(2,1)} %hold.42), channel_id=1, source_target_pairs={{0,4},{4,0},{8,12},{12,8},{1,5},{5,1},{9,13},{13,9},{2,6},{6,2},{1... | collective-permute-start | bytes 3145736 | tf_op jit(solution)/shard_map/ppermute | solution.py:93
  142.0 40.5 %collective-permute-start.18 = (bf16[256,2048]{1,0:T(8,128)(2,1)}, bf16[256,2048]{1,0:T(8,128)(2,1)S(1)}, u32[]{:S(2)}, u32[]{:S(2)}) collective-permute-start(bf16[256,2048]{1,0:T(8,128)(2,1)} %hold.46), channel_id=1, source_target_pairs={{0,4},{4,0},{8,12},{12,8},{1,5},{5,1},{9,13},{13,9},{2,6},{6,2},{1... | collective-permute-start | bytes 3145736 | tf_op jit(solution)/shard_map/ppermute | solution.py:93
  143.5 40.0 %collective-permute-start.20 = (bf16[256,2048]{1,0:T(8,128)(2,1)}, bf16[256,2048]{1,0:T(8,128)(2,1)S(1)}, u32[]{:S(2)}, u32[]{:S(2)}) collective-permute-start(bf16[256,2048]{1,0:T(8,128)(2,1)} %hold.48), channel_id=1, source_target_pairs={{0,8},{4,12},{8,0},{12,4},{1,9},{5,13},{9,1},{13,5},{2,10},{6,14},... | collective-permute-start | bytes 3145736 | tf_op jit(solution)/shard_map/ppermute | solution.py:93
  144.0 68.9 %collective-permute-start.25 = (bf16[256,2048]{1,0:T(8,128)(2,1)}, bf16[256,2048]{1,0:T(8,128)(2,1)}, u32[]{:S(2)}, u32[]{:S(2)}) collective-permute-start(bf16[256,2048]{1,0:T(8,128)(2,1)} %hold.45.refs_6_.refs_2_.refs_1_), channel_id=1, source_target_pairs={{0,4},{4,0},{8,12},{12,8},{1,5},{5,1},{9,13},{13,9},{2,6},{6,2},{1... | collective-permute-start | bytes 3145736 | tf_op jit(solution)/shard_map/ppermute | solution.py:93
  144.5 69.0 %collective-permute-start.24 = (bf16[256,2048]{1,0:T(8,128)(2,1)S(1)}, bf16[256,2048]{1,0:T(8,128)(2,1)}, u32[]{:S(2)}, u32[]{:S(2)}) collective-permute-start(bf16[256,2048]{1,0:T(8,128)(2,1)S(1)} %copy-done.2), channel_id=1, source_target_pairs={{0,8},{4,12},{8,0},{12,4},{1,9},{5,13},{9,1},{13,5},{2,10},{6,14},... | collective-permute-start | bytes 3145736 | tf_op jit(solution)/shard_map/ppermute | solution.py:93
  146.0 67.6 %collective-permute-start.19 = (bf16[256,2048]{1,0:T(8,128)(2,1)S(1)}, bf16[256,2048]{1,0:T(8,128)(2,1)}, u32[]{:S(2)}, u32[]{:S(2)}) collective-permute-start(bf16[256,2048]{1,0:T(8,128)(2,1)S(1)} %copy-done.2), channel_id=1, source_target_pairs={{0,16},{16,0},{1,17},{17,1},{2,18},{18,2},{3,19},{19,3},{4,20},{20... | collective-permute-start | bytes 3145736 | tf_op jit(solution)/shard_map/ppermute | solution.py:93
  182.5 32.6 %collective-permute-start.23 = (bf16[256,2048]{1,0:T(8,128)(2,1)}, bf16[256,2048]{1,0:T(8,128)(2,1)}, u32[]{:S(2)}, u32[]{:S(2)}) collective-permute-start(bf16[256,2048]{1,0:T(8,128)(2,1)} %hold.45.refs_6_.refs_2_.refs_1_), channel_id=1, source_target_pairs={{0,16},{16,0},{1,17},{17,1},{2,18},{18,2},{3,19},{19,3},{4,20},{20... | collective-permute-start | bytes 3145736 | tf_op jit(solution)/shard_map/ppermute | solution.py:93
  183.5 30.6 %collective-permute-start.21 = (bf16[256,2048]{1,0:T(8,128)(2,1)}, bf16[256,2048]{1,0:T(8,128)(2,1)S(1)}, u32[]{:S(2)}, u32[]{:S(2)}) collective-permute-start(bf16[256,2048]{1,0:T(8,128)(2,1)} %hold.47.refs_4_.refs_2_.refs_1_), channel_id=1, source_target_pairs={{0,16},{16,0},{1,17},{17,1},{2,18},{18,2},{3,19},{19,3},{4,20},{20... | collective-permute-start | bytes 3145736 | tf_op jit(solution)/shard_map/ppermute | solution.py:93
  220.8 375.3 %reduce-scatter.8.cloned.1.call-start = ((), (), s32[]{:S(2)}) async-start(), calls=%async_computation.5 | async-start | bytes 5242880 | tf_op jit(solution)/shard_map/reduce_scatter | solution.py:1085
  256.5 347.5 %reduce-scatter.6.cloned.1.call-start = ((), (), s32[]{:S(2)}) async-start(), calls=%async_computation.4 | async-start | bytes 5242880 | tf_op jit(solution)/shard_map/reduce_scatter | solution.py:1085
  257.1 70.4 %collective-permute-start.29 = (bf16[4,2,1024,256]{3,2,1,0:T(8,128)(2,1)}, bf16[4,2,1024,256]{3,2,1,0:T(8,128)(2,1)}, u32[]{:S(2)}, u32[]{:S(2)}) collective-permute-start(bf16[4,2,1024,256]{3,2,1,0:T(8,128)(2,1)} %bitcast.119), channel_id=1, source_target_pairs={{0,16},{16,0},{1,17},{17,1},{2,18},{18,2},{3,19},{19,3},{4,20},{20... | collective-permute-start | bytes 12582920 | tf_op jit(solution)/shard_map/ppermute | solution.py:93
  301.9 41.0 %collective-permute-start.28 = (bf16[4,2,256,256]{3,2,1,0:T(8,128)(2,1)}, bf16[4,2,256,256]{3,2,1,0:T(8,128)(2,1)S(1)}, u32[]{:S(2)}, u32[]{:S(2)}) collective-permute-start(bf16[4,2,256,256]{3,2,1,0:T(8,128)(2,1)} %bitcast.140), channel_id=1, source_target_pairs={{0,16},{16,0},{1,17},{17,1},{2,18},{18,2},{3,19},{19,3},{4,20},{20... | collective-permute-start | bytes 3145736 | tf_op jit(solution)/shard_map/ppermute | solution.py:93
  327.4 300.4 %reduce-scatter.4.cloned.1.call-start = ((), (), s32[]{:S(2)}) async-start(), calls=%async_computation.3 | async-start | bytes 5242880 | tf_op jit(solution)/shard_map/reduce_scatter | solution.py:1085
  355.6 32.6 %collective-permute-start.35 = (bf16[256,2048]{1,0:T(8,128)(2,1)S(1)}, bf16[256,2048]{1,0:T(8,128)(2,1)S(1)}, u32[]{:S(2)}, u32[]{:S(2)}) collective-permute-start(bf16[256,2048]{1,0:T(8,128)(2,1)S(1)} %get-tuple-element.166.refs_10_), channel_id=1, source_target_pairs={{0,4},{4,0},{8,12},{12,8},{1,5},{5,1},{9,13},{13,9},{2,6},{6,2},{1... | collective-permute-start | bytes 3145736 | tf_op jit(solution)/shard_map/ppermute | solution.py:93
  357.3 35.9 %collective-permute-start.33 = (bf16[256,2048]{1,0:T(8,128)(2,1)S(1)}, bf16[256,2048]{1,0:T(8,128)(2,1)S(1)}, u32[]{:S(2)}, u32[]{:S(2)}) collective-permute-start(bf16[256,2048]{1,0:T(8,128)(2,1)S(1)} %get-tuple-element.167.refs_9_), channel_id=1, source_target_pairs={{0,8},{4,12},{8,0},{12,4},{1,9},{5,13},{9,1},{13,5},{2,10},{6,14},... | collective-permute-start | bytes 3145736 | tf_op jit(solution)/shard_map/ppermute | solution.py:93
  392.1 63.2 %collective-permute-start.36 = (bf16[512,2048]{1,0:T(8,128)(2,1)}, bf16[512,2048]{1,0:T(8,128)(2,1)S(1)}, u32[]{:S(2)}, u32[]{:S(2)}) collective-permute-start(bf16[512,2048]{1,0:T(8,128)(2,1)} %fusion.1.refs_14_), channel_id=1, source_target_pairs={{0,8},{4,12},{8,0},{12,4},{1,9},{5,13},{9,1},{13,5},{2,10},{6,14},... | collective-permute-start | bytes 6291464 | tf_op jit(solution)/shard_map/ppermute | solution.py:93
  397.2 59.6 %collective-permute-start.34 = (bf16[512,2048]{1,0:T(8,128)(2,1)}, bf16[512,2048]{1,0:T(8,128)(2,1)S(1)}, u32[]{:S(2)}, u32[]{:S(2)}) collective-permute-start(bf16[512,2048]{1,0:T(8,128)(2,1)} %fusion.refs_13_), channel_id=1, source_target_pairs={{0,4},{4,0},{8,12},{12,8},{1,5},{5,1},{9,13},{13,9},{2,6},{6,2},{1... | collective-permute-start | bytes 6291464 | tf_op jit(solution)/shard_map/ppermute | solution.py:93
  397.7 84.1 %collective-permute-start.38 = (bf16[4,2,256,768]{3,2,1,0:T(8,128)(2,1)S(1)}, bf16[4,2,256,768]{3,2,1,0:T(8,128)(2,1)}, u32[]{:S(2)}, u32[]{:S(2)}) collective-permute-start(bf16[4,2,256,768]{3,2,1,0:T(8,128)(2,1)S(1)} %bitcast.118), channel_id=1, source_target_pairs={{0,16},{16,0},{1,17},{17,1},{2,18},{18,2},{3,19},{19,3},{4,20},{20... | collective-permute-start | bytes 9437192 | tf_op jit(solution)/shard_map/ppermute | solution.py:93
  497.8 30.6 %collective-permute-start.41 = (bf16[256,2048]{1,0:T(8,128)(2,1)S(1)}, bf16[256,2048]{1,0:T(8,128)(2,1)S(1)}, u32[]{:S(2)}, u32[]{:S(2)}) collective-permute-start(bf16[256,2048]{1,0:T(8,128)(2,1)S(1)} %get-tuple-element.164.refs_13_), channel_id=1, source_target_pairs={{0,4},{4,0},{8,12},{12,8},{1,5},{5,1},{9,13},{13,9},{2,6},{6,2},{1... | collective-permute-start | bytes 3145736 | tf_op jit(solution)/shard_map/ppermute | solution.py:93
  526.9 47.5 %collective-permute-start.42 = (bf16[512,2048]{1,0:T(8,128)(2,1)}, bf16[512,2048]{1,0:T(8,128)(2,1)S(1)}, u32[]{:S(2)}, u32[]{:S(2)}) collective-permute-start(bf16[512,2048]{1,0:T(8,128)(2,1)} %fusion.2.refs_14_), channel_id=1, source_target_pairs={{0,4},{4,0},{8,12},{12,8},{1,5},{5,1},{9,13},{13,9},{2,6},{6,2},{1... | collective-permute-start | bytes 6291464 | tf_op jit(solution)/shard_map/ppermute | solution.py:93
  545.7 61.7 %collective-permute-start.44 = (bf16[512,2048]{1,0:T(8,128)(2,1)}, bf16[512,2048]{1,0:T(8,128)(2,1)}, u32[]{:S(2)}, u32[]{:S(2)}) collective-permute-start(bf16[512,2048]{1,0:T(8,128)(2,1)} %fusion.3.refs_13_), channel_id=1, source_target_pairs={{0,8},{4,12},{8,0},{12,4},{1,9},{5,13},{9,1},{13,5},{2,10},{6,14},... | collective-permute-start | bytes 6291464 | tf_op jit(solution)/shard_map/ppermute | solution.py:93
  596.1 38.7 %collective-permute-start.43 = (bf16[512,2048]{1,0:T(8,128)(2,1)}, bf16[512,2048]{1,0:T(8,128)(2,1)}, u32[]{:S(2)}, u32[]{:S(2)}) collective-permute-start(bf16[512,2048]{1,0:T(8,128)(2,1)} %get-tuple-element.106.refs_1_), channel_id=1, source_target_pairs={{0,16},{16,0},{1,17},{17,1},{2,18},{18,2},{3,19},{19,3},{4,20},{20... | collective-permute-start | bytes 6291464 | tf_op jit(solution)/shard_map/ppermute | solution.py:93
  (88 other events, 610.5 us)
Sparse Core Ops, SparseCore 0:
  12.4 66.1 all-gather.8
  80.2 79.3 all-gather.10
  161.2 79.2 all-gather.14
  242.5 26.4 all-gather.12
  271.1 76.2 reduce-scatter.7
  349.7 77.2 reduce-scatter.5
  481.8 77.5 reduce-scatter.3
